TPU v7x, 256 devices: a whole 4x4x8 slice. The times are simulated.
256 devices in a mesh: py: 16 (over z, core), pz: 16 (over x, y).
Axes of the slice: x: 4, y: 4, z: 8, core: 2. Of those that a mesh axis runs over, the one named last changes fastest.
Arguments:
- velocity: float32 [192, 384, 1536], P('pz', 'py'), may hold values from -4 to 4
- wind_profile: float32 [192], P('pz'), may hold values from 0.5 to 1.5
- thrust_coef: float32 [100], replicated, may hold values from 0.5 to 2
- turbine_bricks: int32 [100, 4], replicated, may hold values from 0 to 383
- turbine_offset: int32 [100, 3], replicated, may hold values from 6 to 95, as said below
Outputs:
- tendency: float32 [192, 384, 1536], P('pz', 'py')
- rotor_speed: float32 [100], replicated
Inputs may be any that keep to these rules, and one draw needn't show every extreme that they name: `turbine_offset`: oz lies in [h / 2, 3 h / 2) with h = 192 / 16, oy in [w / 2, 3 w / 2) with w = 384 / 16, ox in [32, 96).
All inputs are finite; a program needn't handle non-finite values.
Results may differ from a plain program's by a relative error of at most 0.000064.
Values sent between devices are 32-bit elements; how exact they have to be, the bound alone decides.
No kernel may reach another device: no remote copies, remote signals or barrier semaphores. Data moves between devices by JAX's collectives and lax.ppermute only.
A program may use at most 192 MiB of HBM per device.

v0:
```python
import math

import jax
import jax.numpy as jnp
from jax import lax
from jax.sharding import PartitionSpec as P

BX = 128


VISCOSITY = 0.2
CROSS_WIND = 0.4
DISK_DEPTH = 1.5
DISK_EDGE = 1.0
RADIUS_SHARE = 0.6
COLUMN_BLOCK = 384
PRECISE = lax.Precision.HIGHEST


def tables(length, offset, counted):
    source = lax.broadcasted_iota(jnp.int32, (length, counted), 0)
    target = lax.broadcasted_iota(jnp.int32, (length, counted), 1) + offset
    folded = (target - source) % length
    folded = jnp.where(folded > length // 2, folded - length, folded)
    parity = jnp.where(folded % 2 == 0, 1.0, -1.0).astype(jnp.float32)
    phase_angle = math.pi / length * folded.astype(jnp.float32)
    sine_value = jnp.where(folded == 0, 1.0, jnp.sin(phase_angle))
    first_table = jnp.where(
        folded == 0, 0.0, math.pi / length * parity * jnp.cos(phase_angle) / sine_value
    )
    diagonal = -math.pi**2 / 3.0 - 2.0 * math.pi**2 / (3.0 * length * length)
    second_table = jnp.where(
        folded == 0,
        diagonal,
        -(2.0 * math.pi**2 / (length * length)) * parity / (sine_value * sine_value),
    )
    return (first_table, second_table)


def disk_weights(rel_z, rel_y, rel_x, radius):
    axial = jnp.exp(-0.5 * (rel_x / DISK_DEPTH) ** 2)
    radial = jax.nn.sigmoid(
        (radius * radius - rel_y * rel_y - rel_z * rel_z) / (2.0 * radius * DISK_EDGE)
    )
    return axial * radial


def arrange(membership, capacity):
    counted = membership.astype(jnp.int32)
    pair_rank = jnp.cumsum(counted, axis=0) - counted
    slot_ids = jnp.arange(capacity, dtype=jnp.int32)
    matched = membership[None, :, :] & (pair_rank[None, :, :] == slot_ids[:, None, None])
    groups = membership.shape[1]
    return (
        jnp.transpose(matched, (2, 0, 1))
        .reshape(groups * capacity, membership.shape[0])
        .astype(jnp.float32)
    )


def along_x(velocity, wind_profile):
    depth_z, span_y, length_x = velocity.shape
    flattened = velocity.reshape(depth_z * span_y, length_x)
    block_width = min(length_x, COLUMN_BLOCK)
    slopes = []
    curves = []
    for offset in range(0, length_x, block_width):
        first_table, second_table = tables(length_x, offset, block_width)
        slopes.append(
            jnp.dot(flattened, first_table, precision=PRECISE, preferred_element_type=jnp.float32)
        )
        curves.append(
            jnp.dot(flattened, second_table, precision=PRECISE, preferred_element_type=jnp.float32)
        )
    slope_all = jnp.concatenate(slopes, axis=1).reshape(depth_z, span_y, length_x)
    curve_all = jnp.concatenate(curves, axis=1).reshape(depth_z, span_y, length_x)
    return VISCOSITY * curve_all - wind_profile[:, None, None] * slope_all


def disk_force(velocity, wind_profile, thrust_coef, turbine_bricks, turbine_offset):
    depth_z, span_y, length_x = velocity.shape
    columns = lax.axis_size("py")
    level = lax.axis_index("pz")
    column = lax.axis_index("py")
    blocks_x = length_x // BX
    capacity = 2 * min(blocks_x, columns)
    turbines = turbine_bricks.shape[0]
    per_turbine = turbine_bricks.shape[1]
    radius = RADIUS_SHARE * depth_z
    pair_ids = turbine_bricks.reshape(-1)
    pair_row = pair_ids // (columns * blocks_x)
    pair_col = pair_ids // blocks_x % columns
    pair_blk = pair_ids % blocks_x
    base_brick = turbine_bricks[:, 0]
    left_column = base_brick // blocks_x % columns
    x_block = base_brick % blocks_x
    pair_turb = jnp.repeat(jnp.arange(turbines, dtype=jnp.int32), per_turbine)
    centre_z = turbine_offset[:, 0]
    centre_y = left_column * span_y + turbine_offset[:, 1]
    centre_x = x_block * BX + turbine_offset[:, 2]
    pair_geometry = jnp.stack(
        [
            jnp.repeat(centre_z, per_turbine),
            jnp.repeat(centre_y, per_turbine),
            jnp.repeat(centre_x, per_turbine),
            pair_row * depth_z,
            pair_col * span_y,
            pair_blk * BX,
        ],
        axis=1,
    ).astype(jnp.float32)
    local_pair = (pair_row == level) & (pair_col == column)
    slot_select = arrange(local_pair[:, None], capacity)
    turb_hot = (pair_turb[:, None] == jnp.arange(turbines, dtype=jnp.int32)[None, :]).astype(
        jnp.float32
    )
    block_hot = (pair_blk[:, None] == jnp.arange(blocks_x, dtype=jnp.int32)[None, :]).astype(
        jnp.float32
    )
    brick_pick = jnp.dot(
        slot_select, block_hot, precision=PRECISE, preferred_element_type=jnp.float32
    )
    grid_bricks = velocity.reshape(depth_z, span_y, blocks_x, BX)
    local_bricks = jnp.einsum(
        "sb,zybx->szyx",
        brick_pick,
        grid_bricks,
        precision=PRECISE,
        preferred_element_type=jnp.float32,
    )
    slot_geometry = jnp.dot(
        slot_select, pair_geometry, precision=PRECISE, preferred_element_type=jnp.float32
    )
    filled = jnp.sum(slot_select, axis=1)
    height = jnp.arange(depth_z, dtype=jnp.int32).astype(jnp.float32)
    across = jnp.arange(span_y, dtype=jnp.int32).astype(jnp.float32)
    along_cells = jnp.arange(BX, dtype=jnp.int32).astype(jnp.float32)
    rel_z = (slot_geometry[:, 3, None] + height[None, :] - slot_geometry[:, 0, None])[
        :, :, None, None
    ]
    rel_y = (slot_geometry[:, 4, None] + across[None, :] - slot_geometry[:, 1, None])[
        :, None, :, None
    ]
    rel_x = (slot_geometry[:, 5, None] + along_cells[None, :] - slot_geometry[:, 2, None])[
        :, None, None, :
    ]
    weights = filled[:, None, None, None] * disk_weights(rel_z, rel_y, rel_x, radius)
    slot_numer = jnp.sum(
        weights * (wind_profile[None, :, None, None] + local_bricks), axis=(1, 2, 3)
    )
    slot_denom = jnp.sum(weights, axis=(1, 2, 3))
    slot_turb = jnp.dot(
        slot_select, turb_hot, precision=PRECISE, preferred_element_type=jnp.float32
    )
    numerator = jnp.dot(
        slot_numer, slot_turb, precision=PRECISE, preferred_element_type=jnp.float32
    )
    denominator = jnp.dot(
        slot_denom, slot_turb, precision=PRECISE, preferred_element_type=jnp.float32
    )
    numerator, denominator = lax.psum((numerator, denominator), ("py", "pz"))
    rotor_speed = numerator / denominator
    thrust = -0.5 * thrust_coef * rotor_speed * jnp.abs(rotor_speed)
    pair_thrust = jnp.dot(turb_hot, thrust, precision=PRECISE, preferred_element_type=jnp.float32)
    slot_thrust = jnp.dot(
        slot_select, pair_thrust, precision=PRECISE, preferred_element_type=jnp.float32
    )
    pushed = weights * slot_thrust[:, None, None, None]
    force = jnp.einsum(
        "sb,szyx->zybx", brick_pick, pushed, precision=PRECISE, preferred_element_type=jnp.float32
    )
    return (force.reshape(depth_z, span_y, length_x), rotor_speed)


def body(velocity, wind_profile, thrust_coef, turbine_bricks, turbine_offset):
    depth_z, span_y, length_x = velocity.shape
    length_y = span_y * lax.axis_size("py")
    length_z = depth_z * lax.axis_size("pz")
    first_y, second_y = tables(length_y, 0, length_y)
    matrix_y = VISCOSITY * second_y - CROSS_WIND * first_y
    first_z, second_z = tables(length_z, 0, length_z)
    matrix_z = VISCOSITY * second_z
    received = lax.all_to_all(velocity, "py", split_axis=2, concat_axis=1, tiled=True)
    term_y = jnp.einsum(
        "zjx,ji->zix", received, matrix_y, precision=PRECISE, preferred_element_type=jnp.float32
    )
    vertical_received = lax.all_to_all(received, "pz", split_axis=1, concat_axis=0, tiled=True)
    term_z = jnp.einsum(
        "jab,ji->iab",
        vertical_received,
        matrix_z,
        precision=PRECISE,
        preferred_element_type=jnp.float32,
    )
    back_z = lax.all_to_all(term_z, "pz", split_axis=0, concat_axis=1, tiled=True)
    summed_y = term_y + back_z
    back_y = lax.all_to_all(summed_y, "py", split_axis=1, concat_axis=2, tiled=True)
    term_x = along_x(velocity, wind_profile)
    force, rotor_speed = disk_force(
        velocity, wind_profile, thrust_coef, turbine_bricks, turbine_offset
    )
    tendency = term_x + back_y + force
    return (tendency, rotor_speed)


def solution(mesh):
    return jax.shard_map(
        body,
        mesh=mesh,
        in_specs=(P("pz", "py", None), P("pz"), P(), P(), P()),
        out_specs=(P("pz", "py", None), P()),
        check_vma=False,
    )
```

profile of v0, /device:TPU:1, one launch (start us, length us, event | category | flops | bytes accessed | tf_op | source)
XLA Modules:
  0.0 426.1 jit_solution(15084412837382969558)
XLA Ops:
  0.6 9.6 %copy.83 = f32[12,24,1536]{1,0,2:T(8,128)} copy(f32[12,24,1536]{2,1,0:T(8,128)} %param.5) | data formatting | bytes 3538944 | tf_op args[0]
  10.2 11.4 %reshape.661 = f32[16,1,27648]{2,1,0:T(1,128)} reshape(f32[1536,12,24]{2,1,0:T(8,128)} %bitcast.129) | data formatting | bytes 3538944
  21.6 10.1 %all-to-all-start = ((f32[16,1,27648]{2,1,0:T(1,128)}), f32[16,1,27648]{2,1,0:T(1,128)S(1)}, u32[]{:S(2)}, u32[]{:S(2)}) async-start(f32[16,1,27648]{2,1,0:T(1,128)} %reshape.661), calls=%async_computation | async-start | bytes 3538944 | tf_op jit(solution)/shard_map/all_to_all | solution.py:183
  33.5 1.5 div.155
  35.0 1.5 div.153
  40.7 1.5 div.151
  42.2 1.7 reshape.645
  47.9 1.5 rem.419
  49.4 1.5 rem.449
  50.9 1.5 div.159
  53.8 1.5 div.158
  68.8 1.5 stack_reshape.9
  71.6 1.5 stack_reshape.10
  74.4 1.5 stack_reshape.11
  81.7 4.8 %multiply_reduce_fusion = f32[24]{0:T(128)S(1)} fusion(f32[24,12,1,1]{0,1,3,2:T(8,128)} %convolution_bitcast_fusion, f32[12,24,12,128]{3,2,1,0:T(8,128)} %reshape.645, f32[12]{0:T(128)} %param.6, f32[24,12,24]{0,2,1:T(8,128)S(1)} %add_divide_fusion, f32[24,128]{1,0:T(8,128)S(1)} %multiply_exponential_fusion, f32[24]{0:T(128)S(1)} %convert_reduce_fusion), kind=kOutput, calls=%fused_computation.6 | convolution fusion | flops 131825640 | bytes 1810800 | tf_op jit(solution)/shard_map/sb,zybx->szyx/dot_general | solution.py:124
  89.0 77.8 %all-reduce.1 = (f32[100]{0:T(128)}, f32[100]{0:T(128)}) all-reduce(f32[100]{0:T(128)} %convolution_bitcast_fusion.4, f32[100]{0:T(128)} %convolution_bitcast_fusion.3), channel_id=1, replica_groups=mesh['py'=16,'pz'=16] {'py','pz'}, use_global_device_ids=true, to_apply=%region_4.5 | all-reduce | flops 200 | bytes 1600 | tf_op jit(solution)/shard_map/psum | solution.py:161
  170.4 14.8 %fusion.77 = f32[288,384]{1,0:T(8,128)} fusion(f32[288,1536]{1,0:T(8,128)S(1)} %bitcast.137, s32[384]{0:T(512)S(1)} %iota_add_fusion), kind=kOutput, calls=%fused_computation.107 | convolution fusion | flops 2056716288 | bytes 2213376 | tf_op jit(solution)/shard_map/dot_general | solution.py:73
  185.3 14.6 %fusion.74 = f32[288,384]{1,0:T(8,128)} fusion(f32[288,1536]{1,0:T(8,128)S(1)} %bitcast.138, s32[384]{0:T(512)S(1)} %iota_add_fusion.1), kind=kOutput, calls=%fused_computation.106 | convolution fusion | flops 2056716288 | bytes 2213376 | tf_op jit(solution)/shard_map/dot_general | solution.py:73
  200.4 4.9 %reduce.2 = f32[16,27648]{1,0:T(8,128)S(1)} reduce(f32[16,1,27648]{2,1,0:T(1,128)S(1)} %all-to-all-done, f32[]{:T(128)} %broadcast.883), dimensions={1}, to_apply=%all_to_all.52.reduce_sub_computation | reduce | bytes 3538948 | tf_op jit(solution)/shard_map/all_to_all | solution.py:183
  205.3 11.4 %reshape.662 = f32[1536,12,24]{2,1,0:T(8,128)} reshape(f32[16,27648]{1,0:T(8,128)S(1)} %reduce.2) | data formatting | bytes 3538944
  216.7 9.9 %copy.111 = f32[12,24,16,96]{3,0,1,2:T(8,128)} copy(f32[12,24,16,96]{1,0,3,2:T(8,128)} %bitcast.127) | data formatting | bytes 3538944 | tf_op jit(solution)/shard_map/all_to_all | solution.py:183
  226.5 4.1 all-to-all-start.1
  230.7 16.1 %fusion.68 = f32[288,384]{1,0:T(8,128)} fusion(f32[288,1536]{1,0:T(8,128)} %bitcast.136), kind=kOutput, calls=%fused_computation.104 | convolution fusion | flops 2056716288 | bytes 2211840 | tf_op jit(solution)/shard_map/dot_general | solution.py:73
  246.8 14.7 %fusion.71 = f32[288,384]{1,0:T(8,128)} fusion(f32[288,1536]{1,0:T(8,128)S(1)} %bitcast.139, s32[384]{0:T(512)S(1)} %copy-done.17), kind=kOutput, calls=%fused_computation.105 | convolution fusion | flops 2056716288 | bytes 2213376 | tf_op jit(solution)/shard_map/dot_general | solution.py:73
  261.6 9.0 %all-to-all-done.1 = f32[12,384,96]{2,0,1:T(8,128)S(1)} async-done(((f32[12,384,96]{2,0,1:T(8,128)}), f32[12,384,96]{2,0,1:T(8,128)S(1)}, u32[]{:S(2)}, u32[]{:S(2)}) %all-to-all-start.1) | async-done | bytes 1769504 | tf_op jit(solution)/shard_map/all_to_all | solution.py:187
  271.3 3.2 fusion.31
  274.6 2.7 copy.90
  277.3 8.8 %all-to-all-start.2 = ((f32[192,24,96]{2,1,0:T(8,128)}), f32[192,24,96]{2,1,0:T(8,128)}, u32[]{:S(2)}, u32[]{:S(2)}) async-start(f32[192,24,96]{2,1,0:T(8,128)} %copy.90), calls=%async_computation.2 | async-start | bytes 4718592 | tf_op jit(solution)/shard_map/all_to_all | solution.py:195
  286.1 4.1 fusion.65
  290.2 3.2 reshape.646
  293.4 15.1 %fusion.80 = f32[288,384]{1,0:T(8,128)} fusion(f32[288,1536]{1,0:T(8,128)S(1)} %bitcast.140), kind=kOutput, calls=%fused_computation.108 | convolution fusion | flops 2056716288 | bytes 2211840 | tf_op jit(solution)/shard_map/dot_general | solution.py:70
  308.5 8.1 %copy.84 = f32[12,24,16,96]{3,1,2,0:T(8,128)S(1)} copy(f32[12,24,16,96]{1,0,3,2:T(8,128)} %bitcast.128) | data formatting | bytes 3538944 | tf_op jit(solution)/shard_map/all_to_all | solution.py:183
  316.6 1.8 copy.85
  318.4 8.9 %fusion.140 = f32[384,1152]{0,1} fusion(f32[384,1152]{0,1:T(8,128)} %bitcast.146), kind=kOutput, calls=%fused_computation.167 | convolution fusion | flops 2044035072 | bytes 3538944
  327.4 1.9 copy.91
  329.3 1.8 copy.92
  331.1 2.2 add.315
  333.3 2.4 copy.93
  335.7 9.1 %all-to-all-start.3 = ((f32[12,384,96]{2,0,1:T(8,128)}), f32[12,384,96]{2,0,1:T(8,128)S(1)}, u32[]{:S(2)}, u32[]{:S(2)}) async-start(f32[12,384,96]{2,0,1:T(8,128)} %copy.93), calls=%async_computation.3 | async-start | bytes 6291456 | tf_op jit(solution)/shard_map/all_to_all | solution.py:197
  344.9 3.0 maximum_multiply_fusion
  347.9 14.8 %fusion.89 = f32[288,384]{1,0:T(8,128)S(1)} fusion(f32[288,1536]{1,0:T(8,128)S(1)} %bitcast.141, s32[384]{0:T(512)S(1)} %copy-done.21), kind=kOutput, calls=%fused_computation.111 | convolution fusion | flops 2056716288 | bytes 2213376 | tf_op jit(solution)/shard_map/dot_general | solution.py:70
  362.7 14.5 %fusion.86 = f32[288,384]{1,0:T(8,128)S(1)} fusion(f32[288,1536]{1,0:T(8,128)S(1)} %bitcast.142, s32[384]{0:T(512)S(1)} %copy-done.19), kind=kOutput, calls=%fused_computation.110 | convolution fusion | flops 2056716288 | bytes 2213376 | tf_op jit(solution)/shard_map/dot_general | solution.py:70
  377.2 14.6 %fusion.83 = f32[288,384]{1,0:T(8,128)S(1)} fusion(f32[288,1536]{1,0:T(8,128)S(1)} %bitcast.143, s32[384]{0:T(512)S(1)} %copy-done.17), kind=kOutput, calls=%fused_computation.109 | convolution fusion | flops 2056716288 | bytes 2213376 | tf_op jit(solution)/shard_map/dot_general | solution.py:70
  391.8 1.5 pad_maximum_fusion
  393.3 22.3 %all-to-all-done.3 = f32[12,384,96]{2,0,1:T(8,128)S(1)} async-done(((f32[12,384,96]{2,0,1:T(8,128)}), f32[12,384,96]{2,0,1:T(8,128)S(1)}, u32[]{:S(2)}, u32[]{:S(2)}) %all-to-all-start.3) | async-done | bytes 1769504 | tf_op jit(solution)/shard_map/all_to_all | solution.py:197
  415.6 2.8 copy.95
  418.4 3.5 all_to_all.67
  421.9 4.0 add_add_fusion
  (114 shorter events, 40.5 us)
Async XLA Ops:
  21.6 10.1 %copy-start.10 = (s32[100,4]{0,1:T(4,128)S(1)}, s32[100,4]{0,1:T(4,128)}, u32[]{:S(2)}) copy-start(s32[100,4]{0,1:T(4,128)} %param.8) | copy-start | bytes 4804
  21.6 20.6 %copy-start = (f32[12,24,1536]{2,1,0:T(8,128)S(1)}, f32[12,24,1536]{2,1,0:T(8,128)}, u32[]{:S(2)}) copy-start(f32[12,24,1536]{2,1,0:T(8,128)} %param.5) | copy-start | bytes 5308420
  21.6 178.3 %all-to-all-start = ((f32[16,1,27648]{2,1,0:T(1,128)}), f32[16,1,27648]{2,1,0:T(1,128)S(1)}, u32[]{:S(2)}, u32[]{:S(2)}) async-start(f32[16,1,27648]{2,1,0:T(1,128)} %reshape.661), calls=%async_computation | async-start | bytes 3538944 | tf_op jit(solution)/shard_map/all_to_all | solution.py:183
  32.2 4.3 %copy-start.13 = (pred[100,4]{0,1:T(4,128)(4,1)}, pred[100,4]{0,1:T(4,128)(4,1)S(1)}, u32[]{:S(2)}) copy-start(pred[100,4]{0,1:T(4,128)(4,1)S(1)} %get-tuple-element.7) | copy-start | bytes 1204
  64.8 12.4 %copy-start.14 = (s32[400]{0:T(512)}, s32[400]{0:T(512)S(1)}, u32[]{:S(2)}) copy-start(s32[400]{0:T(512)S(1)} %eq.211) | copy-start | bytes 4804
  65.6 0.9 copy-start.11
  65.6 1.8 copy-start.22
  80.2 7.0 %copy-start.6 = (f32[24,12,24]{0,2,1:T(8,128)}, f32[24,12,24]{0,2,1:T(8,128)S(1)}, u32[]{:S(2)}) copy-start(f32[24,12,24]{0,2,1:T(8,128)S(1)} %add_divide_fusion) | copy-start | bytes 82948
  81.7 5.5 %copy-start.15 = (f32[24]{0:T(128)}, f32[24]{0:T(128)S(1)}, u32[]{:S(2)}) copy-start(f32[24]{0:T(128)S(1)} %convert_reduce_fusion) | copy-start | bytes 292
  81.7 4.8 %copy-start.9 = (f32[24,100]{1,0:T(8,128)S(1)}, f32[24,100]{1,0:T(8,128)}, u32[]{:S(2)}) copy-start(f32[24,100]{1,0:T(8,128)} %fusion.178) | copy-start | bytes 28804
  81.7 87.4 %copy-start.12 = (s32[400]{0:T(512)S(1)}, s32[400]{0:T(512)}, u32[]{:S(2)}) copy-start(s32[400]{0:T(512)} %copy-done.11) | copy-start | bytes 4804
  167.5 2.9 copy-start.24
  167.5 17.7 %copy-start.20 = (s32[384]{0:T(512)}, s32[384]{0:T(512)S(1)}, u32[]{:S(2)}) copy-start(s32[384]{0:T(512)S(1)} %iota_add_fusion) | copy-start | bytes 4612
  167.6 17.7 %copy-start.18 = (s32[384]{0:T(512)}, s32[384]{0:T(512)S(1)}, u32[]{:S(2)}) copy-start(s32[384]{0:T(512)S(1)} %iota_add_fusion.1) | copy-start | bytes 4612
  226.5 44.0 %all-to-all-start.1 = ((f32[12,384,96]{2,0,1:T(8,128)}), f32[12,384,96]{2,0,1:T(8,128)S(1)}, u32[]{:S(2)}, u32[]{:S(2)}) async-start(f32[12,384,96]{2,0,1:T(8,128)} %bitcast.132), calls=%async_computation.1 | async-start | bytes 6291456 | tf_op jit(solution)/shard_map/all_to_all | solution.py:187
  230.7 16.1 %copy-start.1 = (f32[12,24,1536]{2,1,0:T(8,128)S(1)}, f32[12,24,1536]{2,1,0:T(8,128)}, u32[]{:S(2)}) copy-start(f32[12,24,1536]{2,1,0:T(8,128)} %param.5) | copy-start | bytes 5308420
  230.7 16.1 %copy-start.17 = (s32[384]{0:T(512)S(1)}, s32[384]{0:T(512)}, u32[]{:S(2)}) copy-start(s32[384]{0:T(512)} %iota_add_fusion.2) | copy-start | bytes 4612
  277.3 8.8 %copy-start.7 = (f32[24,12,24]{0,2,1:T(8,128)S(1)}, f32[24,12,24]{0,2,1:T(8,128)}, u32[]{:S(2)}) copy-start(f32[24,12,24]{0,2,1:T(8,128)} %copy-done.6) | copy-start | bytes 82948
  277.3 8.8 %copy-start.16 = (f32[24]{0:T(128)S(1)}, f32[24]{0:T(128)}, u32[]{:S(2)}) copy-start(f32[24]{0:T(128)} %copy-done.15) | copy-start | bytes 292
  277.3 8.8 %copy-start.25 = (f32[24,12,1,1]{0,1,3,2:T(8,128)S(1)}, f32[24,12,1,1]{0,1,3,2:T(8,128)}, u32[]{:S(2)}) copy-start(f32[24,12,1,1]{0,1,3,2:T(8,128)} %convolution_bitcast_fusion) | copy-start | bytes 3460
  277.3 8.8 %copy-start.26 = (f32[24]{0:T(128)S(1)}, f32[24]{0:T(128)}, u32[]{:S(2)}) copy-start(f32[24]{0:T(128)} %convolution_bitcast_fusion.2) | copy-start | bytes 292
  277.3 50.1 %all-to-all-start.2 = ((f32[192,24,96]{2,1,0:T(8,128)}), f32[192,24,96]{2,1,0:T(8,128)}, u32[]{:S(2)}, u32[]{:S(2)}) async-start(f32[192,24,96]{2,1,0:T(8,128)} %copy.90), calls=%async_computation.2 | async-start | bytes 4718592 | tf_op jit(solution)/shard_map/all_to_all | solution.py:195
  290.2 3.2 copy-start.2
  335.7 79.9 %all-to-all-start.3 = ((f32[12,384,96]{2,0,1:T(8,128)}), f32[12,384,96]{2,0,1:T(8,128)S(1)}, u32[]{:S(2)}, u32[]{:S(2)}) async-start(f32[12,384,96]{2,0,1:T(8,128)} %copy.93), calls=%async_computation.3 | async-start | bytes 6291456 | tf_op jit(solution)/shard_map/all_to_all | solution.py:197
  344.8 3.1 copy-start.3
  344.8 3.1 copy-start.21
  347.9 14.8 %copy-start.19 = (s32[384]{0:T(512)S(1)}, s32[384]{0:T(512)}, u32[]{:S(2)}) copy-start(s32[384]{0:T(512)} %copy-done.18) | copy-start | bytes 4612
  377.2 14.6 %copy-start.8 = (f32[288,384]{1,0:T(8,128)S(1)}, f32[288,384]{1,0:T(8,128)}, u32[]{:S(2)}) copy-start(f32[288,384]{1,0:T(8,128)} %fusion.80) | copy-start | bytes 1327108
  418.4 3.5 copy-start.4
  418.4 3.5 copy-start.5
  418.4 3.5 copy-start.23
where the time goes:
time: 434 us; the launch traced here: 426 us
  matrix products  146 us (34%)
  local copies, waits for them, and re-layouts  108 us (25%)
  blocking collectives  77.8 us (18%)
  starting transfers between devices  32.2 us (7%)
  waiting for transfers between devices  31.4 us (7%)
  other arithmetic  28.7 us (7%)
    psum x1, blocking collectives, disk_force(): numerator, denominator = lax.psum((numerator, denominator), ('py', 'pz'))  77.8 us
    dot_general x4, matrix products, along_x(): jnp.dot(flattened, second_table, precision=PRECISE, preferred_element_typ...  60.3 us
    dot_general x4, matrix products, along_x(): jnp.dot(flattened, first_table, precision=PRECISE, preferred_element_type...  58.9 us
    unnamed x57, local copies, waits for them, and re-layouts  32.5 us
    all_to_all x1, waiting for transfers between devices, body(): lax.all_to_all(summed_y, 'py', split_axis=1, concat_axis=2, tiled=True)  22.3 us
    all_to_all x4, local copies, waits for them, and re-layouts, body(): lax.all_to_all(velocity, 'py', split_axis=2, concat_axis=1, tiled=True)  20.3 us
    all_to_all x1, starting transfers between devices, body(): lax.all_to_all(velocity, 'py', split_axis=2, concat_axis=1, tiled=True)  10.1 us
    all_to_all x1, starting transfers between devices, body(): lax.all_to_all(summed_y, 'py', split_axis=1, concat_axis=2, tiled=True)  9.13 us
  transfers between devices with their start and end apart: 4, of which 2 were waited for; matrix products, arithmetic and copies ran while one was open for 49% of the time, Pallas kernels for 0%

commit v1 on v0

v1 whole, which is shorter than its diff:
```python
import math

import jax
import jax.numpy as jnp
import ml_dtypes
import numpy as np
from jax import lax
from jax.experimental import pallas as pl
from jax.experimental.pallas import tpu as pltpu
from jax.sharding import PartitionSpec as P

NX, NY, NZ, BX = 1536, 384, 192, 128
TURB = 100
N = 16
DZ, DY, XB = NZ // N, NY // N, NX // BX
HALF = NX // 2
VISCOSITY = 0.2
CROSS_WIND = 0.4
DISK_DEPTH = 1.5
RADIUS = 0.6 * DZ
F32, BF16 = jnp.float32, jnp.bfloat16
VM = pl.BlockSpec(memory_space=pltpu.VMEM)
SM = pl.BlockSpec(memory_space=pltpu.SMEM)
ROUTES = (("x", "y", (0, 1, 2, 3, 4)), ("y", "x", (5, 6, 7, 8)))


def params(mib=40):
    return pltpu.CompilerParams(vmem_limit_bytes=mib * 1024 * 1024)


def kernels_of(length):
    m = np.arange(length)
    m = np.where(m > length // 2, m - length, m).astype(np.float64)
    parity = np.where(m % 2 == 0, 1.0, -1.0)
    angle = math.pi / length * m
    sine = np.where(m == 0, 1.0, np.sin(angle))
    first = np.where(m == 0, 0.0, math.pi / length * parity * np.cos(angle) / sine)
    second = np.where(
        m == 0,
        -math.pi**2 / 3.0 - 2.0 * math.pi**2 / (3.0 * length * length),
        -(2.0 * math.pi**2 / (length * length)) * parity / (sine * sine),
    )
    return first, second


def split(table):
    high = table.astype(np.float32).astype(ml_dtypes.bfloat16)
    low = (table - high.astype(np.float64)).astype(np.float32).astype(ml_dtypes.bfloat16)
    return high, low


def x_tables():
    first, second = kernels_of(NX)
    source, target = np.arange(HALF)[:, None], np.arange(HALF)[None, :]
    near, far = (target - source) % NX, (target - source + HALF) % NX
    mats = []
    for sign in (1.0, -1.0):
        for table in (VISCOSITY * second, first):
            mats.extend(split(0.5 * (table[near] + sign * table[far])))
    stacked = np.stack(mats)
    return np.ascontiguousarray(
        stacked.reshape(8, HALF, 3, 256).transpose(2, 0, 1, 3)
    )


def y_matrix():
    first, second = kernels_of(NY)
    i = np.arange(NY)
    return split((VISCOSITY * second - CROSS_WIND * first)[(i[:, None] - i[None, :]) % NY])


def z_matrix():
    _, second = kernels_of(NZ)
    row = np.arange(N * 2 * DZ)
    block, inner = row // (2 * DZ), row % (2 * DZ)
    half, height = inner // DZ, block * DZ + inner % DZ
    table = VISCOSITY * second[(height[:, None] - height[None, :]) % NZ]
    return split(np.where(half[:, None] == half[None, :], table, 0.0))


def halves(value):
    high = value.astype(BF16)
    return high, (value - high.astype(F32)).astype(BF16)


def dot(a, b):
    return jnp.dot(a, b, preferred_element_type=F32)


def x_kernel(wind_ref, v_ref, table_ref, out_ref, lhs_ref):
    step = pl.program_id(0)
    rows = DZ * DY

    @pl.when(step == 0)
    def _():
        low_x = v_ref[:, :, :HALF].reshape(rows, HALF)
        high_x = v_ref[:, :, HALF:].reshape(rows, HALF)
        for part, value in enumerate((low_x + high_x, low_x - high_x)):
            high, low = halves(value)
            lhs_ref[part, :rows] = high
            lhs_ref[part, rows:] = low

    terms = []
    for part in range(2):
        lhs = lhs_ref[part]
        got = []
        for which in range(2):
            both = dot(lhs, table_ref[0, 4 * part + 2 * which])
            extra = dot(lhs[:rows], table_ref[0, 4 * part + 2 * which + 1])
            got.append((both[:rows] + both[rows:] + extra).reshape(DZ, DY, 256))
        terms.append(got)
    here = pl.ds(pl.multiple_of(step * 256, 256), 256)
    there = pl.ds(pl.multiple_of(HALF + step * 256, 256), 256)
    for z in range(DZ):
        even = terms[0][0][z] - wind_ref[z] * terms[0][1][z]
        odd = terms[1][0][z] - wind_ref[z] * terms[1][1][z]
        out_ref[z, :, here] = even + odd
        out_ref[z, :, there] = even - odd


def along_x(velocity, wind):
    tables = jnp.asarray(x_tables())
    return pl.pallas_call(
        x_kernel,
        grid=(3,),
        in_specs=[
            SM,
            pl.BlockSpec((DZ, DY, NX), lambda i: (0, 0, 0)),
            pl.BlockSpec((1, 8, HALF, 256), lambda i: (i, 0, 0, 0)),
        ],
        out_specs=pl.BlockSpec((DZ, DY, NX), lambda i: (0, 0, 0)),
        out_shape=jax.ShapeDtypeStruct((DZ, DY, NX), F32),
        scratch_shapes=[pltpu.VMEM((2, 2 * DZ * DY, HALF), BF16)],
        compiler_params=params(),
        cost_estimate=pl.CostEstimate(
            flops=2 * 288 * 768 * 768 * 12, bytes_accessed=13 * 2**20, transcendentals=0
        ),
        name="x_derivative",
    )(wind, velocity, tables)


def y_pack_kernel(v_ref, out_ref):
    for local in range(36):
        d, j = local // 9, local % 9
        z, xb = local // XB, local % XB
        for yt in range(3):
            out_ref[d, yt * 9 + j] = v_ref[z, yt * 8 : yt * 8 + 8, xb * BX : xb * BX + BX]


def y_pack(velocity):
    return pl.pallas_call(
        y_pack_kernel,
        grid=(4,),
        in_specs=[pl.BlockSpec((3, DY, NX), lambda i: (i, 0, 0))],
        out_specs=pl.BlockSpec((4, 27, 8, BX), lambda i: (i, 0, 0, 0)),
        out_shape=jax.ShapeDtypeStruct((N, 27, 8, BX), F32),
        compiler_params=params(16),
        name="y_pack",
    )(velocity)


def line_product(high_ref, low_ref, read, write):
    for group in range(3):
        tiles = [read(group * 3 + k) for k in range(3)]
        high, low = halves(jnp.concatenate(tiles, axis=1))
        got = dot(high_ref[...], high) + dot(low_ref[...], high) + dot(high_ref[...], low)
        for k in range(3):
            write(group * 3 + k, got[:, k * BX : k * BX + BX])


def y_kernel(high_ref, low_ref, in_ref, sums_ref, out_ref):
    def read(j):
        return jnp.stack([in_ref[:, yt * 9 + j] for yt in range(3)], axis=1).reshape(NY, BX)

    def write(j, value):
        value = value.reshape(N, 3, 8, BX)
        for yt in range(3):
            out_ref[:, yt * 9 + j] = value[:, yt]

    line_product(high_ref, low_ref, read, write)
    for d in range(N):
        out_ref[d, 27] = sums_ref[...]


def y_lines(received, sums):
    high, low = y_matrix()
    return pl.pallas_call(
        y_kernel,
        in_specs=[VM] * 4,
        out_specs=VM,
        out_shape=jax.ShapeDtypeStruct((N, 28, 8, BX), F32),
        compiler_params=params(),
        name="y_lines",
    )(jnp.asarray(high), jnp.asarray(low), received, sums)


def device_at(route, place_first, place_second):
    return place_first * 4 + place_second if route[0] == "x" else place_second * 4 + place_first


def places(route, where_ref):
    x, y = where_ref[1], where_ref[2]
    return (x, y) if route[0] == "x" else (y, x)


def tiles_of(route):
    return 3 * len(route[2])


def columns_of(device, j, h):
    y = (device // 2) * 3 + j // 3
    xb = ((device % 2) * 2 + h) * 3 + j % 3
    return y, xb


def z_pack_kernel(where_ref, in_ref, sums_ref, *refs):
    out_refs, v_ref = refs[:8], refs[8]
    for xb in range(XB):
        v_ref[xb] = in_ref[:, xb * BX : xb * BX + BX]
    for r, route in enumerate(ROUTES):
        first, second = places(route, where_ref)
        width = len(route[2])
        for k1 in range(4):
            out = out_refs[r * 4 + k1]
            out[4 * 3 * width] = sums_ref[...]
            for k2 in range(4):
                device = device_at(route, (first + k1) % 4, (second + k2) % 4)
                for n, j in enumerate(route[2]):
                    y, low_cols = columns_of(device, j, 0)
                    y, high_cols = columns_of(device, j, 1)
                    base = k2 * 3 * width + n
                    out[base] = v_ref[low_cols, pl.ds(y, 8, stride=DY), :]
                    out[base + width, 0:4] = v_ref[low_cols, pl.ds(y + 8 * DY, 4, stride=DY), :]
                    out[base + width, 4:8] = v_ref[high_cols, pl.ds(y, 4, stride=DY), :]
                    out[base + 2 * width] = v_ref[high_cols, pl.ds(y + 4 * DY, 8, stride=DY), :]


def z_pack(where, velocity, sums):
    shapes = []
    for route in ROUTES:
        shapes += [jax.ShapeDtypeStruct((4 * tiles_of(route) + 1, 8, BX), F32)] * 4
    return pl.pallas_call(
        z_pack_kernel,
        in_specs=[SM, VM, VM],
        out_specs=[VM] * 8,
        out_shape=shapes,
        scratch_shapes=[pltpu.VMEM((XB, DZ * DY, BX), F32)],
        compiler_params=params(),
        name="z_pack",
    )(where, velocity.reshape(DZ * DY, NX), sums)


def regroup(arrays, tiles, with_sums):
    def kernel(*refs):
        for i in range(4):
            for k in range(4):
                refs[4 + i][k * tiles : (k + 1) * tiles] = refs[k][i * tiles : (i + 1) * tiles]
            if with_sums:
                last = 4 * tiles
                refs[4 + i][last] = (refs[0][last] + refs[1][last]) + (refs[2][last] + refs[3][last])

    shape = jax.ShapeDtypeStruct((4 * tiles + (1 if with_sums else 0), 8, BX), F32)
    return pl.pallas_call(
        kernel,
        in_specs=[VM] * 4,
        out_specs=[VM] * 4,
        out_shape=[shape] * 4,
        compiler_params=params(16),
        name="regroup",
    )(*arrays)


def shift(value, axis, by):
    moves = []
    for i in range(N):
        x, y = i // 4, i % 4
        moves.append((i, ((x + by) % 4) * 4 + y if axis == "x" else x * 4 + (y + by) % 4))
    return lax.ppermute(value, "pz", moves)


def send_stage(arrays, axis, sign):
    return [arrays[0]] + [shift(arrays[k], axis, sign * k) for k in range(1, 4)]


def z_kernel(where_ref, high_ref, low_ref, *refs):
    ins, outs, sums_ref, lines_ref = refs[:8], refs[8:16], refs[16], refs[17]
    total = None
    for r, route in enumerate(ROUTES):
        first, second = places(route, where_ref)
        tiles, width = tiles_of(route), len(route[2])
        for k2 in range(4):
            got = ins[r * 4 + k2]
            if r == 0:
                total = got[4 * tiles] if total is None else total + got[4 * tiles]
            for k1 in range(4):
                source = device_at(route, (first - k1) % 4, (second - k2) % 4)
                for rt in range(3):
                    at = k1 * tiles + rt * width
                    lines_ref[source, rt * 9 + route[2][0] : rt * 9 + route[2][0] + width] = got[at : at + width]
    sums_ref[...] = total

    def read(j):
        return jnp.stack([lines_ref[:, rt * 9 + j] for rt in range(3)], axis=1).reshape(N * 24, BX)

    def write(j, value):
        value = value.reshape(N, 3, 8, BX)
        for rt in range(3):
            lines_ref[:, rt * 9 + j] = value[:, rt]

    line_product(high_ref, low_ref, read, write)
    for r, route in enumerate(ROUTES):
        first, second = places(route, where_ref)
        tiles, width = tiles_of(route), len(route[2])
        for k2 in range(4):
            for k1 in range(4):
                target = device_at(route, (first - k1) % 4, (second - k2) % 4)
                for rt in range(3):
                    at = k1 * tiles + rt * width
                    outs[r * 4 + k2][at : at + width] = lines_ref[target, rt * 9 + route[2][0] : rt * 9 + route[2][0] + width]


def z_lines(where, arrays):
    high, low = z_matrix()
    shapes = []
    for route in ROUTES:
        shapes += [jax.ShapeDtypeStruct((4 * tiles_of(route), 8, BX), F32)] * 4
    return pl.pallas_call(
        z_kernel,
        in_specs=[SM] + [VM] * 10,
        out_specs=[VM] * 9,
        out_shape=shapes + [jax.ShapeDtypeStruct((8, BX), F32)],
        scratch_shapes=[pltpu.VMEM((N, 27, 8, BX), F32)],
        compiler_params=params(),
        name="z_lines",
    )(where, jnp.asarray(high), jnp.asarray(low), *arrays)


def z_unpack_kernel(where_ref, term_ref, *refs):
    out_ref, sum_ref = refs[8], refs[9]
    for r, route in enumerate(ROUTES):
        first, second = places(route, where_ref)
        width = len(route[2])
        for k1 in range(4):
            got = refs[r * 4 + k1]
            for k2 in range(4):
                device = device_at(route, (first + k1) % 4, (second + k2) % 4)
                for n, j in enumerate(route[2]):
                    y, low_cols = columns_of(device, j, 0)
                    y, high_cols = columns_of(device, j, 1)
                    base = k2 * 3 * width + n
                    for at, count, cols, tile, row in (
                        (0, 8, low_cols, base, 0),
                        (8, 4, low_cols, base + width, 0),
                        (0, 4, high_cols, base + width, 4),
                        (4, 8, high_cols, base + 2 * width, 0),
                    ):
                        spot = pl.ds(y + at * DY, count, stride=DY)
                        sum_ref[cols, spot, :] = got[tile, row : row + count]
    for xb in range(XB):
        cols = slice(xb * BX, xb * BX + BX)
        out_ref[:, cols] = term_ref[:, cols] + sum_ref[xb]


def z_unpack(where, term, arrays):
    return pl.pallas_call(
        z_unpack_kernel,
        in_specs=[SM] + [VM] * 9,
        out_specs=VM,
        out_shape=jax.ShapeDtypeStruct((DZ * DY, NX), F32),
        scratch_shapes=[pltpu.VMEM((XB, DZ * DY, BX), F32)],
        compiler_params=params(),
        name="z_unpack",
    )(where, term.reshape(DZ * DY, NX), *arrays).reshape(DZ, DY, NX)


def sigmoid(value):
    return 1.0 / (1.0 + jnp.exp(-value))


def axial(rel):
    return jnp.exp(-0.5 * (rel / DISK_DEPTH) ** 2)


def radial(rel_z, rel_y):
    return sigmoid((RADIUS * RADIUS - rel_y * rel_y - rel_z * rel_z) / (2.0 * RADIUS))


def disk_kernel(where_ref, brick_ref, offset_ref, wind_ref, lanes_ref, v_ref, sums_ref, denom_ref, disk_ref, slot_ref):
    level, column = where_ref[0], where_ref[3]
    sub = lax.broadcasted_iota(jnp.int32, (8, BX), 0).astype(F32)
    lane = lax.broadcasted_iota(jnp.int32, (8, BX), 1)
    top = lax.broadcasted_iota(jnp.int32, (8, BX), 0) == 0
    sums_ref[...] = jnp.zeros((8, BX), F32)

    centre_z, centre_y, centre_x = (lanes_ref[i : i + 1, :] for i in range(3))

    def add_radial(z, total):
        for yt in range(6):
            total = total + radial(z.astype(F32) - centre_z, sub + (8.0 * yt) - centre_y)
        return total

    area = jnp.sum(lax.fori_loop(0, 2 * DZ, add_radial, jnp.zeros((8, BX), F32)), axis=0, keepdims=True)
    depth = jnp.zeros((8, BX), F32)
    for xt in range(BX // 8):
        depth = depth + axial(sub + (8.0 * xt) - centre_x)
    denom_ref[...] = jnp.broadcast_to(area * jnp.sum(depth, axis=0, keepdims=True), (8, BX))

    for s in range(2 * XB):
        slot_ref[s] = -1

    @pl.when(level < 2)
    def _():
        def place(t, carry):
            base = brick_ref[t, 0]
            left, block = (base // XB) % N, base % XB
            shifted = column - left

            @pl.when((shifted == 0) | (shifted == 1))
            def _():
                slot_ref[shifted * XB + block] = t

            return carry

        lax.fori_loop(0, TURB, place, 0)

        def one(s, carry):
            k, block = s // XB, s % XB
            cols = pl.ds(pl.multiple_of(block * BX, BX), BX)
            t = slot_ref[s]

            @pl.when(t < 0)
            def _():
                for z in range(DZ):
                    disk_ref[k, z, :, cols] = jnp.zeros((DY, BX), F32)

            @pl.when(t >= 0)
            def _():
                base_z = (level * DZ - offset_ref[t, 0]).astype(F32)
                base_y = (k * DY - offset_ref[t, 1]).astype(F32)
                shape_x = axial((lane - offset_ref[t, 2]).astype(F32))
                total = jnp.zeros((8, BX), F32)
                for z in range(DZ):
                    for yt in range(3):
                        weight = shape_x * radial(base_z + float(z), sub + (base_y + 8.0 * yt))
                        disk_ref[k, z, yt * 8 : yt * 8 + 8, cols] = weight
                        total = total + weight * (wind_ref[z] + v_ref[z, yt * 8 : yt * 8 + 8, cols])
                found = jnp.sum(total)
                sums_ref[...] = sums_ref[...] + jnp.where((lane == t) & top, found, 0.0)

            return carry

        lax.fori_loop(0, 2 * XB, one, 0)


def disks(where, bricks, offset, wind, velocity):
    lanes = jnp.pad(offset.T.astype(F32), ((0, 5), (0, BX - TURB)))
    return pl.pallas_call(
        disk_kernel,
        in_specs=[SM, SM, SM, SM, VM, VM],
        out_specs=[VM, VM, VM, SM],
        out_shape=[
            jax.ShapeDtypeStruct((8, BX), F32),
            jax.ShapeDtypeStruct((8, BX), F32),
            jax.ShapeDtypeStruct((2, DZ, DY, NX), F32),
            jax.ShapeDtypeStruct((2 * XB,), jnp.int32),
        ],
        compiler_params=params(),
        name="disks",
    )(where, bricks, offset, wind, lanes, velocity)


def final_kernel(where_ref, slot_ref, terms_ref, lines_ref, sums_ref, denom_ref, coef_ref, disk_ref, out_ref, speed_ref, push_ref):
    level = where_ref[0]

    @pl.when(pl.program_id(0) == 0)
    def _():
        total = sums_ref[0, 0]
        for d in range(1, N):
            total = total + sums_ref[d, 0]
        speed = total[0:1, :] / denom_ref[0:1, :]
        speed_ref[...] = speed
        thrust = -0.5 * coef_ref[...] * speed * jnp.abs(speed)
        lane = lax.broadcasted_iota(jnp.int32, (1, BX), 1)
        for s in range(2 * XB):
            mine = jnp.sum(jnp.where(lane == slot_ref[s], thrust, 0.0), axis=1, keepdims=True)
            push_ref[s] = jnp.broadcast_to(mine, (8, BX))

    def cell(local, yt):
        z, xb = local // XB, local % XB
        rows, cols = slice(yt * 8, yt * 8 + 8), slice(xb * BX, xb * BX + BX)
        return z, xb, rows, cols, terms_ref[z, rows, cols] + lines_ref[local // 9, yt * 9 + local % 9]

    @pl.when(level < 2)
    def _():
        for local in range(36):
            for yt in range(3):
                z, xb, rows, cols, value = cell(local, yt)
                out_ref[z, rows, cols] = (
                    value
                    + push_ref[xb] * disk_ref[0, z, rows, cols]
                    + push_ref[XB + xb] * disk_ref[1, z, rows, cols]
                )

    @pl.when(level >= 2)
    def _():
        for local in range(36):
            for yt in range(3):
                z, xb, rows, cols, value = cell(local, yt)
                out_ref[z, rows, cols] = value


def finish(where, slots, terms, lines, denom, coef, disk):
    return pl.pallas_call(
        final_kernel,
        grid=(4,),
        in_specs=[
            SM,
            SM,
            pl.BlockSpec((3, DY, NX), lambda i: (i, 0, 0)),
            pl.BlockSpec((4, 28, 8, BX), lambda i: (i, 0, 0, 0)),
            pl.BlockSpec((N, 1, 8, BX), lambda i: (0, 27, 0, 0)),
            pl.BlockSpec((8, BX), lambda i: (0, 0)),
            pl.BlockSpec((1, BX), lambda i: (0, 0)),
            pl.BlockSpec((2, 3, DY, NX), lambda i: (0, i, 0, 0)),
        ],
        out_specs=[
            pl.BlockSpec((3, DY, NX), lambda i: (i, 0, 0)),
            pl.BlockSpec((1, BX), lambda i: (0, 0)),
        ],
        out_shape=[jax.ShapeDtypeStruct((DZ, DY, NX), F32), jax.ShapeDtypeStruct((1, BX), F32)],
        scratch_shapes=[pltpu.VMEM((2 * XB, 8, BX), F32)],
        compiler_params=params(),
        name="finish",
    )(where, slots, terms, lines, lines, denom, coef, disk)


def body(velocity, wind, thrust_coef, bricks, offset):
    pz, py = lax.axis_index("pz"), lax.axis_index("py")
    where = jnp.stack([pz, pz // 4, pz % 4, py]).astype(jnp.int32)
    with jax.named_scope("spanwise_send"):
        received = lax.all_to_all(y_pack(velocity), "py", 0, 0, tiled=True)
    sums, denom, disk, slots = disks(where, bricks, offset, wind, velocity)
    packed = z_pack(where, velocity, sums)
    with jax.named_scope("vertical_send"):
        arrived = []
        for r, route in enumerate(ROUTES):
            stage = send_stage(packed[4 * r : 4 * r + 4], route[0], 1)
            stage = regroup(stage, tiles_of(route), True)
            arrived += send_stage(stage, route[1], 1)
    term_x = along_x(velocity, wind)
    *vertical, level_sums = z_lines(where, arrived)
    spanwise = y_lines(received, level_sums)
    with jax.named_scope("spanwise_return"):
        returned = lax.all_to_all(spanwise, "py", 0, 0, tiled=True)
    with jax.named_scope("vertical_return"):
        back = []
        for r, route in enumerate(ROUTES):
            stage = send_stage(vertical[4 * r : 4 * r + 4], route[1], -1)
            stage = regroup(stage, tiles_of(route), False)
            back += send_stage(stage, route[0], -1)
    terms = z_unpack(where, term_x, back)
    coef = jnp.pad(thrust_coef, (0, BX - TURB)).reshape(1, BX)
    tendency, speed = finish(where, slots, terms, returned, denom, coef, disk)
    return tendency, speed[0, :TURB]


def solution(mesh):
    return jax.shard_map(
        body,
        mesh=mesh,
        in_specs=(P("pz", "py", None), P("pz"), P(), P(), P()),
        out_specs=(P("pz", "py", None), P()),
        check_vma=False,
    )
```

time: 434 us -> 131 us (0.30); the launches traced: 426 us -> 130 us
  matrix products: 146 us -> 0 us
  local copies, waits for them, and re-layouts: 108 us -> 17.7 us
  blocking collectives: 77.8 us -> 0 us
  other arithmetic: 28.7 us -> 0.08 us
  Pallas kernels: 0 us -> 26.3 us
  waiting for transfers between devices: 31.4 us -> 47.1 us
  starting transfers between devices: 32.2 us -> 38.2 us
    dot_general x18 -> x0, matrix products: 137 us -> none  [the longest x4 60.3 us: along_x(): jnp.dot(flattened, second_table, precision=PRECISE, preferred_element_typ...]
    psum x1 -> x0, blocking collectives: 77.8 us -> none  [disk_force(): numerator, denominator = lax.psum((numerator, denominator), ('py', 'pz'))]
    ppermute x0 -> x24, waiting for transfers between devices: none -> 42.2 us  [shift(): return lax.ppermute(value, 'pz', moves)]
    all_to_all x9 -> x0, local copies, waits for them, and re-layouts: 31.1 us -> none  [the longest x4 20.3 us: body(): lax.all_to_all(velocity, 'py', split_axis=2, concat_axis=1, tiled=True)]
    all_to_all x4 -> x2, waiting for transfers between devices: 31.4 us -> 4.85 us  [the longest x1 4.85 us: body(): returned = lax.all_to_all(spanwise, 'py', 0, 0, tiled=True)]
    pallas_call x0 -> x12, Pallas kernels: none -> 26.3 us  [the longest x1 10.1 us: disks(): pl.pallas_call(disk_kernel, in_specs=[SM, SM, SM, SM, VM, VM], out_specs=...]
    ppermute x0 -> x24, starting transfers between devices: none -> 21.6 us  [shift(): return lax.ppermute(value, 'pz', moves)]
    all_to_all x4 -> x2, starting transfers between devices: 32.2 us -> 16.6 us  [the longest x1 10.1 us: body(): received = lax.all_to_all(y_pack(velocity), 'py', 0, 0, tiled=True)]
  transfers between devices with their start and end apart: 4 -> 26, of which waited for: 2 -> 13; matrix products, arithmetic and copies ran while one was open for 49% -> 1% of each run, Pallas kernels for 0% -> 17%
where the time goes in v1:
time: 131 us; the launch traced here: 130 us
  waiting for transfers between devices  47.1 us (36%)
  starting transfers between devices  38.2 us (29%)
  Pallas kernels  26.3 us (20%)
  local copies, waits for them, and re-layouts  17.7 us (14%)
    ppermute x24, waiting for transfers between devices, shift(): return lax.ppermute(value, 'pz', moves)  42.2 us
    ppermute x24, starting transfers between devices, shift(): return lax.ppermute(value, 'pz', moves)  21.6 us
    unnamed x42, local copies, waits for them, and re-layouts  17.1 us
    pallas_call x1, Pallas kernels, disks(): pl.pallas_call(disk_kernel, in_specs=[SM, SM, SM, SM, VM, VM], out_specs=...  10.1 us
    all_to_all x1, starting transfers between devices, body(): received = lax.all_to_all(y_pack(velocity), 'py', 0, 0, tiled=True)  10.1 us
    all_to_all x1, starting transfers between devices, body(): returned = lax.all_to_all(spanwise, 'py', 0, 0, tiled=True)  6.47 us
    pallas_call x1, Pallas kernels, along_x(): pl.pallas_call(x_kernel, grid=(3,), in_specs=[SM, pl.BlockSpec((DZ, DY, N...  5.54 us
    all_to_all x1, waiting for transfers between devices, body(): returned = lax.all_to_all(spanwise, 'py', 0, 0, tiled=True)  4.85 us
  transfers between devices with their start and end apart: 26, of which 13 were waited for; matrix products, arithmetic and copies ran while one was open for 1% of the time, Pallas kernels for 17%

profile of v1, /device:TPU:1, one launch (start us, length us, event | category | flops | bytes accessed | tf_op | source)
XLA Modules:
  0.0 130.2 jit_solution(16699827507617479813)
XLA Ops:
  0.6 1.5 %copy-done = f32[12,24,1536]{2,1,0:T(8,128)S(1)} copy-done((f32[12,24,1536]{2,1,0:T(8,128)S(1)}, f32[12,24,1536]{2,1,0:T(8,128)}, u32[]{:S(2)}) %copy-start) | copy-done | bytes 1769496
  2.3 1.2 copy-done.4
  3.5 10.1 %all-to-all-start = ((f32[16,27,8,128]{3,2,1,0:T(8,128)}), f32[16,27,8,128]{3,2,1,0:T(8,128)S(1)}, u32[]{:S(2)}, u32[]{:S(2)}) async-start(f32[16,27,8,128]{3,2,1,0:T(8,128)} %copy-done.4), calls=%async_computation | async-start | bytes 3538944 | tf_op jit(solution)/shard_map/spanwise_send/all_to_all | solution.py:541
  13.6 0.7 copy.12.brick_ref
  14.4 0.7 copy.13.offset_ref
  15.2 0.8 copy-done.13
  16.0 0.8 copy-done.14
  16.8 10.1 %disks.1 = (f32[8,128]{1,0:T(8,128)S(1)}, f32[8,128]{1,0:T(8,128)S(1)}, f32[2,12,24,1536]{3,2,1,0:T(8,128)S(1)}, s32[24]{0:T(128)S(1)}) custom-call(s32[4]{0:T(128)S(1)} %pad_add_fusion.where_ref, s32[100,4]{1,0:T(8,128)S(1)} %copy-done.13, s32[100,3]{1,0:T(8,128)S(1)} %copy-done.14, f32[12]{0:T(128)S(1)} %copy-done.15, f32[8,128]{1,0:T(8,128)S(1)} %pad.8.lanes_ref, ...), custom_call_target="tpu_custom_call" | custom-call | tf_op jit(solution)/shard_map/disks/pallas_call | solution.py:457
  27.0 1.7 %copy-done.7 = f32[2,12,24,1536]{3,2,1,0:T(8,128)} copy-done((f32[2,12,24,1536]{3,2,1,0:T(8,128)}, f32[2,12,24,1536]{3,2,1,0:T(8,128)S(1)}, u32[]{:S(2)}) %copy-start.7) | copy-done | bytes 3538968
  28.7 1.1 z_pack.1
  29.8 1.4 %collective-permute-start.6 = (f32[49,8,128]{2,1,0:T(8,128)S(1)}, f32[49,8,128]{2,1,0:T(8,128)S(1)}, u32[]{:S(2)}, u32[]{:S(2)}) collective-permute-start(f32[49,8,128]{2,1,0:T(8,128)S(1)} %get-tuple-element.52), channel_id=1, source_target_pairs={{0,1},{1,2},{2,3},{3,0},{4,5},{5,6},{6,7},{7,4},{8,9},{9,10},{10,1... | collective-permute-start | bytes 602120 | tf_op jit(solution)/shard_map/vertical_send/ppermute | solution.py:278
  31.2 2.5 %collective-permute-start.8 = (f32[49,8,128]{2,1,0:T(8,128)S(1)}, f32[49,8,128]{2,1,0:T(8,128)S(1)}, u32[]{:S(2)}, u32[]{:S(2)}) collective-permute-start(f32[49,8,128]{2,1,0:T(8,128)S(1)} %get-tuple-element.54), channel_id=1, source_target_pairs={{0,3},{1,0},{2,1},{3,2},{4,7},{5,4},{6,5},{7,6},{8,11},{9,8},{10,9... | collective-permute-start | bytes 602120 | tf_op jit(solution)/shard_map/vertical_send/ppermute | solution.py:278
  33.7 7.4 %collective-permute-done.6.refs_1_ = f32[49,8,128]{2,1,0:T(8,128)S(1)} collective-permute-done((f32[49,8,128]{2,1,0:T(8,128)S(1)}, f32[49,8,128]{2,1,0:T(8,128)S(1)}, u32[]{:S(2)}, u32[]{:S(2)}) %collective-permute-start.6) | collective-permute-done | bytes 200736 | tf_op jit(solution)/shard_map/vertical_send/ppermute | solution.py:278
  41.1 0.9 collective-permute-done.8.refs_3_
  42.1 9.7 %collective-permute-done.refs_1_ = f32[61,8,128]{2,1,0:T(8,128)S(1)} collective-permute-done((f32[61,8,128]{2,1,0:T(8,128)S(1)}, f32[61,8,128]{2,1,0:T(8,128)S(1)}, u32[]{:S(2)}, u32[]{:S(2)}) %collective-permute-start) | collective-permute-done | bytes 249888 | tf_op jit(solution)/shard_map/vertical_send/ppermute | solution.py:278
  52.0 1.6 %collective-permute-start.4 = (f32[61,8,128]{2,1,0:T(8,128)S(1)}, f32[61,8,128]{2,1,0:T(8,128)S(1)}, u32[]{:S(2)}, u32[]{:S(2)}) collective-permute-start(f32[61,8,128]{2,1,0:T(8,128)S(1)} %get-tuple-element.49), channel_id=1, source_target_pairs={{0,2},{1,3},{2,0},{3,1},{4,6},{5,7},{6,4},{7,5},{8,10},{9,11},{10,... | collective-permute-start | bytes 749576 | tf_op jit(solution)/shard_map/vertical_send/ppermute | solution.py:278
  53.6 2.0 %collective-permute-start.5 = (f32[61,8,128]{2,1,0:T(8,128)S(1)}, f32[61,8,128]{2,1,0:T(8,128)S(1)}, u32[]{:S(2)}, u32[]{:S(2)}) collective-permute-start(f32[61,8,128]{2,1,0:T(8,128)S(1)} %get-tuple-element.50), channel_id=1, source_target_pairs={{0,3},{1,0},{2,1},{3,2},{4,7},{5,4},{6,5},{7,6},{8,11},{9,8},{10,9... | collective-permute-start | bytes 749576 | tf_op jit(solution)/shard_map/vertical_send/ppermute | solution.py:278
  55.6 1.5 %collective-permute-start.9 = (f32[49,8,128]{2,1,0:T(8,128)S(1)}, f32[49,8,128]{2,1,0:T(8,128)S(1)}, u32[]{:S(2)}, u32[]{:S(2)}) collective-permute-start(f32[49,8,128]{2,1,0:T(8,128)S(1)} %get-tuple-element.56), channel_id=1, source_target_pairs={{0,4},{1,5},{2,6},{3,7},{4,8},{5,9},{6,10},{7,11},{8,12},{9,13},{1... | collective-permute-start | bytes 602120 | tf_op jit(solution)/shard_map/vertical_send/ppermute | solution.py:278
  57.0 4.2 %collective-permute-done.11.refs_7_ = f32[49,8,128]{2,1,0:T(8,128)S(1)} collective-permute-done((f32[49,8,128]{2,1,0:T(8,128)S(1)}, f32[49,8,128]{2,1,0:T(8,128)S(1)}, u32[]{:S(2)}, u32[]{:S(2)}) %collective-permute-start.11) | collective-permute-done | bytes 200736 | tf_op jit(solution)/shard_map/vertical_send/ppermute | solution.py:278
  61.3 1.2 collective-permute-done.9.refs_5_
  62.5 4.0 %collective-permute-done.3.refs_1_ = f32[61,8,128]{2,1,0:T(8,128)S(1)} collective-permute-done((f32[61,8,128]{2,1,0:T(8,128)S(1)}, f32[61,8,128]{2,1,0:T(8,128)S(1)}, u32[]{:S(2)}, u32[]{:S(2)}) %collective-permute-start.3) | collective-permute-done | bytes 249888 | tf_op jit(solution)/shard_map/vertical_send/ppermute | solution.py:278
  66.5 0.4 collective-permute-done.5.refs_3_
  66.9 3.4 %z_lines.1 = (f32[60,8,128]{2,1,0:T(8,128)S(1)}, f32[60,8,128]{2,1,0:T(8,128)}, f32[60,8,128]{2,1,0:T(8,128)S(1)}, f32[60,8,128]{2,1,0:T(8,128)S(1)}, f32[48,8,1...) custom-call(s32[4]{0:T(128)S(1)} %pad_add_fusion.where_ref, ...), custom_call_target="tpu_custom_call" | custom-call | tf_op jit(solution)/shard_map/z_lines/pallas_call | solution.py:327
  70.4 1.8 %y_lines.1 = f32[16,28,8,128]{3,2,1,0:T(8,128)S(1)} custom-call(bf16[384,384]{1,0:T(8,128)(2,1)S(1)} %copy-done.9, bf16[384,384]{1,0:T(8,128)(2,1)S(1)} %copy-done.10, f32[16,27,8,128]{3,2,1,0:T(8,128)S(1)} %all-to-all-done.in_ref, f32[8,128]{1,0:T(8,128)S(1)} %get-tuple-element.75.sums_ref), custom_call_target="tpu_custom_call" | custom-call | tf_op jit(solution)/shard_map/y_lines/pallas_call | solution.py:187
  72.2 1.2 copy-done.3
  73.4 6.5 %all-to-all-start.1 = ((f32[16,28,8,128]{3,2,1,0:T(8,128)}), f32[16,28,8,128]{3,2,1,0:T(8,128)S(1)}, u32[]{:S(2)}, u32[]{:S(2)}) async-start(f32[16,28,8,128]{3,2,1,0:T(8,128)} %copy-done.3), calls=%async_computation.1 | async-start | bytes 3670016 | tf_op jit(solution)/shard_map/spanwise_return/all_to_all | solution.py:554
  80.1 1.4 %collective-permute-start.20 = (f32[48,8,128]{2,1,0:T(8,128)S(1)}, f32[48,8,128]{2,1,0:T(8,128)S(1)}, u32[]{:S(2)}, u32[]{:S(2)}) collective-permute-start(f32[48,8,128]{2,1,0:T(8,128)S(1)} %get-tuple-element.70), channel_id=1, source_target_pairs={{0,4},{1,5},{2,6},{3,7},{4,8},{5,9},{6,10},{7,11},{8,12},{9,13},{1... | collective-permute-start | bytes 589832 | tf_op jit(solution)/shard_map/vertical_return/ppermute | solution.py:278
  81.5 2.1 %collective-permute-start.12 = (f32[60,8,128]{2,1,0:T(8,128)}, f32[60,8,128]{2,1,0:T(8,128)S(1)}, u32[]{:S(2)}, u32[]{:S(2)}) collective-permute-start(f32[60,8,128]{2,1,0:T(8,128)} %get-tuple-element.60), channel_id=1, source_target_pairs={{0,3},{1,0},{2,1},{3,2},{4,7},{5,4},{6,5},{7,6},{8,11},{9,8},{10,9... | collective-permute-start | bytes 737288 | tf_op jit(solution)/shard_map/vertical_return/ppermute | solution.py:278
  83.6 3.0 %collective-permute-done.18.refs_1_ = f32[48,8,128]{2,1,0:T(8,128)S(1)} collective-permute-done((f32[48,8,128]{2,1,0:T(8,128)}, f32[48,8,128]{2,1,0:T(8,128)S(1)}, u32[]{:S(2)}, u32[]{:S(2)}) %collective-permute-start.18) | collective-permute-done | bytes 196640 | tf_op jit(solution)/shard_map/vertical_return/ppermute | solution.py:278
  86.6 0.4 collective-permute-start.14
  87.0 1.3 collective-permute-done.19.refs_2_
  88.3 4.6 %collective-permute-done.20.refs_3_ = f32[48,8,128]{2,1,0:T(8,128)S(1)} collective-permute-done((f32[48,8,128]{2,1,0:T(8,128)S(1)}, f32[48,8,128]{2,1,0:T(8,128)S(1)}, u32[]{:S(2)}, u32[]{:S(2)}) %collective-permute-start.20) | collective-permute-done | bytes 196640 | tf_op jit(solution)/shard_map/vertical_return/ppermute | solution.py:278
  92.9 2.1 %collective-permute-start.21 = (f32[48,8,128]{2,1,0:T(8,128)S(1)}, f32[48,8,128]{2,1,0:T(8,128)S(1)}, u32[]{:S(2)}, u32[]{:S(2)}) collective-permute-start(f32[48,8,128]{2,1,0:T(8,128)S(1)} %get-tuple-element.72), channel_id=1, source_target_pairs={{0,3},{1,0},{2,1},{3,2},{4,7},{5,4},{6,5},{7,6},{8,11},{9,8},{10,9... | collective-permute-start | bytes 589832 | tf_op jit(solution)/shard_map/vertical_return/ppermute | solution.py:278
  95.2 0.5 collective-permute-start.23
  95.8 2.1 %collective-permute-done.14.refs_3_ = f32[60,8,128]{2,1,0:T(8,128)S(1)} collective-permute-done((f32[60,8,128]{2,1,0:T(8,128)S(1)}, f32[60,8,128]{2,1,0:T(8,128)S(1)}, u32[]{:S(2)}, u32[]{:S(2)}) %collective-permute-start.14) | collective-permute-done | bytes 245792 | tf_op jit(solution)/shard_map/vertical_return/ppermute | solution.py:278
  97.9 3.7 %collective-permute-start.15 = (f32[60,8,128]{2,1,0:T(8,128)S(1)}, f32[60,8,128]{2,1,0:T(8,128)S(1)}, u32[]{:S(2)}, u32[]{:S(2)}) collective-permute-start(f32[60,8,128]{2,1,0:T(8,128)S(1)} %get-tuple-element.64), channel_id=1, source_target_pairs={{0,12},{1,13},{2,14},{3,15},{4,0},{5,1},{6,2},{7,3},{8,4},{9,5},{1... | collective-permute-start | bytes 737288 | tf_op jit(solution)/shard_map/vertical_return/ppermute | solution.py:278
  101.5 1.2 collective-permute-start.16
  102.7 0.8 collective-permute-start.17
  103.5 3.7 %copy-done.16 = bf16[3,8,768,256]{3,2,1,0:T(8,128)(2,1)S(1)} copy-done((bf16[3,8,768,256]{3,2,1,0:T(8,128)(2,1)S(1)}, bf16[3,8,768,256]{3,2,1,0:T(8,128)(2,1)}, u32[]{:S(2)}) %copy-start.16) | copy-done | bytes 9437208
  107.2 5.5 %x_derivative.1 = f32[12,24,1536]{2,1,0:T(8,128)S(1)} custom-call(f32[12]{0:T(128)S(1)} %copy-done.15, f32[12,24,1536]{2,1,0:T(8,128)S(1)} %copy-done.2, bf16[3,8,768,256]{3,2,1,0:T(8,128)(2,1)S(1)} %copy-done.16), custom_call_target="tpu_custom_call" | custom-call | flops 4076863488 | bytes 13631488 | tf_op jit(solution)/shard_map/x_derivative/pallas_call | solution.py:123
  112.8 3.4 %collective-permute-done.17.refs_3_ = f32[60,8,128]{2,1,0:T(8,128)S(1)} collective-permute-done((f32[60,8,128]{2,1,0:T(8,128)S(1)}, f32[60,8,128]{2,1,0:T(8,128)S(1)}, u32[]{:S(2)}, u32[]{:S(2)}) %collective-permute-start.17) | collective-permute-done | bytes 245792 | tf_op jit(solution)/shard_map/vertical_return/ppermute | solution.py:278
  116.2 1.3 z_unpack.1
  117.5 1.2 copy-done.5
  118.7 4.8 %all-to-all-done.1.lines_ref.sums_ref = f32[16,28,8,128]{3,2,1,0:T(8,128)S(1)} async-done(((f32[16,28,8,128]{3,2,1,0:T(8,128)}), f32[16,28,8,128]{3,2,1,0:T(8,128)S(1)}, u32[]{:S(2)}, u32[]{:S(2)}) %all-to-all-start.1) | async-done | bytes 1835040 | tf_op jit(solution)/shard_map/spanwise_return/all_to_all | solution.py:554
  123.5 1.5 %copy-done.6 = f32[288,1536]{1,0:T(8,128)S(1)} copy-done((f32[288,1536]{1,0:T(8,128)S(1)}, f32[288,1536]{1,0:T(8,128)}, u32[]{:S(2)}) %copy-start.6) | copy-done | bytes 1769496
  125.0 2.0 %copy-done.8 = f32[2,12,24,1536]{3,2,1,0:T(8,128)S(1)} copy-done((f32[2,12,24,1536]{3,2,1,0:T(8,128)S(1)}, f32[2,12,24,1536]{3,2,1,0:T(8,128)}, u32[]{:S(2)}) %copy-start.8) | copy-done | bytes 3538968
  127.0 2.7 %finish.1 = (f32[12,24,1536]{2,1,0:T(8,128)}, f32[1,128]{1,0:T(1,128)S(1)}) custom-call(s32[4]{0:T(128)S(1)} %pad_add_fusion.where_ref, s32[24]{0:T(128)S(1)} %get-tuple-element.41.slot_ref, f32[12,24,1536]{2,1,0:T(8,128)S(1)} %bitcast.14, f32[16,28,8,128]{3,2,1,0:T(8,128)S(1)} %all-to-all-done.1.lines_ref.sums_ref, ...), custom_call_target="tpu_custom_call" | custom-call | tf_op jit(solution)/shard_map/finish/pallas_call | solution.py:513
  129.7 0.5 slice_bitcast_fusion
  (63 shorter events, 1.2 us)
Async XLA Ops:
  0.6 1.5 %copy-start = (f32[12,24,1536]{2,1,0:T(8,128)S(1)}, f32[12,24,1536]{2,1,0:T(8,128)}, u32[]{:S(2)}) copy-start(f32[12,24,1536]{2,1,0:T(8,128)} %v_ref.5) | copy-start | bytes 5308420
  2.3 1.2 copy-start.4
  3.5 10.1 %copy-start.18 = (s32[100,4]{0,1:T(4,128)S(1)}, s32[100,4]{0,1:T(4,128)}, u32[]{:S(2)}) copy-start(s32[100,4]{0,1:T(4,128)} %param.13) | copy-start | bytes 4804
  3.5 10.9 %copy-start.17 = (s32[100,3]{0,1:T(4,128)S(1)}, s32[100,3]{0,1:T(4,128)}, u32[]{:S(2)}) copy-start(s32[100,3]{0,1:T(4,128)} %param.14) | copy-start | bytes 3604
  3.5 11.7 %copy-start.1 = (f32[12,24,1536]{2,1,0:T(8,128)S(1)}, f32[12,24,1536]{2,1,0:T(8,128)}, u32[]{:S(2)}) copy-start(f32[12,24,1536]{2,1,0:T(8,128)} %v_ref.5) | copy-start | bytes 5308420
  3.5 11.7 %copy-start.15 = (f32[12]{0:T(128)S(1)}, f32[12]{0:T(128)}, u32[]{:S(2)}) copy-start(f32[12]{0:T(128)} %wind_ref.3) | copy-start | bytes 148
  3.5 66.9 %all-to-all-start = ((f32[16,27,8,128]{3,2,1,0:T(8,128)}), f32[16,27,8,128]{3,2,1,0:T(8,128)S(1)}, u32[]{:S(2)}, u32[]{:S(2)}) async-start(f32[16,27,8,128]{3,2,1,0:T(8,128)} %copy-done.4), calls=%async_computation | async-start | bytes 3538944 | tf_op jit(solution)/shard_map/spanwise_send/all_to_all | solution.py:541
  15.2 0.8 copy-start.13
  16.0 0.8 copy-start.14
  27.0 1.8 %copy-start.7 = (f32[2,12,24,1536]{3,2,1,0:T(8,128)}, f32[2,12,24,1536]{3,2,1,0:T(8,128)S(1)}, u32[]{:S(2)}) copy-start(f32[2,12,24,1536]{3,2,1,0:T(8,128)S(1)} %get-tuple-element.77.disk_ref) | copy-start | bytes 10616836
  28.7 38.2 %copy-start.11 = (bf16[384,384]{1,0:T(8,128)(2,1)S(1)}, bf16[384,384]{1,0:T(8,128)(2,1)}, u32[]{:S(2)}) copy-start(bf16[384,384]{1,0:T(8,128)(2,1)} %constant.47.clone.high_ref) | copy-start | bytes 884740
  28.7 38.2 %copy-start.12 = (bf16[384,384]{1,0:T(8,128)(2,1)S(1)}, bf16[384,384]{1,0:T(8,128)(2,1)}, u32[]{:S(2)}) copy-start(bf16[384,384]{1,0:T(8,128)(2,1)} %constant.48.clone.low_ref) | copy-start | bytes 884740
  29.8 11.3 %collective-permute-start.6 = (f32[49,8,128]{2,1,0:T(8,128)S(1)}, f32[49,8,128]{2,1,0:T(8,128)S(1)}, u32[]{:S(2)}, u32[]{:S(2)}) collective-permute-start(f32[49,8,128]{2,1,0:T(8,128)S(1)} %get-tuple-element.52), channel_id=1, source_target_pairs={{0,1},{1,2},{2,3},{3,0},{4,5},{5,6},{6,7},{7,4},{8,9},{9,10},{10,1... | collective-permute-start | bytes 602120 | tf_op jit(solution)/shard_map/vertical_send/ppermute | solution.py:278
  31.2 9.9 %collective-permute-start.7 = (f32[49,8,128]{2,1,0:T(8,128)S(1)}, f32[49,8,128]{2,1,0:T(8,128)S(1)}, u32[]{:S(2)}, u32[]{:S(2)}) collective-permute-start(f32[49,8,128]{2,1,0:T(8,128)S(1)} %get-tuple-element.53), channel_id=1, source_target_pairs={{0,2},{1,3},{2,0},{3,1},{4,6},{5,7},{6,4},{7,5},{8,10},{9,11},{10,... | collective-permute-start | bytes 602120 | tf_op jit(solution)/shard_map/vertical_send/ppermute | solution.py:278
  31.2 10.8 %collective-permute-start.8 = (f32[49,8,128]{2,1,0:T(8,128)S(1)}, f32[49,8,128]{2,1,0:T(8,128)S(1)}, u32[]{:S(2)}, u32[]{:S(2)}) collective-permute-start(f32[49,8,128]{2,1,0:T(8,128)S(1)} %get-tuple-element.54), channel_id=1, source_target_pairs={{0,3},{1,0},{2,1},{3,2},{4,7},{5,4},{6,5},{7,6},{8,11},{9,8},{10,9... | collective-permute-start | bytes 602120 | tf_op jit(solution)/shard_map/vertical_send/ppermute | solution.py:278
  33.7 18.1 %collective-permute-start = (f32[61,8,128]{2,1,0:T(8,128)S(1)}, f32[61,8,128]{2,1,0:T(8,128)S(1)}, u32[]{:S(2)}, u32[]{:S(2)}) collective-permute-start(f32[61,8,128]{2,1,0:T(8,128)S(1)} %get-tuple-element.44), channel_id=1, source_target_pairs={{0,4},{1,5},{2,6},{3,7},{4,8},{5,9},{6,10},{7,11},{8,12},{9,13},{1... | collective-permute-start | bytes 749576 | tf_op jit(solution)/shard_map/vertical_send/ppermute | solution.py:278
  33.7 18.1 %collective-permute-start.1 = (f32[61,8,128]{2,1,0:T(8,128)S(1)}, f32[61,8,128]{2,1,0:T(8,128)S(1)}, u32[]{:S(2)}, u32[]{:S(2)}) collective-permute-start(f32[61,8,128]{2,1,0:T(8,128)S(1)} %get-tuple-element.45), channel_id=1, source_target_pairs={{0,8},{1,9},{2,10},{3,11},{4,12},{5,13},{6,14},{7,15},{8,0},{9,1},... | collective-permute-start | bytes 749576 | tf_op jit(solution)/shard_map/vertical_send/ppermute | solution.py:278
  41.1 10.8 %collective-permute-start.2 = (f32[61,8,128]{2,1,0:T(8,128)S(1)}, f32[61,8,128]{2,1,0:T(8,128)S(1)}, u32[]{:S(2)}, u32[]{:S(2)}) collective-permute-start(f32[61,8,128]{2,1,0:T(8,128)S(1)} %get-tuple-element.46), channel_id=1, source_target_pairs={{0,12},{1,13},{2,14},{3,15},{4,0},{5,1},{6,2},{7,3},{8,4},{9,5},{1... | collective-permute-start | bytes 749576 | tf_op jit(solution)/shard_map/vertical_send/ppermute | solution.py:278
  42.0 28.3 %copy-start.9 = (bf16[384,384]{1,0:T(8,128)(2,1)S(1)}, bf16[384,384]{1,0:T(8,128)(2,1)}, u32[]{:S(2)}) copy-start(bf16[384,384]{1,0:T(8,128)(2,1)} %constant.49.clone.high_ref) | copy-start | bytes 884740
  42.0 28.3 %copy-start.10 = (bf16[384,384]{1,0:T(8,128)(2,1)S(1)}, bf16[384,384]{1,0:T(8,128)(2,1)}, u32[]{:S(2)}) copy-start(bf16[384,384]{1,0:T(8,128)(2,1)} %constant.50.clone.low_ref) | copy-start | bytes 884740
  42.0 13.5 %collective-permute-start.10 = (f32[49,8,128]{2,1,0:T(8,128)S(1)}, f32[49,8,128]{2,1,0:T(8,128)S(1)}, u32[]{:S(2)}, u32[]{:S(2)}) collective-permute-start(f32[49,8,128]{2,1,0:T(8,128)S(1)} %get-tuple-element.57), channel_id=1, source_target_pairs={{0,8},{1,9},{2,10},{3,11},{4,12},{5,13},{6,14},{7,15},{8,0},{9,1},... | collective-permute-start | bytes 602120 | tf_op jit(solution)/shard_map/vertical_send/ppermute | solution.py:278
  51.9 14.6 %collective-permute-start.3 = (f32[61,8,128]{2,1,0:T(8,128)S(1)}, f32[61,8,128]{2,1,0:T(8,128)S(1)}, u32[]{:S(2)}, u32[]{:S(2)}) collective-permute-start(f32[61,8,128]{2,1,0:T(8,128)S(1)} %get-tuple-element.48), channel_id=1, source_target_pairs={{0,1},{1,2},{2,3},{3,0},{4,5},{5,6},{6,7},{7,4},{8,9},{9,10},{10,1... | collective-permute-start | bytes 749576 | tf_op jit(solution)/shard_map/vertical_send/ppermute | solution.py:278
  52.0 14.5 %collective-permute-start.4 = (f32[61,8,128]{2,1,0:T(8,128)S(1)}, f32[61,8,128]{2,1,0:T(8,128)S(1)}, u32[]{:S(2)}, u32[]{:S(2)}) collective-permute-start(f32[61,8,128]{2,1,0:T(8,128)S(1)} %get-tuple-element.49), channel_id=1, source_target_pairs={{0,2},{1,3},{2,0},{3,1},{4,6},{5,7},{6,4},{7,5},{8,10},{9,11},{10,... | collective-permute-start | bytes 749576 | tf_op jit(solution)/shard_map/vertical_send/ppermute | solution.py:278
  53.6 13.3 %collective-permute-start.5 = (f32[61,8,128]{2,1,0:T(8,128)S(1)}, f32[61,8,128]{2,1,0:T(8,128)S(1)}, u32[]{:S(2)}, u32[]{:S(2)}) collective-permute-start(f32[61,8,128]{2,1,0:T(8,128)S(1)} %get-tuple-element.50), channel_id=1, source_target_pairs={{0,3},{1,0},{2,1},{3,2},{4,7},{5,4},{6,5},{7,6},{8,11},{9,8},{10,9... | collective-permute-start | bytes 749576 | tf_op jit(solution)/shard_map/vertical_send/ppermute | solution.py:278
  55.6 5.7 %collective-permute-start.11 = (f32[49,8,128]{2,1,0:T(8,128)S(1)}, f32[49,8,128]{2,1,0:T(8,128)S(1)}, u32[]{:S(2)}, u32[]{:S(2)}) collective-permute-start(f32[49,8,128]{2,1,0:T(8,128)S(1)} %get-tuple-element.58), channel_id=1, source_target_pairs={{0,12},{1,13},{2,14},{3,15},{4,0},{5,1},{6,2},{7,3},{8,4},{9,5},{1... | collective-permute-start | bytes 602120 | tf_op jit(solution)/shard_map/vertical_send/ppermute | solution.py:278
  55.6 6.9 %collective-permute-start.9 = (f32[49,8,128]{2,1,0:T(8,128)S(1)}, f32[49,8,128]{2,1,0:T(8,128)S(1)}, u32[]{:S(2)}, u32[]{:S(2)}) collective-permute-start(f32[49,8,128]{2,1,0:T(8,128)S(1)} %get-tuple-element.56), channel_id=1, source_target_pairs={{0,4},{1,5},{2,6},{3,7},{4,8},{5,9},{6,10},{7,11},{8,12},{9,13},{1... | collective-permute-start | bytes 602120 | tf_op jit(solution)/shard_map/vertical_send/ppermute | solution.py:278
  72.2 1.3 copy-start.3
  73.4 50.1 %all-to-all-start.1 = ((f32[16,28,8,128]{3,2,1,0:T(8,128)}), f32[16,28,8,128]{3,2,1,0:T(8,128)S(1)}, u32[]{:S(2)}, u32[]{:S(2)}) async-start(f32[16,28,8,128]{3,2,1,0:T(8,128)} %copy-done.3), calls=%async_computation.1 | async-start | bytes 3670016 | tf_op jit(solution)/shard_map/spanwise_return/all_to_all | solution.py:554
  79.9 23.6 %copy-start.2 = (f32[12,24,1536]{2,1,0:T(8,128)S(1)}, f32[12,24,1536]{2,1,0:T(8,128)}, u32[]{:S(2)}) copy-start(f32[12,24,1536]{2,1,0:T(8,128)} %v_ref.5) | copy-start | bytes 5308420
  79.9 6.8 %collective-permute-start.18 = (f32[48,8,128]{2,1,0:T(8,128)}, f32[48,8,128]{2,1,0:T(8,128)S(1)}, u32[]{:S(2)}, u32[]{:S(2)}) collective-permute-start(f32[48,8,128]{2,1,0:T(8,128)} %get-tuple-element.68), channel_id=1, source_target_pairs={{0,12},{1,13},{2,14},{3,15},{4,0},{5,1},{6,2},{7,3},{8,4},{9,5},{1... | collective-permute-start | bytes 589832 | tf_op jit(solution)/shard_map/vertical_return/ppermute | solution.py:278
  80.0 8.3 %collective-permute-start.19 = (f32[48,8,128]{2,1,0:T(8,128)}, f32[48,8,128]{2,1,0:T(8,128)S(1)}, u32[]{:S(2)}, u32[]{:S(2)}) collective-permute-start(f32[48,8,128]{2,1,0:T(8,128)} %get-tuple-element.69), channel_id=1, source_target_pairs={{0,8},{1,9},{2,10},{3,11},{4,12},{5,13},{6,14},{7,15},{8,0},{9,1},... | collective-permute-start | bytes 589832 | tf_op jit(solution)/shard_map/vertical_return/ppermute | solution.py:278
  80.1 12.8 %collective-permute-start.20 = (f32[48,8,128]{2,1,0:T(8,128)S(1)}, f32[48,8,128]{2,1,0:T(8,128)S(1)}, u32[]{:S(2)}, u32[]{:S(2)}) collective-permute-start(f32[48,8,128]{2,1,0:T(8,128)S(1)} %get-tuple-element.70), channel_id=1, source_target_pairs={{0,4},{1,5},{2,6},{3,7},{4,8},{5,9},{6,10},{7,11},{8,12},{9,13},{1... | collective-permute-start | bytes 589832 | tf_op jit(solution)/shard_map/vertical_return/ppermute | solution.py:278
  81.5 13.8 %collective-permute-start.12 = (f32[60,8,128]{2,1,0:T(8,128)}, f32[60,8,128]{2,1,0:T(8,128)S(1)}, u32[]{:S(2)}, u32[]{:S(2)}) collective-permute-start(f32[60,8,128]{2,1,0:T(8,128)} %get-tuple-element.60), channel_id=1, source_target_pairs={{0,3},{1,0},{2,1},{3,2},{4,7},{5,4},{6,5},{7,6},{8,11},{9,8},{10,9... | collective-permute-start | bytes 737288 | tf_op jit(solution)/shard_map/vertical_return/ppermute | solution.py:278
  83.5 12.2 %collective-permute-start.13 = (f32[60,8,128]{2,1,0:T(8,128)S(1)}, f32[60,8,128]{2,1,0:T(8,128)S(1)}, u32[]{:S(2)}, u32[]{:S(2)}) collective-permute-start(f32[60,8,128]{2,1,0:T(8,128)S(1)} %get-tuple-element.61), channel_id=1, source_target_pairs={{0,2},{1,3},{2,0},{3,1},{4,6},{5,7},{6,4},{7,5},{8,10},{9,11},{10,... | collective-permute-start | bytes 737288 | tf_op jit(solution)/shard_map/vertical_return/ppermute | solution.py:278
  86.6 11.2 %collective-permute-start.14 = (f32[60,8,128]{2,1,0:T(8,128)S(1)}, f32[60,8,128]{2,1,0:T(8,128)S(1)}, u32[]{:S(2)}, u32[]{:S(2)}) collective-permute-start(f32[60,8,128]{2,1,0:T(8,128)S(1)} %get-tuple-element.62), channel_id=1, source_target_pairs={{0,1},{1,2},{2,3},{3,0},{4,5},{5,6},{6,7},{7,4},{8,9},{9,10},{10,1... | collective-permute-start | bytes 737288 | tf_op jit(solution)/shard_map/vertical_return/ppermute | solution.py:278
  92.9 9.8 %collective-permute-start.21 = (f32[48,8,128]{2,1,0:T(8,128)S(1)}, f32[48,8,128]{2,1,0:T(8,128)S(1)}, u32[]{:S(2)}, u32[]{:S(2)}) collective-permute-start(f32[48,8,128]{2,1,0:T(8,128)S(1)} %get-tuple-element.72), channel_id=1, source_target_pairs={{0,3},{1,0},{2,1},{3,2},{4,7},{5,4},{6,5},{7,6},{8,11},{9,8},{10,9... | collective-permute-start | bytes 589832 | tf_op jit(solution)/shard_map/vertical_return/ppermute | solution.py:278
  95.1 17.7 %collective-permute-start.22 = (f32[48,8,128]{2,1,0:T(8,128)S(1)}, f32[48,8,128]{2,1,0:T(8,128)S(1)}, u32[]{:S(2)}, u32[]{:S(2)}) collective-permute-start(f32[48,8,128]{2,1,0:T(8,128)S(1)} %get-tuple-element.73), channel_id=1, source_target_pairs={{0,2},{1,3},{2,0},{3,1},{4,6},{5,7},{6,4},{7,5},{8,10},{9,11},{10,... | collective-permute-start | bytes 589832 | tf_op jit(solution)/shard_map/vertical_return/ppermute | solution.py:278
  95.2 17.5 %collective-permute-start.23 = (f32[48,8,128]{2,1,0:T(8,128)S(1)}, f32[48,8,128]{2,1,0:T(8,128)S(1)}, u32[]{:S(2)}, u32[]{:S(2)}) collective-permute-start(f32[48,8,128]{2,1,0:T(8,128)S(1)} %get-tuple-element.74), channel_id=1, source_target_pairs={{0,1},{1,2},{2,3},{3,0},{4,5},{5,6},{6,7},{7,4},{8,9},{9,10},{10,1... | collective-permute-start | bytes 589832 | tf_op jit(solution)/shard_map/vertical_return/ppermute | solution.py:278
  97.9 14.9 %collective-permute-start.15 = (f32[60,8,128]{2,1,0:T(8,128)S(1)}, f32[60,8,128]{2,1,0:T(8,128)S(1)}, u32[]{:S(2)}, u32[]{:S(2)}) collective-permute-start(f32[60,8,128]{2,1,0:T(8,128)S(1)} %get-tuple-element.64), channel_id=1, source_target_pairs={{0,12},{1,13},{2,14},{3,15},{4,0},{5,1},{6,2},{7,3},{8,4},{9,5},{1... | collective-permute-start | bytes 737288 | tf_op jit(solution)/shard_map/vertical_return/ppermute | solution.py:278
  101.5 11.2 %collective-permute-start.16 = (f32[60,8,128]{2,1,0:T(8,128)S(1)}, f32[60,8,128]{2,1,0:T(8,128)S(1)}, u32[]{:S(2)}, u32[]{:S(2)}) collective-permute-start(f32[60,8,128]{2,1,0:T(8,128)S(1)} %get-tuple-element.65), channel_id=1, source_target_pairs={{0,8},{1,9},{2,10},{3,11},{4,12},{5,13},{6,14},{7,15},{8,0},{9,1},... | collective-permute-start | bytes 737288 | tf_op jit(solution)/shard_map/vertical_return/ppermute | solution.py:278
  102.7 13.5 %collective-permute-start.17 = (f32[60,8,128]{2,1,0:T(8,128)S(1)}, f32[60,8,128]{2,1,0:T(8,128)S(1)}, u32[]{:S(2)}, u32[]{:S(2)}) collective-permute-start(f32[60,8,128]{2,1,0:T(8,128)S(1)} %get-tuple-element.66), channel_id=1, source_target_pairs={{0,4},{1,5},{2,6},{3,7},{4,8},{5,9},{6,10},{7,11},{8,12},{9,13},{1... | collective-permute-start | bytes 737288 | tf_op jit(solution)/shard_map/vertical_return/ppermute | solution.py:278
  103.5 3.7 %copy-start.16 = (bf16[3,8,768,256]{3,2,1,0:T(8,128)(2,1)S(1)}, bf16[3,8,768,256]{3,2,1,0:T(8,128)(2,1)}, u32[]{:S(2)}) copy-start(bf16[3,8,768,256]{3,2,1,0:T(8,128)(2,1)} %constant.46.clone.table_ref) | copy-start | bytes 28311556
  107.2 5.5 %copy-start.19 = (f32[100]{0:T(128)S(1)}, f32[100]{0:T(128)}, u32[]{:S(2)}) copy-start(f32[100]{0:T(128)} %param.12) | copy-start | bytes 1204
  117.5 1.2 copy-start.5
  123.5 1.5 %copy-start.6 = (f32[288,1536]{1,0:T(8,128)S(1)}, f32[288,1536]{1,0:T(8,128)}, u32[]{:S(2)}) copy-start(f32[288,1536]{1,0:T(8,128)} %copy-done.5) | copy-start | bytes 5308420
  125.0 2.0 %copy-start.8 = (f32[2,12,24,1536]{3,2,1,0:T(8,128)S(1)}, f32[2,12,24,1536]{3,2,1,0:T(8,128)}, u32[]{:S(2)}) copy-start(f32[2,12,24,1536]{3,2,1,0:T(8,128)} %copy-done.7) | copy-start | bytes 10616836

commit v2 on v1

v2 whole, which is shorter than its diff:
```python
import functools
import math

import jax
import jax.numpy as jnp
import ml_dtypes
import numpy as np
from jax import lax
from jax.experimental import pallas as pl
from jax.experimental.pallas import tpu as pltpu
from jax.sharding import PartitionSpec as P

NX, NY, NZ, BX = 1536, 384, 192, 128
TURB = 100
N = 16
DZ, DY, XB = NZ // N, NY // N, NX // BX
HALF = NX // 2
VISCOSITY = 0.2
CROSS_WIND = 0.4
DISK_DEPTH = 1.5
RADIUS = 0.6 * DZ
F32, BF16 = jnp.float32, jnp.bfloat16
VM = pl.BlockSpec(memory_space=pltpu.VMEM)
SM = pl.BlockSpec(memory_space=pltpu.SMEM)
HB = pl.BlockSpec(memory_space=pltpu.HBM)
ROUTES = (("x", "y", (0, 1, 2, 3, 4)), ("y", "x", (5, 6, 7, 8)))


WHOLE = 57


class Mover:
    def __init__(self, sems):
        self.sems, self.used = sems, 0

    def start(self, source, target):
        copy = pltpu.make_async_copy(source, target, self.sems.at[self.used])
        self.used += 1
        copy.start()
        return copy


def wait(copies):
    for copy in copies:
        copy.wait()


def params(mib=8):
    return pltpu.CompilerParams(vmem_limit_bytes=mib * 1024 * 1024)


def kernels_of(length):
    m = np.arange(length)
    m = np.where(m > length // 2, m - length, m).astype(np.float64)
    parity = np.where(m % 2 == 0, 1.0, -1.0)
    angle = math.pi / length * m
    sine = np.where(m == 0, 1.0, np.sin(angle))
    first = np.where(m == 0, 0.0, math.pi / length * parity * np.cos(angle) / sine)
    second = np.where(
        m == 0,
        -math.pi**2 / 3.0 - 2.0 * math.pi**2 / (3.0 * length * length),
        -(2.0 * math.pi**2 / (length * length)) * parity / (sine * sine),
    )
    return first, second


def split(table):
    high = table.astype(np.float32).astype(ml_dtypes.bfloat16)
    low = (table - high.astype(np.float64)).astype(np.float32).astype(ml_dtypes.bfloat16)
    return high, low


def x_tables():
    first, second = kernels_of(NX)
    source, target = np.arange(HALF)[:, None], np.arange(256)[None, :]
    near, far = (target - source) % NX, (target - source + HALF) % NX
    mats = []
    for sign in (1.0, -1.0):
        for table in (VISCOSITY * second, first):
            mats.extend(split(0.5 * (table[near] + sign * table[far])))
    return np.stack(mats)


def y_matrix():
    first, second = kernels_of(NY)
    i = np.arange(NY)
    return split((VISCOSITY * second - CROSS_WIND * first)[(i[:, None] - i[None, :]) % NY])


def z_matrix():
    _, second = kernels_of(NZ)
    row = np.arange(N * 2 * DZ)
    block, inner = row // (2 * DZ), row % (2 * DZ)
    half, height = inner // DZ, block * DZ + inner % DZ
    table = VISCOSITY * second[(height[:, None] - height[None, :]) % NZ]
    return split(np.where(half[:, None] == half[None, :], table, 0.0))


def halves(value):
    high = value.astype(BF16)
    return high, (value - high.astype(F32)).astype(BF16)


def dot(a, b):
    return jnp.dot(a, b, preferred_element_type=F32)


def x_kernel(wind_ref, offset_ref, v_ref, table_ref, out_ref, denom_ref, lhs_ref, hold_ref):
    rows = DZ * DY
    for part in range(2):
        for block in range(3):
            low_x = v_ref[:, :, block * 256 : block * 256 + 256].reshape(rows, 256)
            high_x = v_ref[:, :, HALF + block * 256 : HALF + block * 256 + 256].reshape(rows, 256)
            value = low_x + high_x if part == 0 else low_x - high_x
            for at, number in ((block, value), (block + 3, value if part == 0 else -value)):
                if at < 5:
                    high, low = halves(number)
                    lhs_ref[part, :rows, at * 256 : at * 256 + 256] = high
                    lhs_ref[part, rows:, at * 256 : at * 256 + 256] = low

    for step in range(3):
        terms = []
        for part in range(2):
            lhs = lhs_ref[part, :, step * 256 : step * 256 + HALF]
            got = []
            for which in range(2):
                both = dot(lhs, table_ref[4 * part + 2 * which])
                extra = dot(lhs[:rows], table_ref[4 * part + 2 * which + 1])
                got.append((both[:rows] + both[rows:] + extra).reshape(DZ, DY, 256))
            terms.append(got)
        here = slice(step * 256, step * 256 + 256)
        there = slice(HALF + step * 256, HALF + step * 256 + 256)
        for z in range(DZ):
            even = terms[0][0][z] - wind_ref[z] * terms[0][1][z]
            odd = terms[1][0][z] - wind_ref[z] * terms[1][1][z]
            out_ref[z, :, here] = even + odd
            out_ref[z, :, there] = even - odd

    hold_ref[...] = jnp.zeros((8, BX), F32)
    hold_ref[0:3, 0:TURB] = offset_ref[...].astype(F32)
    centre_z, centre_y, centre_x = (hold_ref[i : i + 1, :] for i in range(3))
    sub = lax.broadcasted_iota(jnp.int32, (8, BX), 0).astype(F32)

    def add_radial(z, total):
        for yt in range(6):
            total = total + radial(z.astype(F32) - centre_z, sub + (8.0 * yt) - centre_y)
        return total

    area = jnp.sum(lax.fori_loop(0, 2 * DZ, add_radial, jnp.zeros((8, BX), F32)), axis=0, keepdims=True)
    depth = jnp.zeros((8, BX), F32)
    for xt in range(BX // 8):
        depth = depth + axial(sub + (8.0 * xt) - centre_x)
    denom_ref[...] = jnp.broadcast_to(area * jnp.sum(depth, axis=0, keepdims=True), (8, BX))


def along_x(velocity, wind, offset):
    return pl.pallas_call(
        x_kernel,
        in_specs=[SM, VM, VM, VM],
        out_specs=[VM, VM],
        out_shape=[jax.ShapeDtypeStruct((DZ, DY, NX), F32), jax.ShapeDtypeStruct((8, BX), F32)],
        scratch_shapes=[pltpu.VMEM((2, 2 * DZ * DY, 1280), BF16), pltpu.VMEM((8, BX), F32)],
        compiler_params=params(24),
        cost_estimate=pl.CostEstimate(
            flops=2 * 288 * 768 * 768 * 12, bytes_accessed=7 * 2**20, transcendentals=0
        ),
        name="x_derivative",
    )(wind, offset.T, velocity, jnp.asarray(x_tables()))


def y_pack_kernel(v_ref, out_ref, from_ref, to_ref, in_sem, out_sem):
    into = [
        pltpu.make_async_copy(v_ref.at[pl.ds(z, 1)], from_ref.at[pl.ds(z, 1)], in_sem.at[z])
        for z in range(DZ)
    ]
    away = [
        pltpu.make_async_copy(to_ref.at[pl.ds(d, 1)], out_ref.at[pl.ds(d, 1)], out_sem.at[d])
        for d in range(N)
    ]
    for copy in into:
        copy.start()
    for pair in range(DZ * XB):
        z, xb, d, j = pair // XB, pair % XB, pair // 9, pair % 9
        if xb == 0:
            into[z].wait()
        for yt in range(3):
            to_ref[d, yt * 9 + j] = from_ref[z, yt * 8 : yt * 8 + 8, xb * BX : xb * BX + BX]
        if j == 8:
            away[d].start()
    wait(away)


def y_pack(velocity):
    return pl.pallas_call(
        y_pack_kernel,
        in_specs=[HB],
        out_specs=HB,
        out_shape=jax.ShapeDtypeStruct((N, 27, 8, BX), F32),
        scratch_shapes=[
            pltpu.VMEM((DZ, DY, NX), F32),
            pltpu.VMEM((N, 27, 8, BX), F32),
            pltpu.SemaphoreType.DMA((DZ,)),
            pltpu.SemaphoreType.DMA((N,)),
        ],
        compiler_params=params(WHOLE),
        name="y_pack",
    )(velocity)


def sums_kernel(*refs):
    sources, (out_ref, sums_ref, sems) = refs[:8], refs[9:]
    move = Mover(sems)
    last = 4 * tiles_of(ROUTES[0])
    wait([move.start(sources[i].at[last], sums_ref.at[i]) for i in range(4)])
    out_ref[...] = (sums_ref[0] + sums_ref[1]) + (sums_ref[2] + sums_ref[3])


def level_sums(arrived, term_x):
    return pl.pallas_call(
        sums_kernel,
        in_specs=[HB] * 9,
        out_specs=VM,
        out_shape=jax.ShapeDtypeStruct((8, BX), F32),
        scratch_shapes=[pltpu.VMEM((4, 8, BX), F32), pltpu.SemaphoreType.DMA((4,))],
        compiler_params=params(WHOLE),
        name="level_sums",
    )(*arrived, term_x)


def y_kernel(matrix_ref, sums_ref, in_ref, after_ref, out_ref):
    for group in range(3):
        tiles = []
        for j in range(3 * group, 3 * group + 3):
            tiles.append(jnp.stack([in_ref[:, yt * 9 + j] for yt in range(3)], axis=1).reshape(NY, BX))
        high, low = halves(jnp.concatenate(tiles, axis=1))
        got = dot(matrix_ref[0], high) + dot(matrix_ref[1], high) + dot(matrix_ref[0], low)
        for k in range(3):
            value = got[:, k * BX : k * BX + BX].reshape(N, 3, 8, BX)
            for yt in range(3):
                out_ref[:, yt * 9 + 3 * group + k] = value[:, yt]
    for d in range(N):
        out_ref[d, 27] = sums_ref[...]


def y_lines(sums, received, after):
    return pl.pallas_call(
        y_kernel,
        in_specs=[VM] * 3 + [HB],
        out_specs=VM,
        out_shape=jax.ShapeDtypeStruct((N, 28, 8, BX), F32),
        compiler_params=params(16),
        name="y_lines",
    )(jnp.asarray(np.stack(y_matrix())), sums, received, after)


def device_at(route, place_first, place_second):
    return place_first * 4 + place_second if route[0] == "x" else place_second * 4 + place_first


def places(route, where_ref):
    x, y = where_ref[1], where_ref[2]
    return (x, y) if route[0] == "x" else (y, x)


def tiles_of(route):
    return 3 * len(route[2])


def columns_of(device, j, h):
    y = (device // 2) * 3 + j // 3
    xb = ((device % 2) * 2 + h) * 3 + j % 3
    return y, xb


def z_pack_kernel(r, where_ref, in_ref, *refs):
    sums_ref, (*out_refs, v_ref) = refs[0], refs[-5:]
    for xb in range(XB):
        v_ref[xb] = in_ref[:, xb * BX : xb * BX + BX]
    route = ROUTES[r]
    first, second = places(route, where_ref)
    width = len(route[2])
    for k1 in range(4):
        out = out_refs[k1]
        if r == 0:
            out[4 * 3 * width] = sums_ref[...]
        for k2 in range(4):
            device = device_at(route, (first + k1) % 4, (second + k2) % 4)
            for n, j in enumerate(route[2]):
                y, low_cols = columns_of(device, j, 0)
                y, high_cols = columns_of(device, j, 1)
                base = k2 * 3 * width + n
                out[base] = v_ref[low_cols, pl.ds(y, 8, stride=DY), :]
                out[base + width, 0:4] = v_ref[low_cols, pl.ds(y + 8 * DY, 4, stride=DY), :]
                out[base + width, 4:8] = v_ref[high_cols, pl.ds(y, 4, stride=DY), :]
                out[base + 2 * width] = v_ref[high_cols, pl.ds(y + 4 * DY, 8, stride=DY), :]


def z_pack(r, where, velocity, sums):
    shape = jax.ShapeDtypeStruct((4 * tiles_of(ROUTES[r]) + (r == 0), 8, BX), F32)
    return pl.pallas_call(
        functools.partial(z_pack_kernel, r),
        in_specs=[SM, VM] + [VM] * (r == 0),
        out_specs=[VM] * 4,
        out_shape=[shape] * 4,
        scratch_shapes=[pltpu.VMEM((XB, DZ * DY, BX), F32)],
        compiler_params=params(),
        name="z_pack",
    )(where, velocity.reshape(DZ * DY, NX), *([sums] if r == 0 else []))


def regroup(arrays, tiles, with_sums):
    def kernel(*refs):
        for i in range(4):
            for k in range(4):
                refs[4 + i][k * tiles : (k + 1) * tiles] = refs[k][i * tiles : (i + 1) * tiles]
            if with_sums:
                last = 4 * tiles
                refs[4 + i][last] = (refs[0][last] + refs[1][last]) + (refs[2][last] + refs[3][last])

    shape = jax.ShapeDtypeStruct((4 * tiles + (1 if with_sums else 0), 8, BX), F32)
    return pl.pallas_call(
        kernel,
        in_specs=[VM] * 4,
        out_specs=[VM] * 4,
        out_shape=[shape] * 4,
        compiler_params=params(),
        name="regroup",
    )(*arrays)


def shift(value, axis, by):
    moves = []
    for i in range(N):
        x, y = i // 4, i % 4
        moves.append((i, ((x + by) % 4) * 4 + y if axis == "x" else x * 4 + (y + by) % 4))
    return lax.ppermute(value, "pz", moves)


def send_stage(arrays, axis, sign):
    return [arrays[0]] + [shift(arrays[k], axis, sign * k) for k in range(1, 4)]


def z_kernel(r, where_ref, matrix_hbm, *refs):
    ins_hbm, outs_hbm, refs = refs[:4], refs[5:9], refs[9:]
    ins, outs, (matrix_ref, lines_ref, sems) = refs[:4], refs[4:8], refs[8:]
    route = ROUTES[r]
    first, second = places(route, where_ref)
    tiles, width = tiles_of(route), len(route[2])
    move = Mover(sems)
    fetch = [move.start(ins_hbm[i], ins[i]) for i in range(4)]
    fetch_matrix = move.start(matrix_hbm, matrix_ref)
    away = []

    def spots(k2):
        for k1 in range(4):
            device = device_at(route, (first - k1) % 4, (second - k2) % 4)
            yield device, slice(k1 * tiles, (k1 + 1) * tiles)

    for k2 in range(4):
        fetch[k2].wait()
        for device, outer in spots(k2):
            lines_ref[device] = ins[k2][outer]
    columns = []
    for j in range(width):
        columns.append(jnp.stack([lines_ref[:, rt * width + j] for rt in range(3)], axis=1).reshape(N * 24, BX))
    high, low = halves(jnp.concatenate(columns, axis=1))
    fetch_matrix.wait()
    got = dot(matrix_ref[0], high) + dot(matrix_ref[1], high) + dot(matrix_ref[0], low)
    for j in range(width):
        value = got[:, j * BX : j * BX + BX].reshape(N, 3, 8, BX)
        for rt in range(3):
            lines_ref[:, rt * width + j] = value[:, rt]
    for k2 in range(4):
        for device, outer in spots(k2):
            outs[k2][outer] = lines_ref[device]
        away.append(move.start(outs[k2], outs_hbm[k2]))
    wait(away)


def z_lines(r, where, after, arrays):
    tiles = tiles_of(ROUTES[r])
    shapes = [jax.ShapeDtypeStruct((4 * tiles, 8, BX), F32)] * 4
    return pl.pallas_call(
        functools.partial(z_kernel, r),
        in_specs=[SM] + [HB] * 6,
        out_specs=[HB] * 4,
        out_shape=shapes,
        scratch_shapes=[pltpu.VMEM(a.shape, F32) for a in arrays]
        + [pltpu.VMEM(a.shape, F32) for a in shapes]
        + [
            pltpu.VMEM((2, N * 24, N * 24), BF16),
            pltpu.VMEM((N, tiles, 8, BX), F32),
            pltpu.SemaphoreType.DMA((9,)),
        ],
        compiler_params=params(WHOLE),
        name="z_lines",
    )(where, jnp.asarray(np.stack(z_matrix())), *arrays, after)


def z_unpack_kernel(where_ref, term_ref, *refs):
    out_ref, sum_ref = refs[8:]
    for r, route in enumerate(ROUTES):
        first, second = places(route, where_ref)
        width = len(route[2])
        for k1 in range(4):
            got = refs[r * 4 + k1]
            for k2 in range(4):
                device = device_at(route, (first + k1) % 4, (second + k2) % 4)
                for n, j in enumerate(route[2]):
                    y, low_cols = columns_of(device, j, 0)
                    y, high_cols = columns_of(device, j, 1)
                    base = k2 * 3 * width + n
                    for at, count, cols, tile, row in (
                        (0, 8, low_cols, base, 0),
                        (8, 4, low_cols, base + width, 0),
                        (0, 4, high_cols, base + width, 4),
                        (4, 8, high_cols, base + 2 * width, 0),
                    ):
                        spot = pl.ds(y + at * DY, count, stride=DY)
                        sum_ref[cols, spot, :] = got[tile, row : row + count]

    for xb in range(XB):
        cols = slice(xb * BX, xb * BX + BX)
        out_ref[:, cols] = term_ref[:, cols] + sum_ref[xb]


def z_unpack(where, term, arrays):
    return pl.pallas_call(
        z_unpack_kernel,
        in_specs=[SM] + [VM] * 9,
        out_specs=VM,
        out_shape=jax.ShapeDtypeStruct((DZ * DY, NX), F32),
        scratch_shapes=[pltpu.VMEM((XB, DZ * DY, BX), F32)],
        compiler_params=params(),
        name="z_unpack",
    )(where, term.reshape(DZ * DY, NX), *arrays).reshape(DZ, DY, NX)


def sigmoid(value):
    return 1.0 / (1.0 + jnp.exp(-value))


def axial(rel):
    return jnp.exp(-0.5 * (rel / DISK_DEPTH) ** 2)


def radial(rel_z, rel_y):
    return sigmoid((RADIUS * RADIUS - rel_y * rel_y - rel_z * rel_z) / (2.0 * RADIUS))


def disk_kernel(where_ref, wind_ref, brick_ref, offset_ref, v_ref, sums_ref, high_ref, low_ref, radial_ref, hold_ref, ahead_ref, behind_ref):
    level, column = where_ref[0], where_ref[3]
    sums_ref[...] = jnp.zeros((8, BX), F32)

    @pl.when(level < 2)
    def _():
        hold_ref[...] = jnp.zeros((8, BX), F32)
        hold_ref[0:1, 0:TURB] = brick_ref[0:1, :].astype(F32)
        hold_ref[1:4, 0:TURB] = offset_ref[...].astype(F32)
        brick, centre_z, centre_y, centre_x = (hold_ref[i : i + 1, :] for i in range(4))
        line = jnp.floor((brick + 0.5) * (1.0 / XB))
        block = brick - XB * line
        left = line - N * jnp.floor((line + 0.5) * (1.0 / N))
        shifted = column.astype(F32) - left
        lane = lax.broadcasted_iota(jnp.int32, (1, BX), 1)
        here = ((shifted == 0.0) | (shifted == 1.0)) & (lane < TURB)
        block = jnp.where(here, block, -1.0)
        sub = lax.broadcasted_iota(jnp.int32, (8, BX), 0).astype(F32)
        along = lax.broadcasted_iota(jnp.int32, (BX, BX), 0).astype(F32)
        shape_x = axial(along - centre_x)
        depth = jnp.sum(shape_x, axis=0, keepdims=True)
        for xb in range(XB):
            weight = jnp.where(block == float(xb), shape_x, 0.0)
            high, low = halves(weight)
            ahead_ref[xb * BX : xb * BX + BX] = high
            behind_ref[xb * BX : xb * BX + BX] = low
            high, low = halves(weight.T)
            high_ref[:, xb * BX : xb * BX + BX] = high
            low_ref[:, xb * BX : xb * BX + BX] = low
        high, low = halves(v_ref[...].reshape(DZ * DY, NX))
        along_disk = dot(high, ahead_ref[...]) + dot(low, ahead_ref[...]) + dot(high, behind_ref[...])
        base_z = (level * DZ).astype(F32) - centre_z
        base_y = shifted * float(DY) - centre_y
        total = jnp.zeros((8, BX), F32)
        for z in range(DZ):
            for yt in range(3):
                rows = slice(z * DY + yt * 8, z * DY + yt * 8 + 8)
                weight = jnp.where(here, radial(base_z + float(z), sub + (base_y + 8.0 * yt)), 0.0)
                radial_ref[rows] = weight
                total = total + weight * (along_disk[rows] + wind_ref[z] * depth)
        sums_ref[0:1] = jnp.sum(total, axis=0, keepdims=True)


def disks(where, wind, bricks, offset, velocity):
    return pl.pallas_call(
        disk_kernel,
        in_specs=[SM, SM, VM, VM, VM],
        out_specs=[VM] * 4,
        out_shape=[
            jax.ShapeDtypeStruct((8, BX), F32),
            jax.ShapeDtypeStruct((BX, NX), BF16),
            jax.ShapeDtypeStruct((BX, NX), BF16),
            jax.ShapeDtypeStruct((DZ * DY, BX), F32),
        ],
        scratch_shapes=[
            pltpu.VMEM((8, BX), F32),
            pltpu.VMEM((NX, BX), BF16),
            pltpu.VMEM((NX, BX), BF16),
        ],
        compiler_params=params(16),
        name="disks",
    )(where, wind, bricks.T, offset.T, velocity)


def final_kernel(where_ref, coef_ref, denom_ref, high_ref, low_ref, radial_ref, terms_ref, lines_ref, out_ref, speed_ref, held_ref, push_ref, sem):
    level = where_ref[0]
    total = lines_ref[0, 27]
    for d in range(1, N):
        total = total + lines_ref[d, 27]
    speed = total[0:1, :] / denom_ref[0:1, :]
    speed_ref[...] = speed[:, :TURB]

    def emit(force):
        copies = []
        for part in range(4):
            for local in range(36 * part, 36 * part + 36):
                z, xb = local // XB, local % XB
                cols = slice(xb * BX, xb * BX + BX)
                for yt in range(3):
                    rows = slice(yt * 8, yt * 8 + 8)
                    value = terms_ref[z, rows, cols] + lines_ref[local // 9, yt * 9 + local % 9]
                    if force is not None:
                        value = value + force[z * DY + yt * 8 : z * DY + yt * 8 + 8, cols]
                    held_ref[z, rows, cols] = value
            span = pl.ds(3 * part, 3)
            copies.append(pltpu.make_async_copy(held_ref.at[span], out_ref.at[span], sem.at[part]))
            copies[-1].start()
        for copy in copies:
            copy.wait()

    @pl.when(level < 2)
    def _():
        push_ref[...] = jnp.zeros((8, BX), F32)
        push_ref[0:1, :TURB] = -0.5 * coef_ref[...] * speed[:, :TURB] * jnp.abs(speed[:, :TURB])
        high, low = halves(radial_ref[...] * push_ref[0:1, :])
        emit(dot(high, high_ref[...]) + dot(low, high_ref[...]) + dot(high, low_ref[...]))

    @pl.when(level >= 2)
    def _():
        emit(None)


def finish(where, coef, denom, basis, terms, lines):
    tendency, speed = pl.pallas_call(
        final_kernel,
        in_specs=[SM] + [VM] * 7,
        out_specs=[HB, VM],
        out_shape=[jax.ShapeDtypeStruct((DZ, DY, NX), F32), jax.ShapeDtypeStruct((1, TURB), F32)],
        scratch_shapes=[
            pltpu.VMEM((DZ, DY, NX), F32),
            pltpu.VMEM((8, BX), F32),
            pltpu.SemaphoreType.DMA((4,)),
        ],
        compiler_params=params(16),
        name="finish",
    )(where, coef, denom, *basis, terms, lines)
    return tendency, speed.reshape(TURB)


def body(velocity, wind, thrust_coef, bricks, offset):
    pz, py = lax.axis_index("pz"), lax.axis_index("py")
    packed = y_pack(velocity)
    packed, pz, py = lax.optimization_barrier((packed, pz, py))
    where = jnp.stack([pz, pz // 4, pz % 4, py]).astype(jnp.int32)
    with jax.named_scope("spanwise_send"):
        received = lax.all_to_all(packed, "py", 0, 0, tiled=True)
    sums, *basis = disks(where, wind, bricks, offset, velocity)
    with jax.named_scope("vertical_send"):
        arrived = []
        for r, route in enumerate(ROUTES):
            stage = send_stage(z_pack(r, where, velocity, sums), route[0], 1)
            stage = regroup(stage, tiles_of(route), r == 0)
            arrived += send_stage(stage, route[1], 1)
    term_x, denom = along_x(velocity, wind, offset)
    turned = z_lines(1, where, term_x, arrived[4:])
    spanwise = y_lines(level_sums(arrived, term_x), received, turned[0])
    vertical = z_lines(0, where, spanwise, arrived[:4]) + turned
    with jax.named_scope("spanwise_return"):
        returned = lax.all_to_all(spanwise, "py", 0, 0, tiled=True)
    with jax.named_scope("vertical_return"):
        back = []
        for r, route in enumerate(ROUTES):
            stage = send_stage(vertical[4 * r : 4 * r + 4], route[1], -1)
            stage = regroup(stage, tiles_of(route), False)
            back += send_stage(stage, route[0], -1)
    terms = z_unpack(where, term_x, back)
    return finish(where, thrust_coef.reshape(1, TURB), denom, basis, terms, returned)


def solution(mesh):
    return jax.shard_map(
        body,
        mesh=mesh,
        in_specs=(P("pz", "py", None), P("pz"), P(), P(), P()),
        out_specs=(P("pz", "py", None), P()),
        check_vma=False,
    )
```

time: 131 us -> 119 us (0.908)
  waiting for transfers between devices: 47.1 us -> 34.3 us
  local copies, waits for them, and re-layouts: 17.7 us -> 8.53 us
  starting transfers between devices: 38.2 us -> 45.8 us
  Pallas kernels: 26.3 us -> 28.7 us
    unnamed x42 -> x68, local copies, waits for them, and re-layouts: 17.1 us -> 8.53 us
    ppermute x24, waiting for transfers between devices: 42.2 us -> 34.2 us  [shift(): return lax.ppermute(value, 'pz', moves)]
    ppermute x24, starting transfers between devices: 21.6 us -> 26.8 us  [shift(): return lax.ppermute(value, 'pz', moves)]
    all_to_all x1, waiting for transfers between devices: 4.85 us -> 0.01 us  [body(): returned = lax.all_to_all(spanwise, 'py', 0, 0, tiled=True)]
    pallas_call x7 -> x10, Pallas kernels: 24.8 us -> 27.2 us  [the longest x2 8.26 us: z_lines(): pl.pallas_call(functools.partial(z_kernel, r), in_specs=[SM] + [HB] * 6,...]
    all_to_all x1, starting transfers between devices: 6.47 us -> 8.91 us  [body(): returned = lax.all_to_all(spanwise, 'py', 0, 0, tiled=True)]
  transfers between devices with their start and end apart: 26 -> 26, of which waited for: 13 -> 11; matrix products, arithmetic and copies ran while one was open for 1% -> 0% of each run, Pallas kernels for 17% -> 17%
where the time goes in v2:
time: 119 us
  starting transfers between devices  45.8 us (38%)
  waiting for transfers between devices  34.3 us (29%)
  Pallas kernels  28.7 us (24%)
  local copies, waits for them, and re-layouts  8.53 us (7%)
  between operations  1.22 us (1%)
    ppermute x24, waiting for transfers between devices, shift(): return lax.ppermute(value, 'pz', moves)  34.2 us
    ppermute x24, starting transfers between devices, shift(): return lax.ppermute(value, 'pz', moves)  26.8 us
    all_to_all x1, starting transfers between devices, body(): received = lax.all_to_all(packed, 'py', 0, 0, tiled=True)  10.1 us
    all_to_all x1, starting transfers between devices, body(): returned = lax.all_to_all(spanwise, 'py', 0, 0, tiled=True)  8.91 us
    unnamed x68, local copies, waits for them, and re-layouts  8.53 us
    pallas_call x2, Pallas kernels, z_lines(): pl.pallas_call(functools.partial(z_kernel, r), in_specs=[SM] + [HB] * 6,...  8.26 us
    pallas_call x1, Pallas kernels, along_x(): pl.pallas_call(x_kernel, in_specs=[SM, VM, VM, VM], out_specs=[VM, VM], o...  5.66 us
    pallas_call x1, Pallas kernels, finish(): pl.pallas_call(final_kernel, in_specs=[SM] + [VM] * 7, out_specs=[HB, VM]...  3.18 us
  transfers between devices with their start and end apart: 26, of which 11 were waited for; matrix products, arithmetic and copies ran while one was open for 0% of the time, Pallas kernels for 17%

profile of v2, /device:TPU:1, one launch (start us, length us, event | category | flops | bytes accessed | tf_op | source)
XLA Modules:
  0.0 118.7 jit_solution(3264679586434890493)
XLA Ops:
  0.6 2.5 %y_pack.1 = f32[16,27,8,128]{3,2,1,0:T(8,128)} custom-call(f32[12,24,1536]{2,1,0:T(8,128)} %v_ref.5), custom_call_target="tpu_custom_call" | custom-call | tf_op jit(solution)/shard_map/y_pack/pallas_call | solution.py:194
  3.2 10.1 %all-to-all-start = ((f32[16,27,8,128]{3,2,1,0:T(8,128)}), f32[16,27,8,128]{3,2,1,0:T(8,128)S(1)}, u32[]{:S(2)}, u32[]{:S(2)}) async-start(f32[16,27,8,128]{3,2,1,0:T(8,128)} %y_pack.1), calls=%async_computation | async-start | bytes 3538944 | tf_op jit(solution)/shard_map/spanwise_send/all_to_all | solution.py:576
  13.4 0.8 z_pack.3
  14.3 1.4 %collective-permute-start.6 = (f32[48,8,128]{2,1,0:T(8,128)S(1)}, f32[48,8,128]{2,1,0:T(8,128)S(1)}, u32[]{:S(2)}, u32[]{:S(2)}) collective-permute-start(f32[48,8,128]{2,1,0:T(8,128)S(1)} %get-tuple-element.62), channel_id=1, source_target_pairs={{0,1},{1,2},{2,3},{3,0},{4,5},{5,6},{6,7},{7,4},{8,9},{9,10},{10,1... | collective-permute-start | bytes 589832 | tf_op jit(solution)/shard_map/vertical_send/ppermute | solution.py:336
  15.7 2.6 %collective-permute-start.7 = (f32[48,8,128]{2,1,0:T(8,128)S(1)}, f32[48,8,128]{2,1,0:T(8,128)S(1)}, u32[]{:S(2)}, u32[]{:S(2)}) collective-permute-start(f32[48,8,128]{2,1,0:T(8,128)S(1)} %get-tuple-element.63), channel_id=1, source_target_pairs={{0,2},{1,3},{2,0},{3,1},{4,6},{5,7},{6,4},{7,5},{8,10},{9,11},{10,... | collective-permute-start | bytes 589832 | tf_op jit(solution)/shard_map/vertical_send/ppermute | solution.py:336
  18.3 1.1 collective-permute-start.8
  19.4 1.5 %disks.1 = (f32[8,128]{1,0:T(8,128)S(1)}, bf16[128,1536]{1,0:T(8,128)(2,1)S(1)}, bf16[128,1536]{1,0:T(8,128)(2,1)S(1)}, f32[288,128]{1,0:T(8,128)S(1)}) custom-call(s32[4]{0:T(128)S(1)} %pad_add_fusion.where_ref, f32[12]{0:T(128)S(1)} %copy-done.22, s32[4,100]{1,0:T(4,128)S(1)} %bitcast.15, s32[3,100]{1,0:T(4,128)S(1)} %bitcast.16, f32[12,24,1536]{2,1,0:T(8,128)S(1)} %copy-done), custom_call_target="tpu_custom_call" | custom-call | tf_op jit(solution)/shard_map/disks/pallas_call | solution.py:495
  20.9 0.9 z_pack.2
  22.1 2.5 %collective-permute-start.1 = (f32[61,8,128]{2,1,0:T(8,128)S(1)}, f32[61,8,128]{2,1,0:T(8,128)S(1)}, u32[]{:S(2)}, u32[]{:S(2)}) collective-permute-start(f32[61,8,128]{2,1,0:T(8,128)S(1)} %get-tuple-element.55), channel_id=1, source_target_pairs={{0,8},{1,9},{2,10},{3,11},{4,12},{5,13},{6,14},{7,15},{8,0},{9,1},... | collective-permute-start | bytes 749576 | tf_op jit(solution)/shard_map/vertical_send/ppermute | solution.py:336
  24.6 1.2 collective-permute-start.2
  25.7 1.7 %collective-permute-done.7.refs_2_ = f32[48,8,128]{2,1,0:T(8,128)S(1)} collective-permute-done((f32[48,8,128]{2,1,0:T(8,128)S(1)}, f32[48,8,128]{2,1,0:T(8,128)S(1)}, u32[]{:S(2)}, u32[]{:S(2)}) %collective-permute-start.7) | collective-permute-done | bytes 196640 | tf_op jit(solution)/shard_map/vertical_send/ppermute | solution.py:336
  27.5 0.7 copy-done.8
  28.2 1.2 %collective-permute-start.9 = (f32[48,8,128]{2,1,0:T(8,128)S(1)}, f32[48,8,128]{2,1,0:T(8,128)S(1)}, u32[]{:S(2)}, u32[]{:S(2)}) collective-permute-start(f32[48,8,128]{2,1,0:T(8,128)S(1)} %get-tuple-element.66), channel_id=1, source_target_pairs={{0,4},{1,5},{2,6},{3,7},{4,8},{5,9},{6,10},{7,11},{8,12},{9,13},{1... | collective-permute-start | bytes 589832 | tf_op jit(solution)/shard_map/vertical_send/ppermute | solution.py:336
  29.5 2.5 %collective-permute-start.10 = (f32[48,8,128]{2,1,0:T(8,128)S(1)}, f32[48,8,128]{2,1,0:T(8,128)S(1)}, u32[]{:S(2)}, u32[]{:S(2)}) collective-permute-start(f32[48,8,128]{2,1,0:T(8,128)S(1)} %get-tuple-element.67), channel_id=1, source_target_pairs={{0,8},{1,9},{2,10},{3,11},{4,12},{5,13},{6,14},{7,15},{8,0},{9,1},... | collective-permute-start | bytes 589832 | tf_op jit(solution)/shard_map/vertical_send/ppermute | solution.py:336
  31.9 1.2 collective-permute-start.11
  33.1 2.1 %collective-permute-done.1.refs_2_ = f32[61,8,128]{2,1,0:T(8,128)S(1)} collective-permute-done((f32[61,8,128]{2,1,0:T(8,128)S(1)}, f32[61,8,128]{2,1,0:T(8,128)S(1)}, u32[]{:S(2)}, u32[]{:S(2)}) %collective-permute-start.1) | collective-permute-done | bytes 249888 | tf_op jit(solution)/shard_map/vertical_send/ppermute | solution.py:336
  35.1 1.9 %collective-permute-done.2.refs_3_ = f32[61,8,128]{2,1,0:T(8,128)S(1)} collective-permute-done((f32[61,8,128]{2,1,0:T(8,128)S(1)}, f32[61,8,128]{2,1,0:T(8,128)S(1)}, u32[]{:S(2)}, u32[]{:S(2)}) %collective-permute-start.2) | collective-permute-done | bytes 249888 | tf_op jit(solution)/shard_map/vertical_send/ppermute | solution.py:336
  37.1 0.7 copy-done.5
  37.8 0.4 collective-permute-start.3
  38.2 3.5 %collective-permute-done.9.refs_5_.refs_1_ = f32[48,8,128]{2,1,0:T(8,128)S(1)} collective-permute-done((f32[48,8,128]{2,1,0:T(8,128)S(1)}, f32[48,8,128]{2,1,0:T(8,128)S(1)}, u32[]{:S(2)}, u32[]{:S(2)}) %collective-permute-start.9) | collective-permute-done | bytes 196640 | tf_op jit(solution)/shard_map/vertical_send/ppermute | solution.py:336
  41.7 5.7 %x_derivative.1 = (f32[12,24,1536]{2,1,0:T(8,128)S(1)}, f32[8,128]{1,0:T(8,128)S(1)}) custom-call(f32[12]{0:T(128)S(1)} %copy-done.22, s32[3,100]{1,0:T(4,128)S(1)} %bitcast.17, f32[12,24,1536]{2,1,0:T(8,128)S(1)} %copy-done, bf16[8,768,256]{2,1,0:T(8,128)(2,1)S(1)} %copy-done.24), custom_call_target="tpu_custom_call" | custom-call | flops 4076863488 | bytes 7340032 | tf_op jit(solution)/shard_map/x_derivative/pallas_call | solution.py:157
  47.4 1.2 %copy-done.1 = f32[12,24,1536]{2,1,0:T(8,128)} copy-done((f32[12,24,1536]{2,1,0:T(8,128)}, f32[12,24,1536]{2,1,0:T(8,128)S(1)}, u32[]{:S(2)}) %copy-start.1) | copy-done | bytes 1769496
  48.6 0.7 copy-done.29
  49.3 3.8 %z_lines.2 = (f32[48,8,128]{2,1,0:T(8,128)}, f32[48,8,128]{2,1,0:T(8,128)}, f32[48,8,128]{2,1,0:T(8,128)}, f32[48,8,128]{2,1,0:T(8,128)}) custom-call(s32[4]{0:T(128)} %copy-done.17, bf16[2,384,384]{2,1,0:T(8,128)(2,1)} %constant.40.clone.matrix_hbm, f32[48,8,128]{2,1,0:T(8,128)} %copy-done.8, f32[48,8,128]{2,1,0:T(8,128)} %copy-done.28, ...), custom_call_target="tpu_custom_call" | custom-call | tf_op jit(solution)/shard_map/z_lines/pallas_call | solution.py:383
  53.2 0.6 copy-done.25
  54.1 1.4 %level_sums.1.sums_ref = f32[8,128]{1,0:T(8,128)} custom-call(f32[61,8,128]{2,1,0:T(8,128)} %copy-done.5, f32[61,8,128]{2,1,0:T(8,128)} %copy-done.25, f32[61,8,128]{2,1,0:T(8,128)} %copy-done.26, f32[61,8,128]{2,1,0:T(8,128)} %copy-done.27, f32[48,8,128]{2,1,0:T(8,128)} %copy-done.8, f32[48,8,128]{2,1,0:T(8,128)} %copy-done.28, f32[48,8,128]{2,1,0:T(8,128)} %copy-done.29, ...), custom_call_target="tpu_custom_call" | custom-call | tf_op jit(solution)/shard_map/level_sums/pallas_call | solution.py:219
  55.7 0.7 copy-done.19
  56.3 3.1 %y_lines.1.refs_4_ = f32[16,28,8,128]{3,2,1,0:T(8,128)} custom-call(bf16[2,384,384]{2,1,0:T(8,128)(2,1)S(1)} %copy-done.9, f32[8,128]{1,0:T(8,128)S(1)} %copy-done.19, f32[16,27,8,128]{3,2,1,0:T(8,128)S(1)} %all-to-all-done.in_ref, f32[48,8,128]{2,1,0:T(8,128)S(1)} %copy-done.6), custom_call_target="tpu_custom_call" | custom-call | tf_op jit(solution)/shard_map/y_lines/pallas_call | solution.py:246
  59.4 8.9 %all-to-all-start.1 = ((f32[16,28,8,128]{3,2,1,0:T(8,128)}), f32[16,28,8,128]{3,2,1,0:T(8,128)S(1)}, u32[]{:S(2)}, u32[]{:S(2)}) async-start(f32[16,28,8,128]{3,2,1,0:T(8,128)} %y_lines.1.refs_4_), calls=%async_computation.1 | async-start | bytes 3670016 | tf_op jit(solution)/shard_map/spanwise_return/all_to_all | solution.py:589
  68.3 3.2 %collective-permute-start.18 = (f32[48,8,128]{2,1,0:T(8,128)S(1)}, f32[48,8,128]{2,1,0:T(8,128)S(1)}, u32[]{:S(2)}, u32[]{:S(2)}) collective-permute-start(f32[48,8,128]{2,1,0:T(8,128)S(1)} %copy-done.33), channel_id=1, source_target_pairs={{0,12},{1,13},{2,14},{3,15},{4,0},{5,1},{6,2},{7,3},{8,4},{9,5},{1... | collective-permute-start | bytes 589832 | tf_op jit(solution)/shard_map/vertical_return/ppermute | solution.py:336
  71.6 1.8 %collective-permute-start.19 = (f32[48,8,128]{2,1,0:T(8,128)S(1)}, f32[48,8,128]{2,1,0:T(8,128)S(1)}, u32[]{:S(2)}, u32[]{:S(2)}) collective-permute-start(f32[48,8,128]{2,1,0:T(8,128)S(1)} %copy-done.32), channel_id=1, source_target_pairs={{0,8},{1,9},{2,10},{3,11},{4,12},{5,13},{6,14},{7,15},{8,0},{9,1},... | collective-permute-start | bytes 589832 | tf_op jit(solution)/shard_map/vertical_return/ppermute | solution.py:336
  73.4 4.4 %z_lines.3 = (f32[60,8,128]{2,1,0:T(8,128)}, f32[60,8,128]{2,1,0:T(8,128)}, f32[60,8,128]{2,1,0:T(8,128)}, f32[60,8,128]{2,1,0:T(8,128)}) custom-call(s32[4]{0:T(128)} %copy-done.17, bf16[2,384,384]{2,1,0:T(8,128)(2,1)} %constant.40.clone.matrix_hbm, f32[61,8,128]{2,1,0:T(8,128)} %copy-done.5, f32[61,8,128]{2,1,0:T(8,128)} %copy-done.25, ...), custom_call_target="tpu_custom_call" | custom-call | tf_op jit(solution)/shard_map/z_lines/pallas_call | solution.py:383
  78.1 0.9 collective-permute-start.13
  79.4 4.7 %collective-permute-done.20.refs_3_ = f32[48,8,128]{2,1,0:T(8,128)S(1)} collective-permute-done((f32[48,8,128]{2,1,0:T(8,128)S(1)}, f32[48,8,128]{2,1,0:T(8,128)S(1)}, u32[]{:S(2)}, u32[]{:S(2)}) %collective-permute-start.20) | collective-permute-done | bytes 196640 | tf_op jit(solution)/shard_map/vertical_return/ppermute | solution.py:336
  84.2 1.4 %collective-permute-start.21 = (f32[48,8,128]{2,1,0:T(8,128)S(1)}, f32[48,8,128]{2,1,0:T(8,128)S(1)}, u32[]{:S(2)}, u32[]{:S(2)}) collective-permute-start(f32[48,8,128]{2,1,0:T(8,128)S(1)} %get-tuple-element.83), channel_id=1, source_target_pairs={{0,3},{1,0},{2,1},{3,2},{4,7},{5,4},{6,5},{7,6},{8,11},{9,8},{10,9... | collective-permute-start | bytes 589832 | tf_op jit(solution)/shard_map/vertical_return/ppermute | solution.py:336
  85.6 0.8 collective-permute-done.13.refs_2_
  86.4 6.6 %collective-permute-done.14.refs_3_ = f32[60,8,128]{2,1,0:T(8,128)S(1)} collective-permute-done((f32[60,8,128]{2,1,0:T(8,128)}, f32[60,8,128]{2,1,0:T(8,128)S(1)}, u32[]{:S(2)}, u32[]{:S(2)}) %collective-permute-start.14) | collective-permute-done | bytes 245792 | tf_op jit(solution)/shard_map/vertical_return/ppermute | solution.py:336
  93.0 0.9 copy-done.14
  94.0 2.6 %collective-permute-start.15 = (f32[60,8,128]{2,1,0:T(8,128)S(1)}, f32[60,8,128]{2,1,0:T(8,128)S(1)}, u32[]{:S(2)}, u32[]{:S(2)}) collective-permute-start(f32[60,8,128]{2,1,0:T(8,128)S(1)} %get-tuple-element.76), channel_id=1, source_target_pairs={{0,12},{1,13},{2,14},{3,15},{4,0},{5,1},{6,2},{7,3},{8,4},{9,5},{1... | collective-permute-start | bytes 737288 | tf_op jit(solution)/shard_map/vertical_return/ppermute | solution.py:336
  96.6 1.3 %collective-permute-start.16 = (f32[60,8,128]{2,1,0:T(8,128)S(1)}, f32[60,8,128]{2,1,0:T(8,128)S(1)}, u32[]{:S(2)}, u32[]{:S(2)}) collective-permute-start(f32[60,8,128]{2,1,0:T(8,128)S(1)} %get-tuple-element.77), channel_id=1, source_target_pairs={{0,8},{1,9},{2,10},{3,11},{4,12},{5,13},{6,14},{7,15},{8,0},{9,1},... | collective-permute-start | bytes 737288 | tf_op jit(solution)/shard_map/vertical_return/ppermute | solution.py:336
  97.9 0.5 collective-permute-start.22
  98.4 6.4 %collective-permute-done.22.refs_6_ = f32[48,8,128]{2,1,0:T(8,128)S(1)} collective-permute-done((f32[48,8,128]{2,1,0:T(8,128)S(1)}, f32[48,8,128]{2,1,0:T(8,128)S(1)}, u32[]{:S(2)}, u32[]{:S(2)}) %collective-permute-start.22) | collective-permute-done | bytes 196640 | tf_op jit(solution)/shard_map/vertical_return/ppermute | solution.py:336
  104.8 5.7 %collective-permute-done.23.refs_7_ = f32[48,8,128]{2,1,0:T(8,128)S(1)} collective-permute-done((f32[48,8,128]{2,1,0:T(8,128)S(1)}, f32[48,8,128]{2,1,0:T(8,128)S(1)}, u32[]{:S(2)}, u32[]{:S(2)}) %collective-permute-start.23) | collective-permute-done | bytes 196640 | tf_op jit(solution)/shard_map/vertical_return/ppermute | solution.py:336
  110.5 0.8 collective-permute-done.17.refs_3_
  111.3 1.3 %z_unpack.1 = f32[288,1536]{1,0:T(8,128)S(1)} custom-call(s32[4]{0:T(128)S(1)} %copy-done.18, f32[288,1536]{1,0:T(8,128)S(1)} %bitcast.13, f32[60,8,128]{2,1,0:T(8,128)S(1)} %get-tuple-element.75.refs_0_, f32[60,8,128]{2,1,0:T(8,128)S(1)} %collective-permute-done.15.refs_1_, f32[60,8,128]{2,1,0:T(8,128)S(1)} %collective-permute-done.16.refs_2_, ...), custom_call_target="tpu_custom_call" | custom-call | tf_op jit(solution)/shard_map/z_unpack/pallas_call | solution.py:428
  112.6 1.2 %copy-done.3 = f32[288,1536]{1,0:T(8,128)} copy-done((f32[288,1536]{1,0:T(8,128)}, f32[288,1536]{1,0:T(8,128)S(1)}, u32[]{:S(2)}) %copy-start.3) | copy-done | bytes 1769496
  113.9 1.5 %copy-done.4 = f32[288,1536]{1,0:T(8,128)S(1)} copy-done((f32[288,1536]{1,0:T(8,128)S(1)}, f32[288,1536]{1,0:T(8,128)}, u32[]{:S(2)}) %copy-start.4) | copy-done | bytes 1769496
  115.3 3.2 %finish.1 = (f32[12,24,1536]{2,1,0:T(8,128)}, f32[1,100]{1,0:T(1,128)}) custom-call(s32[4]{0:T(128)S(1)} %copy-done.18, f32[1,100]{1,0:T(1,128)S(1)} %bitcast.18, f32[8,128]{1,0:T(8,128)S(1)} %get-tuple-element.47.denom_ref, bf16[128,1536]{1,0:T(8,128)(2,1)S(1)} %copy-done.11, bf16[128,1536]{1,0:T(8,128)(2,1)S(1)} %copy-done.13, f32[288,128]{1,0:T(8,128)S(1)} %copy-done.16, ...), custom_call_target="tpu_custom_call" | custom-call | tf_op jit(solution)/shard_map/finish/pallas_call | solution.py:554
  (88 shorter events, 1.9 us)
Async XLA Ops:
  3.1 10.3 %copy-start = (f32[12,24,1536]{2,1,0:T(8,128)S(1)}, f32[12,24,1536]{2,1,0:T(8,128)}, u32[]{:S(2)}) copy-start(f32[12,24,1536]{2,1,0:T(8,128)} %v_ref.5) | copy-start | bytes 5308420
  3.2 52.5 %all-to-all-start = ((f32[16,27,8,128]{3,2,1,0:T(8,128)}), f32[16,27,8,128]{3,2,1,0:T(8,128)S(1)}, u32[]{:S(2)}, u32[]{:S(2)}) async-start(f32[16,27,8,128]{3,2,1,0:T(8,128)} %y_pack.1), calls=%async_computation | async-start | bytes 3538944 | tf_op jit(solution)/shard_map/spanwise_send/all_to_all | solution.py:576
  13.3 6.1 %copy-start.20 = (s32[100,4]{0,1:T(4,128)S(1)}, s32[100,4]{0,1:T(4,128)}, u32[]{:S(2)}) copy-start(s32[100,4]{0,1:T(4,128)} %param.12) | copy-start | bytes 4804
  13.3 6.1 %copy-start.21 = (s32[100,3]{0,1:T(4,128)S(1)}, s32[100,3]{0,1:T(4,128)}, u32[]{:S(2)}) copy-start(s32[100,3]{0,1:T(4,128)} %param.13) | copy-start | bytes 3604
  13.3 6.1 %copy-start.22 = (f32[12]{0:T(128)S(1)}, f32[12]{0:T(128)}, u32[]{:S(2)}) copy-start(f32[12]{0:T(128)} %wind_ref.3) | copy-start | bytes 148
  13.4 7.5 %copy-start.17 = (s32[4]{0:T(128)}, s32[4]{0:T(128)S(1)}, u32[]{:S(2)}) copy-start(s32[4]{0:T(128)S(1)} %pad_add_fusion.where_ref) | copy-start | bytes 52
  14.3 10.3 %collective-permute-start.6 = (f32[48,8,128]{2,1,0:T(8,128)S(1)}, f32[48,8,128]{2,1,0:T(8,128)S(1)}, u32[]{:S(2)}, u32[]{:S(2)}) collective-permute-start(f32[48,8,128]{2,1,0:T(8,128)S(1)} %get-tuple-element.62), channel_id=1, source_target_pairs={{0,1},{1,2},{2,3},{3,0},{4,5},{5,6},{6,7},{7,4},{8,9},{9,10},{10,1... | collective-permute-start | bytes 589832 | tf_op jit(solution)/shard_map/vertical_send/ppermute | solution.py:336
  15.7 11.8 %collective-permute-start.7 = (f32[48,8,128]{2,1,0:T(8,128)S(1)}, f32[48,8,128]{2,1,0:T(8,128)S(1)}, u32[]{:S(2)}, u32[]{:S(2)}) collective-permute-start(f32[48,8,128]{2,1,0:T(8,128)S(1)} %get-tuple-element.63), channel_id=1, source_target_pairs={{0,2},{1,3},{2,0},{3,1},{4,6},{5,7},{6,4},{7,5},{8,10},{9,11},{10,... | collective-permute-start | bytes 589832 | tf_op jit(solution)/shard_map/vertical_send/ppermute | solution.py:336
  18.3 9.2 %collective-permute-start.8 = (f32[48,8,128]{2,1,0:T(8,128)S(1)}, f32[48,8,128]{2,1,0:T(8,128)S(1)}, u32[]{:S(2)}, u32[]{:S(2)}) collective-permute-start(f32[48,8,128]{2,1,0:T(8,128)S(1)} %get-tuple-element.64), channel_id=1, source_target_pairs={{0,3},{1,0},{2,1},{3,2},{4,7},{5,4},{6,5},{7,6},{8,11},{9,8},{10,9... | collective-permute-start | bytes 589832 | tf_op jit(solution)/shard_map/vertical_send/ppermute | solution.py:336
  20.8 16.2 %copy-start.10 = (bf16[128,1536]{1,0:T(8,128)(2,1)}, bf16[128,1536]{1,0:T(8,128)(2,1)S(1)}, u32[]{:S(2)}) copy-start(bf16[128,1536]{1,0:T(8,128)(2,1)S(1)} %get-tuple-element.48.high_ref) | copy-start | bytes 1179652
  20.9 16.2 %copy-start.12 = (bf16[128,1536]{1,0:T(8,128)(2,1)}, bf16[128,1536]{1,0:T(8,128)(2,1)S(1)}, u32[]{:S(2)}) copy-start(bf16[128,1536]{1,0:T(8,128)(2,1)S(1)} %get-tuple-element.49.low_ref) | copy-start | bytes 1179652
  20.9 16.2 %copy-start.15 = (f32[288,128]{1,0:T(8,128)}, f32[288,128]{1,0:T(8,128)S(1)}, u32[]{:S(2)}) copy-start(f32[288,128]{1,0:T(8,128)S(1)} %get-tuple-element.50.radial_ref) | copy-start | bytes 442372
  20.9 20.8 %copy-start.24 = (bf16[8,768,256]{2,1,0:T(8,128)(2,1)S(1)}, bf16[8,768,256]{2,1,0:T(8,128)(2,1)}, u32[]{:S(2)}) copy-start(bf16[8,768,256]{2,1,0:T(8,128)(2,1)} %constant.39.clone.table_ref) | copy-start | bytes 9437188
  21.8 10.1 %collective-permute-start = (f32[61,8,128]{2,1,0:T(8,128)S(1)}, f32[61,8,128]{2,1,0:T(8,128)S(1)}, u32[]{:S(2)}, u32[]{:S(2)}) collective-permute-start(f32[61,8,128]{2,1,0:T(8,128)S(1)} %get-tuple-element.54), channel_id=1, source_target_pairs={{0,4},{1,5},{2,6},{3,7},{4,8},{5,9},{6,10},{7,11},{8,12},{9,13},{1... | collective-permute-start | bytes 749576 | tf_op jit(solution)/shard_map/vertical_send/ppermute | solution.py:336
  22.1 13.0 %collective-permute-start.1 = (f32[61,8,128]{2,1,0:T(8,128)S(1)}, f32[61,8,128]{2,1,0:T(8,128)S(1)}, u32[]{:S(2)}, u32[]{:S(2)}) collective-permute-start(f32[61,8,128]{2,1,0:T(8,128)S(1)} %get-tuple-element.55), channel_id=1, source_target_pairs={{0,8},{1,9},{2,10},{3,11},{4,12},{5,13},{6,14},{7,15},{8,0},{9,1},... | collective-permute-start | bytes 749576 | tf_op jit(solution)/shard_map/vertical_send/ppermute | solution.py:336
  24.6 12.4 %collective-permute-start.2 = (f32[61,8,128]{2,1,0:T(8,128)S(1)}, f32[61,8,128]{2,1,0:T(8,128)S(1)}, u32[]{:S(2)}, u32[]{:S(2)}) collective-permute-start(f32[61,8,128]{2,1,0:T(8,128)S(1)} %get-tuple-element.56), channel_id=1, source_target_pairs={{0,12},{1,13},{2,14},{3,15},{4,0},{5,1},{6,2},{7,3},{8,4},{9,5},{1... | collective-permute-start | bytes 749576 | tf_op jit(solution)/shard_map/vertical_send/ppermute | solution.py:336
  28.2 13.5 %collective-permute-start.9 = (f32[48,8,128]{2,1,0:T(8,128)S(1)}, f32[48,8,128]{2,1,0:T(8,128)S(1)}, u32[]{:S(2)}, u32[]{:S(2)}) collective-permute-start(f32[48,8,128]{2,1,0:T(8,128)S(1)} %get-tuple-element.66), channel_id=1, source_target_pairs={{0,4},{1,5},{2,6},{3,7},{4,8},{5,9},{6,10},{7,11},{8,12},{9,13},{1... | collective-permute-start | bytes 589832 | tf_op jit(solution)/shard_map/vertical_send/ppermute | solution.py:336
  29.5 19.1 %collective-permute-start.10 = (f32[48,8,128]{2,1,0:T(8,128)S(1)}, f32[48,8,128]{2,1,0:T(8,128)S(1)}, u32[]{:S(2)}, u32[]{:S(2)}) collective-permute-start(f32[48,8,128]{2,1,0:T(8,128)S(1)} %get-tuple-element.67), channel_id=1, source_target_pairs={{0,8},{1,9},{2,10},{3,11},{4,12},{5,13},{6,14},{7,15},{8,0},{9,1},... | collective-permute-start | bytes 589832 | tf_op jit(solution)/shard_map/vertical_send/ppermute | solution.py:336
  31.9 16.7 %collective-permute-start.11 = (f32[48,8,128]{2,1,0:T(8,128)S(1)}, f32[48,8,128]{2,1,0:T(8,128)S(1)}, u32[]{:S(2)}, u32[]{:S(2)}) collective-permute-start(f32[48,8,128]{2,1,0:T(8,128)S(1)} %get-tuple-element.68), channel_id=1, source_target_pairs={{0,12},{1,13},{2,14},{3,15},{4,0},{5,1},{6,2},{7,3},{8,4},{9,5},{1... | collective-permute-start | bytes 589832 | tf_op jit(solution)/shard_map/vertical_send/ppermute | solution.py:336
  37.8 15.4 %collective-permute-start.3 = (f32[61,8,128]{2,1,0:T(8,128)S(1)}, f32[61,8,128]{2,1,0:T(8,128)S(1)}, u32[]{:S(2)}, u32[]{:S(2)}) collective-permute-start(f32[61,8,128]{2,1,0:T(8,128)S(1)} %get-tuple-element.58), channel_id=1, source_target_pairs={{0,1},{1,2},{2,3},{3,0},{4,5},{5,6},{6,7},{7,4},{8,9},{9,10},{10,1... | collective-permute-start | bytes 749576 | tf_op jit(solution)/shard_map/vertical_send/ppermute | solution.py:336
  38.2 15.0 %collective-permute-start.4 = (f32[61,8,128]{2,1,0:T(8,128)S(1)}, f32[61,8,128]{2,1,0:T(8,128)S(1)}, u32[]{:S(2)}, u32[]{:S(2)}) collective-permute-start(f32[61,8,128]{2,1,0:T(8,128)S(1)} %get-tuple-element.59), channel_id=1, source_target_pairs={{0,2},{1,3},{2,0},{3,1},{4,6},{5,7},{6,4},{7,5},{8,10},{9,11},{10,... | collective-permute-start | bytes 749576 | tf_op jit(solution)/shard_map/vertical_send/ppermute | solution.py:336
  41.7 5.7 %copy-start.28 = (f32[48,8,128]{2,1,0:T(8,128)}, f32[48,8,128]{2,1,0:T(8,128)S(1)}, u32[]{:S(2)}) copy-start(f32[48,8,128]{2,1,0:T(8,128)S(1)} %collective-permute-done.9.refs_5_.refs_1_) | copy-start | bytes 589828
  41.7 11.5 %collective-permute-start.5 = (f32[61,8,128]{2,1,0:T(8,128)S(1)}, f32[61,8,128]{2,1,0:T(8,128)S(1)}, u32[]{:S(2)}, u32[]{:S(2)}) collective-permute-start(f32[61,8,128]{2,1,0:T(8,128)S(1)} %get-tuple-element.60), channel_id=1, source_target_pairs={{0,3},{1,0},{2,1},{3,2},{4,7},{5,4},{6,5},{7,6},{8,11},{9,8},{10,9... | collective-permute-start | bytes 749576 | tf_op jit(solution)/shard_map/vertical_send/ppermute | solution.py:336
  54.1 1.6 %copy-start.6 = (f32[48,8,128]{2,1,0:T(8,128)S(1)}, f32[48,8,128]{2,1,0:T(8,128)}, u32[]{:S(2)}) copy-start(f32[48,8,128]{2,1,0:T(8,128)} %get-tuple-element.70.after_ref.refs_0_) | copy-start | bytes 589828
  54.1 1.6 %copy-start.9 = (bf16[2,384,384]{2,1,0:T(8,128)(2,1)S(1)}, bf16[2,384,384]{2,1,0:T(8,128)(2,1)}, u32[]{:S(2)}) copy-start(bf16[2,384,384]{2,1,0:T(8,128)(2,1)} %constant.41.clone.matrix_ref) | copy-start | bytes 1769476
  59.4 8.9 %copy-start.33 = (f32[48,8,128]{2,1,0:T(8,128)S(1)}, f32[48,8,128]{2,1,0:T(8,128)}, u32[]{:S(2)}) copy-start(f32[48,8,128]{2,1,0:T(8,128)} %get-tuple-element.79) | copy-start | bytes 589828
  59.4 12.2 %copy-start.32 = (f32[48,8,128]{2,1,0:T(8,128)S(1)}, f32[48,8,128]{2,1,0:T(8,128)}, u32[]{:S(2)}) copy-start(f32[48,8,128]{2,1,0:T(8,128)} %get-tuple-element.80) | copy-start | bytes 589828
  59.4 14.0 %copy-start.31 = (f32[48,8,128]{2,1,0:T(8,128)S(1)}, f32[48,8,128]{2,1,0:T(8,128)}, u32[]{:S(2)}) copy-start(f32[48,8,128]{2,1,0:T(8,128)} %get-tuple-element.81) | copy-start | bytes 589828
  59.4 54.4 %all-to-all-start.1 = ((f32[16,28,8,128]{3,2,1,0:T(8,128)}), f32[16,28,8,128]{3,2,1,0:T(8,128)S(1)}, u32[]{:S(2)}, u32[]{:S(2)}) async-start(f32[16,28,8,128]{3,2,1,0:T(8,128)} %y_lines.1.refs_4_), calls=%async_computation.1 | async-start | bytes 3670016 | tf_op jit(solution)/shard_map/spanwise_return/all_to_all | solution.py:589
  68.3 15.8 %copy-start.7 = (f32[48,8,128]{2,1,0:T(8,128)S(1)}, f32[48,8,128]{2,1,0:T(8,128)}, u32[]{:S(2)}) copy-start(f32[48,8,128]{2,1,0:T(8,128)} %get-tuple-element.70.after_ref.refs_0_) | copy-start | bytes 589828
  68.3 10.7 %collective-permute-start.18 = (f32[48,8,128]{2,1,0:T(8,128)S(1)}, f32[48,8,128]{2,1,0:T(8,128)S(1)}, u32[]{:S(2)}, u32[]{:S(2)}) collective-permute-start(f32[48,8,128]{2,1,0:T(8,128)S(1)} %copy-done.33), channel_id=1, source_target_pairs={{0,12},{1,13},{2,14},{3,15},{4,0},{5,1},{6,2},{7,3},{8,4},{9,5},{1... | collective-permute-start | bytes 589832 | tf_op jit(solution)/shard_map/vertical_return/ppermute | solution.py:336
  71.6 7.8 %collective-permute-start.19 = (f32[48,8,128]{2,1,0:T(8,128)S(1)}, f32[48,8,128]{2,1,0:T(8,128)S(1)}, u32[]{:S(2)}, u32[]{:S(2)}) collective-permute-start(f32[48,8,128]{2,1,0:T(8,128)S(1)} %copy-done.32), channel_id=1, source_target_pairs={{0,8},{1,9},{2,10},{3,11},{4,12},{5,13},{6,14},{7,15},{8,0},{9,1},... | collective-permute-start | bytes 589832 | tf_op jit(solution)/shard_map/vertical_return/ppermute | solution.py:336
  73.4 37.9 %copy-start.2 = (f32[12,24,1536]{2,1,0:T(8,128)S(1)}, f32[12,24,1536]{2,1,0:T(8,128)}, u32[]{:S(2)}) copy-start(f32[12,24,1536]{2,1,0:T(8,128)} %copy-done.1) | copy-start | bytes 5308420
  73.4 37.9 %copy-start.18 = (s32[4]{0:T(128)S(1)}, s32[4]{0:T(128)}, u32[]{:S(2)}) copy-start(s32[4]{0:T(128)} %copy-done.17) | copy-start | bytes 52
  73.4 10.7 %collective-permute-start.20 = (f32[48,8,128]{2,1,0:T(8,128)S(1)}, f32[48,8,128]{2,1,0:T(8,128)S(1)}, u32[]{:S(2)}, u32[]{:S(2)}) collective-permute-start(f32[48,8,128]{2,1,0:T(8,128)S(1)} %copy-done.31), channel_id=1, source_target_pairs={{0,4},{1,5},{2,6},{3,7},{4,8},{5,9},{6,10},{7,11},{8,12},{9,13},{1... | collective-permute-start | bytes 589832 | tf_op jit(solution)/shard_map/vertical_return/ppermute | solution.py:336
  77.9 7.8 %collective-permute-start.12 = (f32[60,8,128]{2,1,0:T(8,128)}, f32[60,8,128]{2,1,0:T(8,128)S(1)}, u32[]{:S(2)}, u32[]{:S(2)}) collective-permute-start(f32[60,8,128]{2,1,0:T(8,128)} %get-tuple-element.72), channel_id=1, source_target_pairs={{0,3},{1,0},{2,1},{3,2},{4,7},{5,4},{6,5},{7,6},{8,11},{9,8},{10,9... | collective-permute-start | bytes 737288 | tf_op jit(solution)/shard_map/vertical_return/ppermute | solution.py:336
  78.1 8.3 %collective-permute-start.13 = (f32[60,8,128]{2,1,0:T(8,128)}, f32[60,8,128]{2,1,0:T(8,128)S(1)}, u32[]{:S(2)}, u32[]{:S(2)}) collective-permute-start(f32[60,8,128]{2,1,0:T(8,128)} %get-tuple-element.73), channel_id=1, source_target_pairs={{0,2},{1,3},{2,0},{3,1},{4,6},{5,7},{6,4},{7,5},{8,10},{9,11},{10,... | collective-permute-start | bytes 737288 | tf_op jit(solution)/shard_map/vertical_return/ppermute | solution.py:336
  79.0 14.0 %collective-permute-start.14 = (f32[60,8,128]{2,1,0:T(8,128)}, f32[60,8,128]{2,1,0:T(8,128)S(1)}, u32[]{:S(2)}, u32[]{:S(2)}) collective-permute-start(f32[60,8,128]{2,1,0:T(8,128)} %get-tuple-element.74), channel_id=1, source_target_pairs={{0,1},{1,2},{2,3},{3,0},{4,5},{5,6},{6,7},{7,4},{8,9},{9,10},{10,1... | collective-permute-start | bytes 737288 | tf_op jit(solution)/shard_map/vertical_return/ppermute | solution.py:336
  84.2 14.2 %collective-permute-start.21 = (f32[48,8,128]{2,1,0:T(8,128)S(1)}, f32[48,8,128]{2,1,0:T(8,128)S(1)}, u32[]{:S(2)}, u32[]{:S(2)}) collective-permute-start(f32[48,8,128]{2,1,0:T(8,128)S(1)} %get-tuple-element.83), channel_id=1, source_target_pairs={{0,3},{1,0},{2,1},{3,2},{4,7},{5,4},{6,5},{7,6},{8,11},{9,8},{10,9... | collective-permute-start | bytes 589832 | tf_op jit(solution)/shard_map/vertical_return/ppermute | solution.py:336
  94.0 16.5 %collective-permute-start.15 = (f32[60,8,128]{2,1,0:T(8,128)S(1)}, f32[60,8,128]{2,1,0:T(8,128)S(1)}, u32[]{:S(2)}, u32[]{:S(2)}) collective-permute-start(f32[60,8,128]{2,1,0:T(8,128)S(1)} %get-tuple-element.76), channel_id=1, source_target_pairs={{0,12},{1,13},{2,14},{3,15},{4,0},{5,1},{6,2},{7,3},{8,4},{9,5},{1... | collective-permute-start | bytes 737288 | tf_op jit(solution)/shard_map/vertical_return/ppermute | solution.py:336
  96.6 13.8 %collective-permute-start.16 = (f32[60,8,128]{2,1,0:T(8,128)S(1)}, f32[60,8,128]{2,1,0:T(8,128)S(1)}, u32[]{:S(2)}, u32[]{:S(2)}) collective-permute-start(f32[60,8,128]{2,1,0:T(8,128)S(1)} %get-tuple-element.77), channel_id=1, source_target_pairs={{0,8},{1,9},{2,10},{3,11},{4,12},{5,13},{6,14},{7,15},{8,0},{9,1},... | collective-permute-start | bytes 737288 | tf_op jit(solution)/shard_map/vertical_return/ppermute | solution.py:336
  97.9 13.4 %collective-permute-start.17 = (f32[60,8,128]{2,1,0:T(8,128)S(1)}, f32[60,8,128]{2,1,0:T(8,128)S(1)}, u32[]{:S(2)}, u32[]{:S(2)}) collective-permute-start(f32[60,8,128]{2,1,0:T(8,128)S(1)} %get-tuple-element.78), channel_id=1, source_target_pairs={{0,4},{1,5},{2,6},{3,7},{4,8},{5,9},{6,10},{7,11},{8,12},{9,13},{1... | collective-permute-start | bytes 737288 | tf_op jit(solution)/shard_map/vertical_return/ppermute | solution.py:336
  97.9 6.9 %collective-permute-start.22 = (f32[48,8,128]{2,1,0:T(8,128)S(1)}, f32[48,8,128]{2,1,0:T(8,128)S(1)}, u32[]{:S(2)}, u32[]{:S(2)}) collective-permute-start(f32[48,8,128]{2,1,0:T(8,128)S(1)} %get-tuple-element.84), channel_id=1, source_target_pairs={{0,2},{1,3},{2,0},{3,1},{4,6},{5,7},{6,4},{7,5},{8,10},{9,11},{10,... | collective-permute-start | bytes 589832 | tf_op jit(solution)/shard_map/vertical_return/ppermute | solution.py:336
  98.4 12.1 %collective-permute-start.23 = (f32[48,8,128]{2,1,0:T(8,128)S(1)}, f32[48,8,128]{2,1,0:T(8,128)S(1)}, u32[]{:S(2)}, u32[]{:S(2)}) collective-permute-start(f32[48,8,128]{2,1,0:T(8,128)S(1)} %get-tuple-element.85), channel_id=1, source_target_pairs={{0,1},{1,2},{2,3},{3,0},{4,5},{5,6},{6,7},{7,4},{8,9},{9,10},{10,1... | collective-permute-start | bytes 589832 | tf_op jit(solution)/shard_map/vertical_return/ppermute | solution.py:336
  111.3 2.5 %copy-start.11 = (bf16[128,1536]{1,0:T(8,128)(2,1)S(1)}, bf16[128,1536]{1,0:T(8,128)(2,1)}, u32[]{:S(2)}) copy-start(bf16[128,1536]{1,0:T(8,128)(2,1)} %copy-done.10) | copy-start | bytes 1179652
  111.3 2.5 %copy-start.13 = (bf16[128,1536]{1,0:T(8,128)(2,1)S(1)}, bf16[128,1536]{1,0:T(8,128)(2,1)}, u32[]{:S(2)}) copy-start(bf16[128,1536]{1,0:T(8,128)(2,1)} %copy-done.12) | copy-start | bytes 1179652
  111.3 2.5 %copy-start.16 = (f32[288,128]{1,0:T(8,128)S(1)}, f32[288,128]{1,0:T(8,128)}, u32[]{:S(2)}) copy-start(f32[288,128]{1,0:T(8,128)} %copy-done.15) | copy-start | bytes 442372
  111.3 2.5 %copy-start.23 = (f32[100]{0:T(128)S(1)}, f32[100]{0:T(128)}, u32[]{:S(2)}) copy-start(f32[100]{0:T(128)} %param.11) | copy-start | bytes 1204
  (12 other events, 10.6 us)

commit v3 on v2

--- a/solution.py
+++ b/solution.py
@@ -23,7 +23,7 @@
 VM = pl.BlockSpec(memory_space=pltpu.VMEM)
 SM = pl.BlockSpec(memory_space=pltpu.SMEM)
 HB = pl.BlockSpec(memory_space=pltpu.HBM)
-ROUTES = (("x", "y", (0, 1, 2, 3, 4)), ("y", "x", (5, 6, 7, 8)))
+ROUTES = (("x", "y", (0, 1, 2, 3, 4, 5)), ("y", "x", (6, 7, 8)))
 
 
 WHOLE = 57
@@ -169,25 +169,26 @@
 
 
 def y_pack_kernel(v_ref, out_ref, from_ref, to_ref, in_sem, out_sem):
+    parts = range(4)
     into = [
-        pltpu.make_async_copy(v_ref.at[pl.ds(z, 1)], from_ref.at[pl.ds(z, 1)], in_sem.at[z])
-        for z in range(DZ)
+        pltpu.make_async_copy(v_ref.at[pl.ds(3 * c, 3)], from_ref.at[pl.ds(3 * c, 3)], in_sem.at[c])
+        for c in parts
     ]
     away = [
-        pltpu.make_async_copy(to_ref.at[pl.ds(d, 1)], out_ref.at[pl.ds(d, 1)], out_sem.at[d])
-        for d in range(N)
+        pltpu.make_async_copy(to_ref.at[pl.ds(4 * c, 4)], out_ref.at[pl.ds(4 * c, 4)], out_sem.at[c])
+        for c in parts
     ]
-    for copy in into:
-        copy.start()
-    for pair in range(DZ * XB):
-        z, xb, d, j = pair // XB, pair % XB, pair // 9, pair % 9
-        if xb == 0:
-            into[z].wait()
-        for yt in range(3):
-            to_ref[d, yt * 9 + j] = from_ref[z, yt * 8 : yt * 8 + 8, xb * BX : xb * BX + BX]
-        if j == 8:
-            away[d].start()
-    wait(away)
+    for c in parts:
+        into[c].start()
+    for c in parts:
+        into[c].wait()
+        for local in range(36 * c, 36 * c + 36):
+            z, xb = local // XB, local % XB
+            for yt in range(3):
+                to_ref[local // 9, yt * 9 + local % 9] = from_ref[z, yt * 8 : yt * 8 + 8, xb * BX : xb * BX + BX]
+        away[c].start()
+    for c in parts:
+        away[c].wait()
 
 
 def y_pack(velocity):
@@ -199,8 +200,8 @@
         scratch_shapes=[
             pltpu.VMEM((DZ, DY, NX), F32),
             pltpu.VMEM((N, 27, 8, BX), F32),
-            pltpu.SemaphoreType.DMA((DZ,)),
-            pltpu.SemaphoreType.DMA((N,)),
+            pltpu.SemaphoreType.DMA((4,)),
+            pltpu.SemaphoreType.DMA((4,)),
         ],
         compiler_params=params(WHOLE),
         name="y_pack",

time: 119 us -> 119 us (level)
  starting transfers between devices: 45.8 us -> 47 us
  waiting for transfers between devices: 34.3 us -> 33.1 us
    ppermute x24, waiting for transfers between devices: 34.2 us -> 31.8 us  [shift(): return lax.ppermute(value, 'pz', moves)]
where the time goes in v3:
time: 119 us
  starting transfers between devices  47 us (39%)
  waiting for transfers between devices  33.1 us (28%)
  Pallas kernels  28.5 us (24%)
  local copies, waits for them, and re-layouts  8.57 us (7%)
  between operations  1.23 us (1%)
    ppermute x24, waiting for transfers between devices, shift(): return lax.ppermute(value, 'pz', moves)  31.8 us
    ppermute x24, starting transfers between devices, shift(): return lax.ppermute(value, 'pz', moves)  27.1 us
    all_to_all x1, starting transfers between devices, body(): received = lax.all_to_all(packed, 'py', 0, 0, tiled=True)  10.1 us
    all_to_all x1, starting transfers between devices, body(): returned = lax.all_to_all(spanwise, 'py', 0, 0, tiled=True)  9.78 us
    unnamed x68, local copies, waits for them, and re-layouts  8.57 us
    pallas_call x2, Pallas kernels, z_lines(): pl.pallas_call(functools.partial(z_kernel, r), in_specs=[SM] + [HB] * 6,...  8.1 us
    pallas_call x1, Pallas kernels, along_x(): pl.pallas_call(x_kernel, in_specs=[SM, VM, VM, VM], out_specs=[VM, VM], o...  5.66 us
    pallas_call x1, Pallas kernels, finish(): pl.pallas_call(final_kernel, in_specs=[SM] + [VM] * 7, out_specs=[HB, VM]...  3.19 us
  transfers between devices with their start and end apart: 26, of which 11 were waited for; matrix products, arithmetic and copies ran while one was open for 0% of the time, Pallas kernels for 17%

profile of v3, /device:TPU:1, one launch (start us, length us, event | category | flops | bytes accessed | tf_op | source)
XLA Modules:
  0.0 118.5 jit_solution(13725716833880221695)
XLA Ops:
  0.6 2.4 %y_pack.1 = f32[16,27,8,128]{3,2,1,0:T(8,128)} custom-call(f32[12,24,1536]{2,1,0:T(8,128)} %v_ref.5), custom_call_target="tpu_custom_call" | custom-call | tf_op jit(solution)/shard_map/y_pack/pallas_call | solution.py:195
  3.0 10.1 %all-to-all-start = ((f32[16,27,8,128]{3,2,1,0:T(8,128)}), f32[16,27,8,128]{3,2,1,0:T(8,128)S(1)}, u32[]{:S(2)}, u32[]{:S(2)}) async-start(f32[16,27,8,128]{3,2,1,0:T(8,128)} %y_pack.1), calls=%async_computation | async-start | bytes 3538944 | tf_op jit(solution)/shard_map/spanwise_send/all_to_all | solution.py:577
  13.3 0.8 z_pack.3
  14.1 1.4 %collective-permute-start.6 = (f32[36,8,128]{2,1,0:T(8,128)S(1)}, f32[36,8,128]{2,1,0:T(8,128)S(1)}, u32[]{:S(2)}, u32[]{:S(2)}) collective-permute-start(f32[36,8,128]{2,1,0:T(8,128)S(1)} %get-tuple-element.62), channel_id=1, source_target_pairs={{0,1},{1,2},{2,3},{3,0},{4,5},{5,6},{6,7},{7,4},{8,9},{9,10},{10,1... | collective-permute-start | bytes 442376 | tf_op jit(solution)/shard_map/vertical_send/ppermute | solution.py:337
  15.5 1.5 %disks.1 = (f32[8,128]{1,0:T(8,128)S(1)}, bf16[128,1536]{1,0:T(8,128)(2,1)S(1)}, bf16[128,1536]{1,0:T(8,128)(2,1)S(1)}, f32[288,128]{1,0:T(8,128)S(1)}) custom-call(s32[4]{0:T(128)S(1)} %pad_add_fusion.where_ref, f32[12]{0:T(128)S(1)} %copy-done.22, s32[4,100]{1,0:T(4,128)S(1)} %bitcast.15, s32[3,100]{1,0:T(4,128)S(1)} %bitcast.16, f32[12,24,1536]{2,1,0:T(8,128)S(1)} %copy-done), custom_call_target="tpu_custom_call" | custom-call | tf_op jit(solution)/shard_map/disks/pallas_call | solution.py:496
  17.0 0.9 z_pack.2
  18.3 2.5 %collective-permute-start.1 = (f32[73,8,128]{2,1,0:T(8,128)S(1)}, f32[73,8,128]{2,1,0:T(8,128)S(1)}, u32[]{:S(2)}, u32[]{:S(2)}) collective-permute-start(f32[73,8,128]{2,1,0:T(8,128)S(1)} %get-tuple-element.55), channel_id=1, source_target_pairs={{0,8},{1,9},{2,10},{3,11},{4,12},{5,13},{6,14},{7,15},{8,0},{9,1},... | collective-permute-start | bytes 897032 | tf_op jit(solution)/shard_map/vertical_send/ppermute | solution.py:337
  20.8 1.2 collective-permute-start.2
  21.9 2.6 %collective-permute-start.7 = (f32[36,8,128]{2,1,0:T(8,128)S(1)}, f32[36,8,128]{2,1,0:T(8,128)S(1)}, u32[]{:S(2)}, u32[]{:S(2)}) collective-permute-start(f32[36,8,128]{2,1,0:T(8,128)S(1)} %get-tuple-element.63), channel_id=1, source_target_pairs={{0,2},{1,3},{2,0},{3,1},{4,6},{5,7},{6,4},{7,5},{8,10},{9,11},{10,... | collective-permute-start | bytes 442376 | tf_op jit(solution)/shard_map/vertical_send/ppermute | solution.py:337
  24.6 1.1 collective-permute-start.8
  25.6 2.1 %collective-permute-done.7.refs_2_ = f32[36,8,128]{2,1,0:T(8,128)S(1)} collective-permute-done((f32[36,8,128]{2,1,0:T(8,128)S(1)}, f32[36,8,128]{2,1,0:T(8,128)S(1)}, u32[]{:S(2)}, u32[]{:S(2)}) %collective-permute-start.7) | collective-permute-done | bytes 147488 | tf_op jit(solution)/shard_map/vertical_send/ppermute | solution.py:337
  27.7 2.6 %collective-permute-done.8.refs_3_ = f32[36,8,128]{2,1,0:T(8,128)S(1)} collective-permute-done((f32[36,8,128]{2,1,0:T(8,128)S(1)}, f32[36,8,128]{2,1,0:T(8,128)S(1)}, u32[]{:S(2)}, u32[]{:S(2)}) %collective-permute-start.8) | collective-permute-done | bytes 147488 | tf_op jit(solution)/shard_map/vertical_send/ppermute | solution.py:337
  30.4 0.7 copy-done.7
  31.4 0.9 collective-permute-start.10
  32.3 1.5 %collective-permute-start.11 = (f32[36,8,128]{2,1,0:T(8,128)S(1)}, f32[36,8,128]{2,1,0:T(8,128)S(1)}, u32[]{:S(2)}, u32[]{:S(2)}) collective-permute-start(f32[36,8,128]{2,1,0:T(8,128)S(1)} %get-tuple-element.68), channel_id=1, source_target_pairs={{0,12},{1,13},{2,14},{3,15},{4,0},{5,1},{6,2},{7,3},{8,4},{9,5},{1... | collective-permute-start | bytes 442376 | tf_op jit(solution)/shard_map/vertical_send/ppermute | solution.py:337
  34.4 0.7 copy-done.5
  35.1 1.3 %collective-permute-start.3 = (f32[73,8,128]{2,1,0:T(8,128)S(1)}, f32[73,8,128]{2,1,0:T(8,128)S(1)}, u32[]{:S(2)}, u32[]{:S(2)}) collective-permute-start(f32[73,8,128]{2,1,0:T(8,128)S(1)} %get-tuple-element.58), channel_id=1, source_target_pairs={{0,1},{1,2},{2,3},{3,0},{4,5},{5,6},{6,7},{7,4},{8,9},{9,10},{10,1... | collective-permute-start | bytes 897032 | tf_op jit(solution)/shard_map/vertical_send/ppermute | solution.py:337
  36.4 2.0 %collective-permute-start.4 = (f32[73,8,128]{2,1,0:T(8,128)S(1)}, f32[73,8,128]{2,1,0:T(8,128)S(1)}, u32[]{:S(2)}, u32[]{:S(2)}) collective-permute-start(f32[73,8,128]{2,1,0:T(8,128)S(1)} %get-tuple-element.59), channel_id=1, source_target_pairs={{0,2},{1,3},{2,0},{3,1},{4,6},{5,7},{6,4},{7,5},{8,10},{9,11},{10,... | collective-permute-start | bytes 897032 | tf_op jit(solution)/shard_map/vertical_send/ppermute | solution.py:337
  38.4 2.2 %collective-permute-start.5 = (f32[73,8,128]{2,1,0:T(8,128)S(1)}, f32[73,8,128]{2,1,0:T(8,128)S(1)}, u32[]{:S(2)}, u32[]{:S(2)}) collective-permute-start(f32[73,8,128]{2,1,0:T(8,128)S(1)} %get-tuple-element.60), channel_id=1, source_target_pairs={{0,3},{1,0},{2,1},{3,2},{4,7},{5,4},{6,5},{7,6},{8,11},{9,8},{10,9... | collective-permute-start | bytes 897032 | tf_op jit(solution)/shard_map/vertical_send/ppermute | solution.py:337
  40.6 5.7 %x_derivative.1 = (f32[12,24,1536]{2,1,0:T(8,128)S(1)}, f32[8,128]{1,0:T(8,128)S(1)}) custom-call(f32[12]{0:T(128)S(1)} %copy-done.22, s32[3,100]{1,0:T(4,128)S(1)} %bitcast.17, f32[12,24,1536]{2,1,0:T(8,128)S(1)} %copy-done, bf16[8,768,256]{2,1,0:T(8,128)(2,1)S(1)} %copy-done.24), custom_call_target="tpu_custom_call" | custom-call | flops 4076863488 | bytes 7340032 | tf_op jit(solution)/shard_map/x_derivative/pallas_call | solution.py:157
  46.3 1.2 %copy-done.1 = f32[12,24,1536]{2,1,0:T(8,128)} copy-done((f32[12,24,1536]{2,1,0:T(8,128)}, f32[12,24,1536]{2,1,0:T(8,128)S(1)}, u32[]{:S(2)}) %copy-start.1) | copy-done | bytes 1769496
  47.5 0.7 copy-done.29
  48.2 3.6 %z_lines.2 = (f32[36,8,128]{2,1,0:T(8,128)}, f32[36,8,128]{2,1,0:T(8,128)}, f32[36,8,128]{2,1,0:T(8,128)}, f32[36,8,128]{2,1,0:T(8,128)}) custom-call(s32[4]{0:T(128)} %copy-done.17, bf16[2,384,384]{2,1,0:T(8,128)(2,1)} %constant.40.clone.matrix_hbm, f32[36,8,128]{2,1,0:T(8,128)} %copy-done.7, f32[36,8,128]{2,1,0:T(8,128)} %copy-done.28, ...), custom_call_target="tpu_custom_call" | custom-call | tf_op jit(solution)/shard_map/z_lines/pallas_call | solution.py:384
  51.9 0.6 copy-done.25
  52.8 1.4 %level_sums.1.sums_ref = f32[8,128]{1,0:T(8,128)} custom-call(f32[73,8,128]{2,1,0:T(8,128)} %copy-done.5, f32[73,8,128]{2,1,0:T(8,128)} %copy-done.25, f32[73,8,128]{2,1,0:T(8,128)} %copy-done.26, f32[73,8,128]{2,1,0:T(8,128)} %copy-done.27, f32[36,8,128]{2,1,0:T(8,128)} %copy-done.7, f32[36,8,128]{2,1,0:T(8,128)} %copy-done.28, f32[36,8,128]{2,1,0:T(8,128)} %copy-done.29, ...), custom_call_target="tpu_custom_call" | custom-call | tf_op jit(solution)/shard_map/level_sums/pallas_call | solution.py:220
  54.2 1.3 %all-to-all-done.in_ref = f32[16,27,8,128]{3,2,1,0:T(8,128)S(1)} async-done(((f32[16,27,8,128]{3,2,1,0:T(8,128)}), f32[16,27,8,128]{3,2,1,0:T(8,128)S(1)}, u32[]{:S(2)}, u32[]{:S(2)}) %all-to-all-start) | async-done | bytes 1769504 | tf_op jit(solution)/shard_map/spanwise_send/all_to_all | solution.py:577
  55.5 0.7 copy-done.19
  56.2 3.1 %y_lines.1.refs_4_ = f32[16,28,8,128]{3,2,1,0:T(8,128)} custom-call(bf16[2,384,384]{2,1,0:T(8,128)(2,1)S(1)} %copy-done.6, f32[8,128]{1,0:T(8,128)S(1)} %copy-done.19, f32[16,27,8,128]{3,2,1,0:T(8,128)S(1)} %all-to-all-done.in_ref, f32[36,8,128]{2,1,0:T(8,128)S(1)} %copy-done.8), custom_call_target="tpu_custom_call" | custom-call | tf_op jit(solution)/shard_map/y_lines/pallas_call | solution.py:247
  59.3 9.8 %all-to-all-start.1 = ((f32[16,28,8,128]{3,2,1,0:T(8,128)}), f32[16,28,8,128]{3,2,1,0:T(8,128)S(1)}, u32[]{:S(2)}, u32[]{:S(2)}) async-start(f32[16,28,8,128]{3,2,1,0:T(8,128)} %y_lines.1.refs_4_), calls=%async_computation.1 | async-start | bytes 3670016 | tf_op jit(solution)/shard_map/spanwise_return/all_to_all | solution.py:590
  69.2 4.5 %z_lines.3 = (f32[72,8,128]{2,1,0:T(8,128)}, f32[72,8,128]{2,1,0:T(8,128)}, f32[72,8,128]{2,1,0:T(8,128)}, f32[72,8,128]{2,1,0:T(8,128)}) custom-call(s32[4]{0:T(128)} %copy-done.17, bf16[2,384,384]{2,1,0:T(8,128)(2,1)} %constant.40.clone.matrix_hbm, f32[73,8,128]{2,1,0:T(8,128)} %copy-done.5, f32[73,8,128]{2,1,0:T(8,128)} %copy-done.25, ...), custom_call_target="tpu_custom_call" | custom-call | tf_op jit(solution)/shard_map/z_lines/pallas_call | solution.py:384
  73.7 2.4 %collective-permute-start.12 = (f32[72,8,128]{2,1,0:T(8,128)}, f32[72,8,128]{2,1,0:T(8,128)S(1)}, u32[]{:S(2)}, u32[]{:S(2)}) collective-permute-start(f32[72,8,128]{2,1,0:T(8,128)} %get-tuple-element.72), channel_id=1, source_target_pairs={{0,3},{1,0},{2,1},{3,2},{4,7},{5,4},{6,5},{7,6},{8,11},{9,8},{10,9... | collective-permute-start | bytes 884744 | tf_op jit(solution)/shard_map/vertical_return/ppermute | solution.py:337
  76.2 0.5 collective-permute-start.13
  76.8 1.3 %collective-permute-start.19 = (f32[36,8,128]{2,1,0:T(8,128)S(1)}, f32[36,8,128]{2,1,0:T(8,128)S(1)}, u32[]{:S(2)}, u32[]{:S(2)}) collective-permute-start(f32[36,8,128]{2,1,0:T(8,128)S(1)} %copy-done.32), channel_id=1, source_target_pairs={{0,8},{1,9},{2,10},{3,11},{4,12},{5,13},{6,14},{7,15},{8,0},{9,1},... | collective-permute-start | bytes 442376 | tf_op jit(solution)/shard_map/vertical_return/ppermute | solution.py:337
  78.2 4.6 %collective-permute-done.19.refs_2_ = f32[36,8,128]{2,1,0:T(8,128)S(1)} collective-permute-done((f32[36,8,128]{2,1,0:T(8,128)S(1)}, f32[36,8,128]{2,1,0:T(8,128)S(1)}, u32[]{:S(2)}, u32[]{:S(2)}) %collective-permute-start.19) | collective-permute-done | bytes 147488 | tf_op jit(solution)/shard_map/vertical_return/ppermute | solution.py:337
  82.8 4.0 %collective-permute-done.20.refs_3_ = f32[36,8,128]{2,1,0:T(8,128)S(1)} collective-permute-done((f32[36,8,128]{2,1,0:T(8,128)S(1)}, f32[36,8,128]{2,1,0:T(8,128)S(1)}, u32[]{:S(2)}, u32[]{:S(2)}) %collective-permute-start.20) | collective-permute-done | bytes 147488 | tf_op jit(solution)/shard_map/vertical_return/ppermute | solution.py:337
  86.9 2.5 %collective-permute-start.21 = (f32[36,8,128]{2,1,0:T(8,128)S(1)}, f32[36,8,128]{2,1,0:T(8,128)S(1)}, u32[]{:S(2)}, u32[]{:S(2)}) collective-permute-start(f32[36,8,128]{2,1,0:T(8,128)S(1)} %get-tuple-element.83), channel_id=1, source_target_pairs={{0,3},{1,0},{2,1},{3,2},{4,7},{5,4},{6,5},{7,6},{8,11},{9,8},{10,9... | collective-permute-start | bytes 442376 | tf_op jit(solution)/shard_map/vertical_return/ppermute | solution.py:337
  89.3 3.8 %collective-permute-done.14.refs_3_ = f32[72,8,128]{2,1,0:T(8,128)S(1)} collective-permute-done((f32[72,8,128]{2,1,0:T(8,128)}, f32[72,8,128]{2,1,0:T(8,128)S(1)}, u32[]{:S(2)}, u32[]{:S(2)}) %collective-permute-start.14) | collective-permute-done | bytes 294944 | tf_op jit(solution)/shard_map/vertical_return/ppermute | solution.py:337
  93.1 1.0 copy-done.14
  94.3 1.5 %collective-permute-start.16 = (f32[72,8,128]{2,1,0:T(8,128)S(1)}, f32[72,8,128]{2,1,0:T(8,128)S(1)}, u32[]{:S(2)}, u32[]{:S(2)}) collective-permute-start(f32[72,8,128]{2,1,0:T(8,128)S(1)} %get-tuple-element.77), channel_id=1, source_target_pairs={{0,8},{1,9},{2,10},{3,11},{4,12},{5,13},{6,14},{7,15},{8,0},{9,1},... | collective-permute-start | bytes 884744 | tf_op jit(solution)/shard_map/vertical_return/ppermute | solution.py:337
  95.8 0.7 collective-permute-start.17
  96.4 0.5 collective-permute-start.22
  97.0 5.3 %collective-permute-done.22.refs_6_ = f32[36,8,128]{2,1,0:T(8,128)S(1)} collective-permute-done((f32[36,8,128]{2,1,0:T(8,128)S(1)}, f32[36,8,128]{2,1,0:T(8,128)S(1)}, u32[]{:S(2)}, u32[]{:S(2)}) %collective-permute-start.22) | collective-permute-done | bytes 147488 | tf_op jit(solution)/shard_map/vertical_return/ppermute | solution.py:337
  102.2 4.2 %collective-permute-done.23.refs_7_ = f32[36,8,128]{2,1,0:T(8,128)S(1)} collective-permute-done((f32[36,8,128]{2,1,0:T(8,128)S(1)}, f32[36,8,128]{2,1,0:T(8,128)S(1)}, u32[]{:S(2)}, u32[]{:S(2)}) %collective-permute-start.23) | collective-permute-done | bytes 147488 | tf_op jit(solution)/shard_map/vertical_return/ppermute | solution.py:337
  106.4 4.7 %collective-permute-done.17.refs_3_ = f32[72,8,128]{2,1,0:T(8,128)S(1)} collective-permute-done((f32[72,8,128]{2,1,0:T(8,128)S(1)}, f32[72,8,128]{2,1,0:T(8,128)S(1)}, u32[]{:S(2)}, u32[]{:S(2)}) %collective-permute-start.17) | collective-permute-done | bytes 294944 | tf_op jit(solution)/shard_map/vertical_return/ppermute | solution.py:337
  111.1 1.3 %z_unpack.1 = f32[288,1536]{1,0:T(8,128)S(1)} custom-call(s32[4]{0:T(128)S(1)} %copy-done.18, f32[288,1536]{1,0:T(8,128)S(1)} %bitcast.13, f32[72,8,128]{2,1,0:T(8,128)S(1)} %get-tuple-element.75.refs_0_, f32[72,8,128]{2,1,0:T(8,128)S(1)} %collective-permute-done.15.refs_1_, f32[72,8,128]{2,1,0:T(8,128)S(1)} %collective-permute-done.16.refs_2_, ...), custom_call_target="tpu_custom_call" | custom-call | tf_op jit(solution)/shard_map/z_unpack/pallas_call | solution.py:429
  112.5 1.2 %copy-done.3 = f32[288,1536]{1,0:T(8,128)} copy-done((f32[288,1536]{1,0:T(8,128)}, f32[288,1536]{1,0:T(8,128)S(1)}, u32[]{:S(2)}) %copy-start.3) | copy-done | bytes 1769496
  113.7 1.5 %copy-done.4 = f32[288,1536]{1,0:T(8,128)S(1)} copy-done((f32[288,1536]{1,0:T(8,128)S(1)}, f32[288,1536]{1,0:T(8,128)}, u32[]{:S(2)}) %copy-start.4) | copy-done | bytes 1769496
  115.2 3.2 %finish.1 = (f32[12,24,1536]{2,1,0:T(8,128)}, f32[1,100]{1,0:T(1,128)}) custom-call(s32[4]{0:T(128)S(1)} %copy-done.18, f32[1,100]{1,0:T(1,128)S(1)} %bitcast.18, f32[8,128]{1,0:T(8,128)S(1)} %get-tuple-element.47.denom_ref, bf16[128,1536]{1,0:T(8,128)(2,1)S(1)} %copy-done.11, bf16[128,1536]{1,0:T(8,128)(2,1)S(1)} %copy-done.13, f32[288,128]{1,0:T(8,128)S(1)} %copy-done.16, ...), custom_call_target="tpu_custom_call" | custom-call | tf_op jit(solution)/shard_map/finish/pallas_call | solution.py:555
  (88 shorter events, 2.4 us)
Async XLA Ops:
  3.0 10.3 %copy-start = (f32[12,24,1536]{2,1,0:T(8,128)S(1)}, f32[12,24,1536]{2,1,0:T(8,128)}, u32[]{:S(2)}) copy-start(f32[12,24,1536]{2,1,0:T(8,128)} %v_ref.5) | copy-start | bytes 5308420
  3.0 52.5 %all-to-all-start = ((f32[16,27,8,128]{3,2,1,0:T(8,128)}), f32[16,27,8,128]{3,2,1,0:T(8,128)S(1)}, u32[]{:S(2)}, u32[]{:S(2)}) async-start(f32[16,27,8,128]{3,2,1,0:T(8,128)} %y_pack.1), calls=%async_computation | async-start | bytes 3538944 | tf_op jit(solution)/shard_map/spanwise_send/all_to_all | solution.py:577
  13.1 2.4 %copy-start.20 = (s32[100,4]{0,1:T(4,128)S(1)}, s32[100,4]{0,1:T(4,128)}, u32[]{:S(2)}) copy-start(s32[100,4]{0,1:T(4,128)} %param.12) | copy-start | bytes 4804
  13.1 2.4 %copy-start.21 = (s32[100,3]{0,1:T(4,128)S(1)}, s32[100,3]{0,1:T(4,128)}, u32[]{:S(2)}) copy-start(s32[100,3]{0,1:T(4,128)} %param.13) | copy-start | bytes 3604
  13.2 2.4 %copy-start.22 = (f32[12]{0:T(128)S(1)}, f32[12]{0:T(128)}, u32[]{:S(2)}) copy-start(f32[12]{0:T(128)} %wind_ref.3) | copy-start | bytes 148
  13.3 3.8 %copy-start.17 = (s32[4]{0:T(128)}, s32[4]{0:T(128)S(1)}, u32[]{:S(2)}) copy-start(s32[4]{0:T(128)S(1)} %pad_add_fusion.where_ref) | copy-start | bytes 52
  14.1 10.5 %collective-permute-start.6 = (f32[36,8,128]{2,1,0:T(8,128)S(1)}, f32[36,8,128]{2,1,0:T(8,128)S(1)}, u32[]{:S(2)}, u32[]{:S(2)}) collective-permute-start(f32[36,8,128]{2,1,0:T(8,128)S(1)} %get-tuple-element.62), channel_id=1, source_target_pairs={{0,1},{1,2},{2,3},{3,0},{4,5},{5,6},{6,7},{7,4},{8,9},{9,10},{10,1... | collective-permute-start | bytes 442376 | tf_op jit(solution)/shard_map/vertical_send/ppermute | solution.py:337
  17.0 17.4 %copy-start.10 = (bf16[128,1536]{1,0:T(8,128)(2,1)}, bf16[128,1536]{1,0:T(8,128)(2,1)S(1)}, u32[]{:S(2)}) copy-start(bf16[128,1536]{1,0:T(8,128)(2,1)S(1)} %get-tuple-element.48.high_ref) | copy-start | bytes 1179652
  17.0 17.4 %copy-start.12 = (bf16[128,1536]{1,0:T(8,128)(2,1)}, bf16[128,1536]{1,0:T(8,128)(2,1)S(1)}, u32[]{:S(2)}) copy-start(bf16[128,1536]{1,0:T(8,128)(2,1)S(1)} %get-tuple-element.49.low_ref) | copy-start | bytes 1179652
  17.0 17.4 %copy-start.15 = (f32[288,128]{1,0:T(8,128)}, f32[288,128]{1,0:T(8,128)S(1)}, u32[]{:S(2)}) copy-start(f32[288,128]{1,0:T(8,128)S(1)} %get-tuple-element.50.radial_ref) | copy-start | bytes 442372
  17.0 23.6 %copy-start.24 = (bf16[8,768,256]{2,1,0:T(8,128)(2,1)S(1)}, bf16[8,768,256]{2,1,0:T(8,128)(2,1)}, u32[]{:S(2)}) copy-start(bf16[8,768,256]{2,1,0:T(8,128)(2,1)} %constant.39.clone.table_ref) | copy-start | bytes 9437188
  18.0 14.3 %collective-permute-start = (f32[73,8,128]{2,1,0:T(8,128)S(1)}, f32[73,8,128]{2,1,0:T(8,128)S(1)}, u32[]{:S(2)}, u32[]{:S(2)}) collective-permute-start(f32[73,8,128]{2,1,0:T(8,128)S(1)} %get-tuple-element.54), channel_id=1, source_target_pairs={{0,4},{1,5},{2,6},{3,7},{4,8},{5,9},{6,10},{7,11},{8,12},{9,13},{1... | collective-permute-start | bytes 897032 | tf_op jit(solution)/shard_map/vertical_send/ppermute | solution.py:337
  18.3 15.7 %collective-permute-start.1 = (f32[73,8,128]{2,1,0:T(8,128)S(1)}, f32[73,8,128]{2,1,0:T(8,128)S(1)}, u32[]{:S(2)}, u32[]{:S(2)}) collective-permute-start(f32[73,8,128]{2,1,0:T(8,128)S(1)} %get-tuple-element.55), channel_id=1, source_target_pairs={{0,8},{1,9},{2,10},{3,11},{4,12},{5,13},{6,14},{7,15},{8,0},{9,1},... | collective-permute-start | bytes 897032 | tf_op jit(solution)/shard_map/vertical_send/ppermute | solution.py:337
  20.8 13.5 %collective-permute-start.2 = (f32[73,8,128]{2,1,0:T(8,128)S(1)}, f32[73,8,128]{2,1,0:T(8,128)S(1)}, u32[]{:S(2)}, u32[]{:S(2)}) collective-permute-start(f32[73,8,128]{2,1,0:T(8,128)S(1)} %get-tuple-element.56), channel_id=1, source_target_pairs={{0,12},{1,13},{2,14},{3,15},{4,0},{5,1},{6,2},{7,3},{8,4},{9,5},{1... | collective-permute-start | bytes 897032 | tf_op jit(solution)/shard_map/vertical_send/ppermute | solution.py:337
  21.9 5.8 %collective-permute-start.7 = (f32[36,8,128]{2,1,0:T(8,128)S(1)}, f32[36,8,128]{2,1,0:T(8,128)S(1)}, u32[]{:S(2)}, u32[]{:S(2)}) collective-permute-start(f32[36,8,128]{2,1,0:T(8,128)S(1)} %get-tuple-element.63), channel_id=1, source_target_pairs={{0,2},{1,3},{2,0},{3,1},{4,6},{5,7},{6,4},{7,5},{8,10},{9,11},{10,... | collective-permute-start | bytes 442376 | tf_op jit(solution)/shard_map/vertical_send/ppermute | solution.py:337
  24.6 5.8 %collective-permute-start.8 = (f32[36,8,128]{2,1,0:T(8,128)S(1)}, f32[36,8,128]{2,1,0:T(8,128)S(1)}, u32[]{:S(2)}, u32[]{:S(2)}) collective-permute-start(f32[36,8,128]{2,1,0:T(8,128)S(1)} %get-tuple-element.64), channel_id=1, source_target_pairs={{0,3},{1,0},{2,1},{3,2},{4,7},{5,4},{6,5},{7,6},{8,11},{9,8},{10,9... | collective-permute-start | bytes 442376 | tf_op jit(solution)/shard_map/vertical_send/ppermute | solution.py:337
  31.1 7.4 %collective-permute-start.9 = (f32[36,8,128]{2,1,0:T(8,128)S(1)}, f32[36,8,128]{2,1,0:T(8,128)S(1)}, u32[]{:S(2)}, u32[]{:S(2)}) collective-permute-start(f32[36,8,128]{2,1,0:T(8,128)S(1)} %get-tuple-element.66), channel_id=1, source_target_pairs={{0,4},{1,5},{2,6},{3,7},{4,8},{5,9},{6,10},{7,11},{8,12},{9,13},{1... | collective-permute-start | bytes 442376 | tf_op jit(solution)/shard_map/vertical_send/ppermute | solution.py:337
  31.4 16.1 %collective-permute-start.10 = (f32[36,8,128]{2,1,0:T(8,128)S(1)}, f32[36,8,128]{2,1,0:T(8,128)S(1)}, u32[]{:S(2)}, u32[]{:S(2)}) collective-permute-start(f32[36,8,128]{2,1,0:T(8,128)S(1)} %get-tuple-element.67), channel_id=1, source_target_pairs={{0,8},{1,9},{2,10},{3,11},{4,12},{5,13},{6,14},{7,15},{8,0},{9,1},... | collective-permute-start | bytes 442376 | tf_op jit(solution)/shard_map/vertical_send/ppermute | solution.py:337
  32.3 15.2 %collective-permute-start.11 = (f32[36,8,128]{2,1,0:T(8,128)S(1)}, f32[36,8,128]{2,1,0:T(8,128)S(1)}, u32[]{:S(2)}, u32[]{:S(2)}) collective-permute-start(f32[36,8,128]{2,1,0:T(8,128)S(1)} %get-tuple-element.68), channel_id=1, source_target_pairs={{0,12},{1,13},{2,14},{3,15},{4,0},{5,1},{6,2},{7,3},{8,4},{9,5},{1... | collective-permute-start | bytes 442376 | tf_op jit(solution)/shard_map/vertical_send/ppermute | solution.py:337
  35.1 16.8 %collective-permute-start.3 = (f32[73,8,128]{2,1,0:T(8,128)S(1)}, f32[73,8,128]{2,1,0:T(8,128)S(1)}, u32[]{:S(2)}, u32[]{:S(2)}) collective-permute-start(f32[73,8,128]{2,1,0:T(8,128)S(1)} %get-tuple-element.58), channel_id=1, source_target_pairs={{0,1},{1,2},{2,3},{3,0},{4,5},{5,6},{6,7},{7,4},{8,9},{9,10},{10,1... | collective-permute-start | bytes 897032 | tf_op jit(solution)/shard_map/vertical_send/ppermute | solution.py:337
  36.4 15.5 %collective-permute-start.4 = (f32[73,8,128]{2,1,0:T(8,128)S(1)}, f32[73,8,128]{2,1,0:T(8,128)S(1)}, u32[]{:S(2)}, u32[]{:S(2)}) collective-permute-start(f32[73,8,128]{2,1,0:T(8,128)S(1)} %get-tuple-element.59), channel_id=1, source_target_pairs={{0,2},{1,3},{2,0},{3,1},{4,6},{5,7},{6,4},{7,5},{8,10},{9,11},{10,... | collective-permute-start | bytes 897032 | tf_op jit(solution)/shard_map/vertical_send/ppermute | solution.py:337
  38.4 7.8 %copy-start.28 = (f32[36,8,128]{2,1,0:T(8,128)}, f32[36,8,128]{2,1,0:T(8,128)S(1)}, u32[]{:S(2)}) copy-start(f32[36,8,128]{2,1,0:T(8,128)S(1)} %collective-permute-done.9.refs_5_.refs_1_) | copy-start | bytes 442372
  38.4 13.5 %collective-permute-start.5 = (f32[73,8,128]{2,1,0:T(8,128)S(1)}, f32[73,8,128]{2,1,0:T(8,128)S(1)}, u32[]{:S(2)}, u32[]{:S(2)}) collective-permute-start(f32[73,8,128]{2,1,0:T(8,128)S(1)} %get-tuple-element.60), channel_id=1, source_target_pairs={{0,3},{1,0},{2,1},{3,2},{4,7},{5,4},{6,5},{7,6},{8,11},{9,8},{10,9... | collective-permute-start | bytes 897032 | tf_op jit(solution)/shard_map/vertical_send/ppermute | solution.py:337
  52.8 2.7 %copy-start.6 = (bf16[2,384,384]{2,1,0:T(8,128)(2,1)S(1)}, bf16[2,384,384]{2,1,0:T(8,128)(2,1)}, u32[]{:S(2)}) copy-start(bf16[2,384,384]{2,1,0:T(8,128)(2,1)} %constant.41.clone.matrix_ref) | copy-start | bytes 1769476
  52.8 2.7 %copy-start.8 = (f32[36,8,128]{2,1,0:T(8,128)S(1)}, f32[36,8,128]{2,1,0:T(8,128)}, u32[]{:S(2)}) copy-start(f32[36,8,128]{2,1,0:T(8,128)} %get-tuple-element.70.after_ref.refs_0_) | copy-start | bytes 442372
  59.3 9.8 %copy-start.33 = (f32[36,8,128]{2,1,0:T(8,128)S(1)}, f32[36,8,128]{2,1,0:T(8,128)}, u32[]{:S(2)}) copy-start(f32[36,8,128]{2,1,0:T(8,128)} %get-tuple-element.79) | copy-start | bytes 442372
  59.3 54.4 %all-to-all-start.1 = ((f32[16,28,8,128]{3,2,1,0:T(8,128)}), f32[16,28,8,128]{3,2,1,0:T(8,128)S(1)}, u32[]{:S(2)}, u32[]{:S(2)}) async-start(f32[16,28,8,128]{3,2,1,0:T(8,128)} %y_lines.1.refs_4_), calls=%async_computation.1 | async-start | bytes 3670016 | tf_op jit(solution)/shard_map/spanwise_return/all_to_all | solution.py:590
  69.0 7.8 %copy-start.32 = (f32[36,8,128]{2,1,0:T(8,128)S(1)}, f32[36,8,128]{2,1,0:T(8,128)}, u32[]{:S(2)}) copy-start(f32[36,8,128]{2,1,0:T(8,128)} %get-tuple-element.80) | copy-start | bytes 442372
  69.1 9.1 %copy-start.31 = (f32[36,8,128]{2,1,0:T(8,128)S(1)}, f32[36,8,128]{2,1,0:T(8,128)}, u32[]{:S(2)}) copy-start(f32[36,8,128]{2,1,0:T(8,128)} %get-tuple-element.81) | copy-start | bytes 442372
  69.1 17.7 %copy-start.9 = (f32[36,8,128]{2,1,0:T(8,128)S(1)}, f32[36,8,128]{2,1,0:T(8,128)}, u32[]{:S(2)}) copy-start(f32[36,8,128]{2,1,0:T(8,128)} %get-tuple-element.70.after_ref.refs_0_) | copy-start | bytes 442372
  69.1 9.1 %collective-permute-start.18 = (f32[36,8,128]{2,1,0:T(8,128)S(1)}, f32[36,8,128]{2,1,0:T(8,128)S(1)}, u32[]{:S(2)}, u32[]{:S(2)}) collective-permute-start(f32[36,8,128]{2,1,0:T(8,128)S(1)} %copy-done.33), channel_id=1, source_target_pairs={{0,12},{1,13},{2,14},{3,15},{4,0},{5,1},{6,2},{7,3},{8,4},{9,5},{1... | collective-permute-start | bytes 442376 | tf_op jit(solution)/shard_map/vertical_return/ppermute | solution.py:337
  69.2 41.9 %copy-start.18 = (s32[4]{0:T(128)S(1)}, s32[4]{0:T(128)}, u32[]{:S(2)}) copy-start(s32[4]{0:T(128)} %copy-done.17) | copy-start | bytes 52
  73.7 37.4 %copy-start.2 = (f32[12,24,1536]{2,1,0:T(8,128)S(1)}, f32[12,24,1536]{2,1,0:T(8,128)}, u32[]{:S(2)}) copy-start(f32[12,24,1536]{2,1,0:T(8,128)} %copy-done.1) | copy-start | bytes 5308420
  73.7 15.6 %collective-permute-start.12 = (f32[72,8,128]{2,1,0:T(8,128)}, f32[72,8,128]{2,1,0:T(8,128)S(1)}, u32[]{:S(2)}, u32[]{:S(2)}) collective-permute-start(f32[72,8,128]{2,1,0:T(8,128)} %get-tuple-element.72), channel_id=1, source_target_pairs={{0,3},{1,0},{2,1},{3,2},{4,7},{5,4},{6,5},{7,6},{8,11},{9,8},{10,9... | collective-permute-start | bytes 884744 | tf_op jit(solution)/shard_map/vertical_return/ppermute | solution.py:337
  76.2 13.2 %collective-permute-start.13 = (f32[72,8,128]{2,1,0:T(8,128)}, f32[72,8,128]{2,1,0:T(8,128)S(1)}, u32[]{:S(2)}, u32[]{:S(2)}) collective-permute-start(f32[72,8,128]{2,1,0:T(8,128)} %get-tuple-element.73), channel_id=1, source_target_pairs={{0,2},{1,3},{2,0},{3,1},{4,6},{5,7},{6,4},{7,5},{8,10},{9,11},{10,... | collective-permute-start | bytes 884744 | tf_op jit(solution)/shard_map/vertical_return/ppermute | solution.py:337
  76.6 16.5 %collective-permute-start.14 = (f32[72,8,128]{2,1,0:T(8,128)}, f32[72,8,128]{2,1,0:T(8,128)S(1)}, u32[]{:S(2)}, u32[]{:S(2)}) collective-permute-start(f32[72,8,128]{2,1,0:T(8,128)} %get-tuple-element.74), channel_id=1, source_target_pairs={{0,1},{1,2},{2,3},{3,0},{4,5},{5,6},{6,7},{7,4},{8,9},{9,10},{10,1... | collective-permute-start | bytes 884744 | tf_op jit(solution)/shard_map/vertical_return/ppermute | solution.py:337
  76.8 5.9 %collective-permute-start.19 = (f32[36,8,128]{2,1,0:T(8,128)S(1)}, f32[36,8,128]{2,1,0:T(8,128)S(1)}, u32[]{:S(2)}, u32[]{:S(2)}) collective-permute-start(f32[36,8,128]{2,1,0:T(8,128)S(1)} %copy-done.32), channel_id=1, source_target_pairs={{0,8},{1,9},{2,10},{3,11},{4,12},{5,13},{6,14},{7,15},{8,0},{9,1},... | collective-permute-start | bytes 442376 | tf_op jit(solution)/shard_map/vertical_return/ppermute | solution.py:337
  78.2 8.6 %collective-permute-start.20 = (f32[36,8,128]{2,1,0:T(8,128)S(1)}, f32[36,8,128]{2,1,0:T(8,128)S(1)}, u32[]{:S(2)}, u32[]{:S(2)}) collective-permute-start(f32[36,8,128]{2,1,0:T(8,128)S(1)} %copy-done.31), channel_id=1, source_target_pairs={{0,4},{1,5},{2,6},{3,7},{4,8},{5,9},{6,10},{7,11},{8,12},{9,13},{1... | collective-permute-start | bytes 442376 | tf_op jit(solution)/shard_map/vertical_return/ppermute | solution.py:337
  86.9 10.1 %collective-permute-start.21 = (f32[36,8,128]{2,1,0:T(8,128)S(1)}, f32[36,8,128]{2,1,0:T(8,128)S(1)}, u32[]{:S(2)}, u32[]{:S(2)}) collective-permute-start(f32[36,8,128]{2,1,0:T(8,128)S(1)} %get-tuple-element.83), channel_id=1, source_target_pairs={{0,3},{1,0},{2,1},{3,2},{4,7},{5,4},{6,5},{7,6},{8,11},{9,8},{10,9... | collective-permute-start | bytes 442376 | tf_op jit(solution)/shard_map/vertical_return/ppermute | solution.py:337
  94.2 12.2 %collective-permute-start.15 = (f32[72,8,128]{2,1,0:T(8,128)S(1)}, f32[72,8,128]{2,1,0:T(8,128)S(1)}, u32[]{:S(2)}, u32[]{:S(2)}) collective-permute-start(f32[72,8,128]{2,1,0:T(8,128)S(1)} %get-tuple-element.76), channel_id=1, source_target_pairs={{0,12},{1,13},{2,14},{3,15},{4,0},{5,1},{6,2},{7,3},{8,4},{9,5},{1... | collective-permute-start | bytes 884744 | tf_op jit(solution)/shard_map/vertical_return/ppermute | solution.py:337
  94.3 12.1 %collective-permute-start.16 = (f32[72,8,128]{2,1,0:T(8,128)S(1)}, f32[72,8,128]{2,1,0:T(8,128)S(1)}, u32[]{:S(2)}, u32[]{:S(2)}) collective-permute-start(f32[72,8,128]{2,1,0:T(8,128)S(1)} %get-tuple-element.77), channel_id=1, source_target_pairs={{0,8},{1,9},{2,10},{3,11},{4,12},{5,13},{6,14},{7,15},{8,0},{9,1},... | collective-permute-start | bytes 884744 | tf_op jit(solution)/shard_map/vertical_return/ppermute | solution.py:337
  95.8 15.3 %collective-permute-start.17 = (f32[72,8,128]{2,1,0:T(8,128)S(1)}, f32[72,8,128]{2,1,0:T(8,128)S(1)}, u32[]{:S(2)}, u32[]{:S(2)}) collective-permute-start(f32[72,8,128]{2,1,0:T(8,128)S(1)} %get-tuple-element.78), channel_id=1, source_target_pairs={{0,4},{1,5},{2,6},{3,7},{4,8},{5,9},{6,10},{7,11},{8,12},{9,13},{1... | collective-permute-start | bytes 884744 | tf_op jit(solution)/shard_map/vertical_return/ppermute | solution.py:337
  96.4 5.8 %collective-permute-start.22 = (f32[36,8,128]{2,1,0:T(8,128)S(1)}, f32[36,8,128]{2,1,0:T(8,128)S(1)}, u32[]{:S(2)}, u32[]{:S(2)}) collective-permute-start(f32[36,8,128]{2,1,0:T(8,128)S(1)} %get-tuple-element.84), channel_id=1, source_target_pairs={{0,2},{1,3},{2,0},{3,1},{4,6},{5,7},{6,4},{7,5},{8,10},{9,11},{10,... | collective-permute-start | bytes 442376 | tf_op jit(solution)/shard_map/vertical_return/ppermute | solution.py:337
  97.0 9.4 %collective-permute-start.23 = (f32[36,8,128]{2,1,0:T(8,128)S(1)}, f32[36,8,128]{2,1,0:T(8,128)S(1)}, u32[]{:S(2)}, u32[]{:S(2)}) collective-permute-start(f32[36,8,128]{2,1,0:T(8,128)S(1)} %get-tuple-element.85), channel_id=1, source_target_pairs={{0,1},{1,2},{2,3},{3,0},{4,5},{5,6},{6,7},{7,4},{8,9},{9,10},{10,1... | collective-permute-start | bytes 442376 | tf_op jit(solution)/shard_map/vertical_return/ppermute | solution.py:337
  111.1 2.6 %copy-start.11 = (bf16[128,1536]{1,0:T(8,128)(2,1)S(1)}, bf16[128,1536]{1,0:T(8,128)(2,1)}, u32[]{:S(2)}) copy-start(bf16[128,1536]{1,0:T(8,128)(2,1)} %copy-done.10) | copy-start | bytes 1179652
  111.1 2.6 %copy-start.13 = (bf16[128,1536]{1,0:T(8,128)(2,1)S(1)}, bf16[128,1536]{1,0:T(8,128)(2,1)}, u32[]{:S(2)}) copy-start(bf16[128,1536]{1,0:T(8,128)(2,1)} %copy-done.12) | copy-start | bytes 1179652
  111.1 2.6 %copy-start.16 = (f32[288,128]{1,0:T(8,128)S(1)}, f32[288,128]{1,0:T(8,128)}, u32[]{:S(2)}) copy-start(f32[288,128]{1,0:T(8,128)} %copy-done.15) | copy-start | bytes 442372
  111.1 2.6 %copy-start.23 = (f32[100]{0:T(128)S(1)}, f32[100]{0:T(128)}, u32[]{:S(2)}) copy-start(f32[100]{0:T(128)} %param.11) | copy-start | bytes 1204
  (12 other events, 10.7 us)

commit v4 on v3

--- a/solution.py
+++ b/solution.py
@@ -23,10 +23,10 @@
 VM = pl.BlockSpec(memory_space=pltpu.VMEM)
 SM = pl.BlockSpec(memory_space=pltpu.SMEM)
 HB = pl.BlockSpec(memory_space=pltpu.HBM)
-ROUTES = (("x", "y", (0, 1, 2, 3, 4, 5)), ("y", "x", (6, 7, 8)))
-
-
-WHOLE = 57
+ROUTES = (("x", "y", (0, 1, 2, 3, 4)), ("y", "x", (5, 6, 7, 8)))
+
+
+WHOLE = 56
 
 
 class Mover:
@@ -209,26 +209,26 @@
 
 
 def sums_kernel(*refs):
-    sources, (out_ref, sums_ref, sems) = refs[:8], refs[9:]
+    sources, (out_ref, sums_ref, sems) = refs[:8], refs[8:]
     move = Mover(sems)
     last = 4 * tiles_of(ROUTES[0])
     wait([move.start(sources[i].at[last], sums_ref.at[i]) for i in range(4)])
     out_ref[...] = (sums_ref[0] + sums_ref[1]) + (sums_ref[2] + sums_ref[3])
 
 
-def level_sums(arrived, term_x):
+def level_sums(arrived):
     return pl.pallas_call(
         sums_kernel,
-        in_specs=[HB] * 9,
+        in_specs=[HB] * 8,
         out_specs=VM,
         out_shape=jax.ShapeDtypeStruct((8, BX), F32),
         scratch_shapes=[pltpu.VMEM((4, 8, BX), F32), pltpu.SemaphoreType.DMA((4,))],
-        compiler_params=params(WHOLE),
+        compiler_params=params(),
         name="level_sums",
-    )(*arrived, term_x)
-
-
-def y_kernel(matrix_ref, sums_ref, in_ref, after_ref, out_ref):
+    )(*arrived)
+
+
+def y_kernel(matrix_ref, sums_ref, in_ref, out_ref, done_ref):
     for group in range(3):
         tiles = []
         for j in range(3 * group, 3 * group + 3):
@@ -241,17 +241,18 @@
                 out_ref[:, yt * 9 + 3 * group + k] = value[:, yt]
     for d in range(N):
         out_ref[d, 27] = sums_ref[...]
-
-
-def y_lines(sums, received, after):
+    done_ref[...] = sums_ref[...]
+
+
+def y_lines(sums, received):
     return pl.pallas_call(
         y_kernel,
-        in_specs=[VM] * 3 + [HB],
-        out_specs=VM,
-        out_shape=jax.ShapeDtypeStruct((N, 28, 8, BX), F32),
+        in_specs=[VM] * 3,
+        out_specs=[VM] * 2,
+        out_shape=[jax.ShapeDtypeStruct((N, 28, 8, BX), F32), jax.ShapeDtypeStruct((8, BX), F32)],
         compiler_params=params(16),
         name="y_lines",
-    )(jnp.asarray(np.stack(y_matrix())), sums, received, after)
+    )(jnp.asarray(np.stack(y_matrix())), sums, received)
 
 
 def device_at(route, place_first, place_second):
@@ -341,61 +342,69 @@
     return [arrays[0]] + [shift(arrays[k], axis, sign * k) for k in range(1, 4)]
 
 
-def z_kernel(r, where_ref, matrix_hbm, *refs):
-    ins_hbm, outs_hbm, refs = refs[:4], refs[5:9], refs[9:]
-    ins, outs, (matrix_ref, lines_ref, sems) = refs[:4], refs[4:8], refs[8:]
-    route = ROUTES[r]
-    first, second = places(route, where_ref)
-    tiles, width = tiles_of(route), len(route[2])
+def z_kernel(where_ref, after_ref, high_hbm, low_hbm, *refs):
+    ins_hbm, outs_hbm, refs = refs[:8], refs[8:16], refs[16:]
+    ins, outs, (high_ref, low_ref, lines_ref, sems) = refs[:8], refs[8:16], refs[16:]
     move = Mover(sems)
-    fetch = [move.start(ins_hbm[i], ins[i]) for i in range(4)]
-    fetch_matrix = move.start(matrix_hbm, matrix_ref)
+    fetch = [move.start(ins_hbm[i], ins[i]) for i in range(8)]
+    fetch_matrix = [move.start(high_hbm, high_ref), move.start(low_hbm, low_ref)]
     away = []
 
-    def spots(k2):
+    def spots(r, k2):
+        route = ROUTES[r]
+        first, second = places(route, where_ref)
+        tiles, width = tiles_of(route), len(route[2])
         for k1 in range(4):
             device = device_at(route, (first - k1) % 4, (second - k2) % 4)
-            yield device, slice(k1 * tiles, (k1 + 1) * tiles)
-
-    for k2 in range(4):
-        fetch[k2].wait()
-        for device, outer in spots(k2):
-            lines_ref[device] = ins[k2][outer]
-    columns = []
-    for j in range(width):
-        columns.append(jnp.stack([lines_ref[:, rt * width + j] for rt in range(3)], axis=1).reshape(N * 24, BX))
-    high, low = halves(jnp.concatenate(columns, axis=1))
-    fetch_matrix.wait()
-    got = dot(matrix_ref[0], high) + dot(matrix_ref[1], high) + dot(matrix_ref[0], low)
-    for j in range(width):
-        value = got[:, j * BX : j * BX + BX].reshape(N, 3, 8, BX)
-        for rt in range(3):
-            lines_ref[:, rt * width + j] = value[:, rt]
-    for k2 in range(4):
-        for device, outer in spots(k2):
-            outs[k2][outer] = lines_ref[device]
-        away.append(move.start(outs[k2], outs_hbm[k2]))
+            for rt in range(3):
+                at = k1 * tiles + rt * width
+                into = rt * 9 + route[2][0]
+                yield device, slice(at, at + width), slice(into, into + width)
+
+    for r in range(2):
+        for k2 in range(4):
+            fetch[r * 4 + k2].wait()
+            for device, outer, inner in spots(r, k2):
+                lines_ref[device, inner] = ins[r * 4 + k2][outer]
+    wait(fetch_matrix)
+    for r, columns in enumerate((ROUTES[0][2], ROUTES[1][2])):
+        tiles = []
+        for j in columns:
+            tiles.append(jnp.stack([lines_ref[:, rt * 9 + j] for rt in range(3)], axis=1).reshape(N * 24, BX))
+        high, low = halves(jnp.concatenate(tiles, axis=1))
+        got = dot(high_ref[...], high) + dot(low_ref[...], high) + dot(high_ref[...], low)
+        for k, j in enumerate(columns):
+            value = got[:, k * BX : k * BX + BX].reshape(N, 3, 8, BX)
+            for rt in range(3):
+                lines_ref[:, rt * 9 + j] = value[:, rt]
+        for k2 in range(4):
+            for device, outer, inner in spots(r, k2):
+                outs[r * 4 + k2][outer] = lines_ref[device, inner]
+            away.append(move.start(outs[r * 4 + k2], outs_hbm[r * 4 + k2]))
     wait(away)
 
 
-def z_lines(r, where, after, arrays):
-    tiles = tiles_of(ROUTES[r])
-    shapes = [jax.ShapeDtypeStruct((4 * tiles, 8, BX), F32)] * 4
-    return pl.pallas_call(
-        functools.partial(z_kernel, r),
-        in_specs=[SM] + [HB] * 6,
-        out_specs=[HB] * 4,
+def z_lines(where, after, arrays):
+    high, low = z_matrix()
+    shapes = []
+    for r, route in enumerate(ROUTES):
+        shapes += [jax.ShapeDtypeStruct((4 * tiles_of(route), 8, BX), F32)] * 4
+    return pl.pallas_call(
+        z_kernel,
+        in_specs=[SM, VM] + [HB] * 10,
+        out_specs=[HB] * 8,
         out_shape=shapes,
         scratch_shapes=[pltpu.VMEM(a.shape, F32) for a in arrays]
         + [pltpu.VMEM(a.shape, F32) for a in shapes]
         + [
-            pltpu.VMEM((2, N * 24, N * 24), BF16),
-            pltpu.VMEM((N, tiles, 8, BX), F32),
-            pltpu.SemaphoreType.DMA((9,)),
+            pltpu.VMEM((N * 24, N * 24), BF16),
+            pltpu.VMEM((N * 24, N * 24), BF16),
+            pltpu.VMEM((N, 27, 8, BX), F32),
+            pltpu.SemaphoreType.DMA((18,)),
         ],
         compiler_params=params(WHOLE),
         name="z_lines",
-    )(where, jnp.asarray(np.stack(z_matrix())), *arrays, after)
+    )(where, after, jnp.asarray(high), jnp.asarray(low), *arrays)
 
 
 def z_unpack_kernel(where_ref, term_ref, *refs):
@@ -583,9 +592,8 @@
             stage = regroup(stage, tiles_of(route), r == 0)
             arrived += send_stage(stage, route[1], 1)
     term_x, denom = along_x(velocity, wind, offset)
-    turned = z_lines(1, where, term_x, arrived[4:])
-    spanwise = y_lines(level_sums(arrived, term_x), received, turned[0])
-    vertical = z_lines(0, where, spanwise, arrived[:4]) + turned
+    spanwise, after = y_lines(level_sums(arrived), received)
+    vertical = z_lines(where, after, arrived)
     with jax.named_scope("spanwise_return"):
         returned = lax.all_to_all(spanwise, "py", 0, 0, tiled=True)
     with jax.named_scope("vertical_return"):

time: 119 us -> 119 us (level)
  Pallas kernels: 28.5 us -> 23.8 us
  starting transfers between devices: 47 us -> 50.6 us
  local copies, waits for them, and re-layouts: 8.57 us -> 11.6 us
  waiting for transfers between devices: 33.1 us -> 30.3 us
    pallas_call x4 -> x3, Pallas kernels: 12.5 us -> 7 us  [the longest x1 5.09 us: z_lines(): pl.pallas_call(z_kernel, in_specs=[SM, VM] + [HB] * 10, out_specs=[HB] *...]
    ppermute x24, waiting for transfers between devices: 31.8 us -> 26.4 us  [shift(): return lax.ppermute(value, 'pz', moves)]
    ppermute x24, starting transfers between devices: 27.1 us -> 32.1 us  [shift(): return lax.ppermute(value, 'pz', moves)]
    all_to_all x1, waiting for transfers between devices: 0.01 us -> 3.83 us  [body(): returned = lax.all_to_all(spanwise, 'py', 0, 0, tiled=True)]
    unnamed x68 -> x54, local copies, waits for them, and re-layouts: 8.57 us -> 11.6 us
    all_to_all x1, starting transfers between devices: 9.78 us -> 8.38 us  [body(): returned = lax.all_to_all(spanwise, 'py', 0, 0, tiled=True)]
    all_to_all x1, waiting for transfers between devices: 1.31 us -> 0.01 us  [body(): received = lax.all_to_all(packed, 'py', 0, 0, tiled=True)]
  transfers between devices with their start and end apart: 26 -> 26, of which waited for: 11 -> 9; matrix products, arithmetic and copies ran while one was open for 0% -> 0% of each run, Pallas kernels for 17% -> 13%
where the time goes in v4:
time: 119 us; the launch traced here: 118 us
  starting transfers between devices  50.6 us (43%)
  waiting for transfers between devices  30.3 us (25%)
  Pallas kernels  23.8 us (20%)
  local copies, waits for them, and re-layouts  11.6 us (10%)
    ppermute x24, starting transfers between devices, shift(): return lax.ppermute(value, 'pz', moves)  32.1 us
    ppermute x24, waiting for transfers between devices, shift(): return lax.ppermute(value, 'pz', moves)  26.4 us
    unnamed x54, local copies, waits for them, and re-layouts  11.6 us
    all_to_all x1, starting transfers between devices, body(): received = lax.all_to_all(packed, 'py', 0, 0, tiled=True)  10.1 us
    all_to_all x1, starting transfers between devices, body(): returned = lax.all_to_all(spanwise, 'py', 0, 0, tiled=True)  8.38 us
    pallas_call x1, Pallas kernels, along_x(): pl.pallas_call(x_kernel, in_specs=[SM, VM, VM, VM], out_specs=[VM, VM], o...  5.66 us
    pallas_call x1, Pallas kernels, z_lines(): pl.pallas_call(z_kernel, in_specs=[SM, VM] + [HB] * 10, out_specs=[HB] *...  5.09 us
    pallas_call x1, Pallas kernels, finish(): pl.pallas_call(final_kernel, in_specs=[SM] + [VM] * 7, out_specs=[HB, VM]...  4.11 us
  transfers between devices with their start and end apart: 26, of which 9 were waited for; matrix products, arithmetic and copies ran while one was open for 0% of the time, Pallas kernels for 13%

profile of v4, /device:TPU:1, one launch (start us, length us, event | category | flops | bytes accessed | tf_op | source)
XLA Modules:
  0.0 117.5 jit_solution(1778802140793131625)
XLA Ops:
  0.6 2.3 %y_pack.1 = f32[16,27,8,128]{3,2,1,0:T(8,128)} custom-call(f32[12,24,1536]{2,1,0:T(8,128)} %v_ref.5), custom_call_target="tpu_custom_call" | custom-call | tf_op jit(solution)/shard_map/y_pack/pallas_call | solution.py:195
  3.0 10.1 %all-to-all-start = ((f32[16,27,8,128]{3,2,1,0:T(8,128)}), f32[16,27,8,128]{3,2,1,0:T(8,128)S(1)}, u32[]{:S(2)}, u32[]{:S(2)}) async-start(f32[16,27,8,128]{3,2,1,0:T(8,128)} %y_pack.1), calls=%async_computation | async-start | bytes 3538944 | tf_op jit(solution)/shard_map/spanwise_send/all_to_all | solution.py:586
  13.2 0.8 z_pack.3
  14.1 1.4 %collective-permute-start.6 = (f32[48,8,128]{2,1,0:T(8,128)S(1)}, f32[48,8,128]{2,1,0:T(8,128)S(1)}, u32[]{:S(2)}, u32[]{:S(2)}) collective-permute-start(f32[48,8,128]{2,1,0:T(8,128)S(1)} %get-tuple-element.64), channel_id=1, source_target_pairs={{0,1},{1,2},{2,3},{3,0},{4,5},{5,6},{6,7},{7,4},{8,9},{9,10},{10,1... | collective-permute-start | bytes 589832 | tf_op jit(solution)/shard_map/vertical_send/ppermute | solution.py:338
  15.5 2.6 %collective-permute-start.7 = (f32[48,8,128]{2,1,0:T(8,128)S(1)}, f32[48,8,128]{2,1,0:T(8,128)S(1)}, u32[]{:S(2)}, u32[]{:S(2)}) collective-permute-start(f32[48,8,128]{2,1,0:T(8,128)S(1)} %get-tuple-element.65), channel_id=1, source_target_pairs={{0,2},{1,3},{2,0},{3,1},{4,6},{5,7},{6,4},{7,5},{8,10},{9,11},{10,... | collective-permute-start | bytes 589832 | tf_op jit(solution)/shard_map/vertical_send/ppermute | solution.py:338
  18.1 1.1 collective-permute-start.8
  19.2 1.5 %disks.1 = (f32[8,128]{1,0:T(8,128)S(1)}, bf16[128,1536]{1,0:T(8,128)(2,1)S(1)}, bf16[128,1536]{1,0:T(8,128)(2,1)S(1)}, f32[288,128]{1,0:T(8,128)S(1)}) custom-call(s32[4]{0:T(128)S(1)} %pad_add_fusion.where_ref, f32[12]{0:T(128)S(1)} %copy-done.24, s32[4,100]{1,0:T(4,128)S(1)} %bitcast.15, s32[3,100]{1,0:T(4,128)S(1)} %bitcast.16, f32[12,24,1536]{2,1,0:T(8,128)S(1)} %copy-done), custom_call_target="tpu_custom_call" | custom-call | tf_op jit(solution)/shard_map/disks/pallas_call | solution.py:505
  20.7 0.9 z_pack.2
  21.9 2.5 %collective-permute-start.1 = (f32[61,8,128]{2,1,0:T(8,128)S(1)}, f32[61,8,128]{2,1,0:T(8,128)S(1)}, u32[]{:S(2)}, u32[]{:S(2)}) collective-permute-start(f32[61,8,128]{2,1,0:T(8,128)S(1)} %get-tuple-element.57), channel_id=1, source_target_pairs={{0,8},{1,9},{2,10},{3,11},{4,12},{5,13},{6,14},{7,15},{8,0},{9,1},... | collective-permute-start | bytes 749576 | tf_op jit(solution)/shard_map/vertical_send/ppermute | solution.py:338
  24.4 1.2 collective-permute-start.2
  25.5 1.7 %collective-permute-done.7.refs_2_ = f32[48,8,128]{2,1,0:T(8,128)S(1)} collective-permute-done((f32[48,8,128]{2,1,0:T(8,128)S(1)}, f32[48,8,128]{2,1,0:T(8,128)S(1)}, u32[]{:S(2)}, u32[]{:S(2)}) %collective-permute-start.7) | collective-permute-done | bytes 196640 | tf_op jit(solution)/shard_map/vertical_send/ppermute | solution.py:338
  27.4 1.3 %collective-permute-start.9 = (f32[48,8,128]{2,1,0:T(8,128)S(1)}, f32[48,8,128]{2,1,0:T(8,128)S(1)}, u32[]{:S(2)}, u32[]{:S(2)}) collective-permute-start(f32[48,8,128]{2,1,0:T(8,128)S(1)} %get-tuple-element.68), channel_id=1, source_target_pairs={{0,4},{1,5},{2,6},{3,7},{4,8},{5,9},{6,10},{7,11},{8,12},{9,13},{1... | collective-permute-start | bytes 589832 | tf_op jit(solution)/shard_map/vertical_send/ppermute | solution.py:338
  28.6 0.8 collective-permute-done.refs_1_
  29.5 5.5 %collective-permute-done.1.refs_2_ = f32[61,8,128]{2,1,0:T(8,128)S(1)} collective-permute-done((f32[61,8,128]{2,1,0:T(8,128)S(1)}, f32[61,8,128]{2,1,0:T(8,128)S(1)}, u32[]{:S(2)}, u32[]{:S(2)}) %collective-permute-start.1) | collective-permute-done | bytes 249888 | tf_op jit(solution)/shard_map/vertical_send/ppermute | solution.py:338
  34.9 0.8 collective-permute-done.2.refs_3_
  36.6 2.2 %collective-permute-start.5 = (f32[61,8,128]{2,1,0:T(8,128)S(1)}, f32[61,8,128]{2,1,0:T(8,128)S(1)}, u32[]{:S(2)}, u32[]{:S(2)}) collective-permute-start(f32[61,8,128]{2,1,0:T(8,128)S(1)} %get-tuple-element.62), channel_id=1, source_target_pairs={{0,3},{1,0},{2,1},{3,2},{4,7},{5,4},{6,5},{7,6},{8,11},{9,8},{10,9... | collective-permute-start | bytes 749576 | tf_op jit(solution)/shard_map/vertical_send/ppermute | solution.py:338
  38.8 1.8 %collective-permute-start.10 = (f32[48,8,128]{2,1,0:T(8,128)S(1)}, f32[48,8,128]{2,1,0:T(8,128)S(1)}, u32[]{:S(2)}, u32[]{:S(2)}) collective-permute-start(f32[48,8,128]{2,1,0:T(8,128)S(1)} %get-tuple-element.69), channel_id=1, source_target_pairs={{0,8},{1,9},{2,10},{3,11},{4,12},{5,13},{6,14},{7,15},{8,0},{9,1},... | collective-permute-start | bytes 589832 | tf_op jit(solution)/shard_map/vertical_send/ppermute | solution.py:338
  40.6 2.8 %collective-permute-start.11 = (f32[48,8,128]{2,1,0:T(8,128)S(1)}, f32[48,8,128]{2,1,0:T(8,128)S(1)}, u32[]{:S(2)}, u32[]{:S(2)}) collective-permute-start(f32[48,8,128]{2,1,0:T(8,128)S(1)} %get-tuple-element.70), channel_id=1, source_target_pairs={{0,12},{1,13},{2,14},{3,15},{4,0},{5,1},{6,2},{7,3},{8,4},{9,5},{1... | collective-permute-start | bytes 589832 | tf_op jit(solution)/shard_map/vertical_send/ppermute | solution.py:338
  43.4 1.7 %collective-permute-done.10.refs_6_ = f32[48,8,128]{2,1,0:T(8,128)S(1)} collective-permute-done((f32[48,8,128]{2,1,0:T(8,128)S(1)}, f32[48,8,128]{2,1,0:T(8,128)S(1)}, u32[]{:S(2)}, u32[]{:S(2)}) %collective-permute-start.10) | collective-permute-done | bytes 196640 | tf_op jit(solution)/shard_map/vertical_send/ppermute | solution.py:338
  45.1 6.2 %collective-permute-done.11.refs_7_ = f32[48,8,128]{2,1,0:T(8,128)S(1)} collective-permute-done((f32[48,8,128]{2,1,0:T(8,128)S(1)}, f32[48,8,128]{2,1,0:T(8,128)S(1)}, u32[]{:S(2)}, u32[]{:S(2)}) %collective-permute-start.11) | collective-permute-done | bytes 196640 | tf_op jit(solution)/shard_map/vertical_send/ppermute | solution.py:338
  51.5 0.7 copy-done.2
  52.2 0.7 copy-done.3
  52.9 0.7 copy-done.4
  53.6 0.7 copy-done.5
  54.3 0.7 copy-done.7
  55.0 0.7 copy-done.8
  55.6 0.7 copy-done.9
  56.3 1.1 copy-done.10
  57.4 1.8 %y_lines.1 = (f32[16,28,8,128]{3,2,1,0:T(8,128)S(1)}, f32[8,128]{1,0:T(8,128)S(1)}) custom-call(bf16[2,384,384]{2,1,0:T(8,128)(2,1)S(1)} %copy-done.10, f32[8,128]{1,0:T(8,128)S(1)} %level_sums.1.sums_ref, f32[16,27,8,128]{3,2,1,0:T(8,128)S(1)} %all-to-all-done.in_ref), custom_call_target="tpu_custom_call" | custom-call | tf_op jit(solution)/shard_map/y_lines/pallas_call | solution.py:248
  59.2 1.2 %copy-done.1 = f32[16,28,8,128]{3,2,1,0:T(8,128)} copy-done((f32[16,28,8,128]{3,2,1,0:T(8,128)}, f32[16,28,8,128]{3,2,1,0:T(8,128)S(1)}, u32[]{:S(2)}) %copy-start.1) | copy-done | bytes 1835032
  61.1 8.4 %all-to-all-start.1 = ((f32[16,28,8,128]{3,2,1,0:T(8,128)}), f32[16,28,8,128]{3,2,1,0:T(8,128)}, u32[]{:S(2)}, u32[]{:S(2)}) async-start(f32[16,28,8,128]{3,2,1,0:T(8,128)} %copy-done.1), calls=%async_computation.1 | async-start | bytes 3670016 | tf_op jit(solution)/shard_map/spanwise_return/all_to_all | solution.py:598
  69.4 5.1 %z_lines.1 = (f32[60,8,128]{2,1,0:T(8,128)}, f32[60,8,128]{2,1,0:T(8,128)}, f32[60,8,128]{2,1,0:T(8,128)}, f32[60,8,128]{2,1,0:T(8,128)}, f32[48,8,128]{2,1,0:T(...) custom-call(s32[4]{0:T(128)} %copy-done.19, f32[8,128]{1,0:T(8,128)} %copy-done.21, ...), custom_call_target="tpu_custom_call" | custom-call | tf_op jit(solution)/shard_map/z_lines/pallas_call | solution.py:392
  74.5 2.4 %collective-permute-start.18 = (f32[48,8,128]{2,1,0:T(8,128)}, f32[48,8,128]{2,1,0:T(8,128)S(1)}, u32[]{:S(2)}, u32[]{:S(2)}) collective-permute-start(f32[48,8,128]{2,1,0:T(8,128)} %get-tuple-element.82), channel_id=1, source_target_pairs={{0,12},{1,13},{2,14},{3,15},{4,0},{5,1},{6,2},{7,3},{8,4},{9,5},{1... | collective-permute-start | bytes 589832 | tf_op jit(solution)/shard_map/vertical_return/ppermute | solution.py:338
  77.0 0.6 collective-permute-start.19
  77.7 2.0 %collective-permute-start.12 = (f32[60,8,128]{2,1,0:T(8,128)}, f32[60,8,128]{2,1,0:T(8,128)S(1)}, u32[]{:S(2)}, u32[]{:S(2)}) collective-permute-start(f32[60,8,128]{2,1,0:T(8,128)} %get-tuple-element.74), channel_id=1, source_target_pairs={{0,3},{1,0},{2,1},{3,2},{4,7},{5,4},{6,5},{7,6},{8,11},{9,8},{10,9... | collective-permute-start | bytes 737288 | tf_op jit(solution)/shard_map/vertical_return/ppermute | solution.py:338
  79.8 5.7 %collective-permute-done.18.refs_1_ = f32[48,8,128]{2,1,0:T(8,128)S(1)} collective-permute-done((f32[48,8,128]{2,1,0:T(8,128)}, f32[48,8,128]{2,1,0:T(8,128)S(1)}, u32[]{:S(2)}, u32[]{:S(2)}) %collective-permute-start.18) | collective-permute-done | bytes 196640 | tf_op jit(solution)/shard_map/vertical_return/ppermute | solution.py:338
  85.9 3.9 %collective-permute-done.20.refs_3_ = f32[48,8,128]{2,1,0:T(8,128)S(1)} collective-permute-done((f32[48,8,128]{2,1,0:T(8,128)}, f32[48,8,128]{2,1,0:T(8,128)S(1)}, u32[]{:S(2)}, u32[]{:S(2)}) %collective-permute-start.20) | collective-permute-done | bytes 196640 | tf_op jit(solution)/shard_map/vertical_return/ppermute | solution.py:338
  89.8 0.9 copy-done.16
  90.8 2.0 %collective-permute-start.21 = (f32[48,8,128]{2,1,0:T(8,128)S(1)}, f32[48,8,128]{2,1,0:T(8,128)S(1)}, u32[]{:S(2)}, u32[]{:S(2)}) collective-permute-start(f32[48,8,128]{2,1,0:T(8,128)S(1)} %get-tuple-element.86), channel_id=1, source_target_pairs={{0,3},{1,0},{2,1},{3,2},{4,7},{5,4},{6,5},{7,6},{8,11},{9,8},{10,9... | collective-permute-start | bytes 589832 | tf_op jit(solution)/shard_map/vertical_return/ppermute | solution.py:338
  93.2 0.8 collective-permute-start.23
  93.9 0.9 copy-done.15
  94.9 3.4 %collective-permute-start.15 = (f32[60,8,128]{2,1,0:T(8,128)S(1)}, f32[60,8,128]{2,1,0:T(8,128)S(1)}, u32[]{:S(2)}, u32[]{:S(2)}) collective-permute-start(f32[60,8,128]{2,1,0:T(8,128)S(1)} %get-tuple-element.78), channel_id=1, source_target_pairs={{0,12},{1,13},{2,14},{3,15},{4,0},{5,1},{6,2},{7,3},{8,4},{9,5},{1... | collective-permute-start | bytes 737288 | tf_op jit(solution)/shard_map/vertical_return/ppermute | solution.py:338
  98.3 2.1 %collective-permute-start.16 = (f32[60,8,128]{2,1,0:T(8,128)S(1)}, f32[60,8,128]{2,1,0:T(8,128)S(1)}, u32[]{:S(2)}, u32[]{:S(2)}) collective-permute-start(f32[60,8,128]{2,1,0:T(8,128)S(1)} %get-tuple-element.79), channel_id=1, source_target_pairs={{0,8},{1,9},{2,10},{3,11},{4,12},{5,13},{6,14},{7,15},{8,0},{9,1},... | collective-permute-start | bytes 737288 | tf_op jit(solution)/shard_map/vertical_return/ppermute | solution.py:338
  100.4 1.9 %copy-done.26 = bf16[8,768,256]{2,1,0:T(8,128)(2,1)S(1)} copy-done((bf16[8,768,256]{2,1,0:T(8,128)(2,1)S(1)}, bf16[8,768,256]{2,1,0:T(8,128)(2,1)}, u32[]{:S(2)}) %copy-start.26) | copy-done | bytes 3145752
  102.3 5.7 %x_derivative.1 = (f32[12,24,1536]{2,1,0:T(8,128)S(1)}, f32[8,128]{1,0:T(8,128)S(1)}) custom-call(f32[12]{0:T(128)S(1)} %copy-done.24, s32[3,100]{1,0:T(4,128)S(1)} %bitcast.17, f32[12,24,1536]{2,1,0:T(8,128)S(1)} %copy-done, bf16[8,768,256]{2,1,0:T(8,128)(2,1)S(1)} %copy-done.26), custom_call_target="tpu_custom_call" | custom-call | flops 4076863488 | bytes 7340032 | tf_op jit(solution)/shard_map/x_derivative/pallas_call | solution.py:157
  108.1 1.3 %z_unpack.1 = f32[288,1536]{1,0:T(8,128)S(1)} custom-call(s32[4]{0:T(128)S(1)} %copy-done.20, f32[288,1536]{1,0:T(8,128)S(1)} %bitcast.14, f32[60,8,128]{2,1,0:T(8,128)S(1)} %get-tuple-element.77.refs_0_, f32[60,8,128]{2,1,0:T(8,128)S(1)} %collective-permute-done.15.refs_1_, f32[60,8,128]{2,1,0:T(8,128)S(1)} %collective-permute-done.16.refs_2_, ...), custom_call_target="tpu_custom_call" | custom-call | tf_op jit(solution)/shard_map/z_unpack/pallas_call | solution.py:438
  109.4 3.8 %all-to-all-done.1.lines_ref = f32[16,28,8,128]{3,2,1,0:T(8,128)} async-done(((f32[16,28,8,128]{3,2,1,0:T(8,128)}), f32[16,28,8,128]{3,2,1,0:T(8,128)}, u32[]{:S(2)}, u32[]{:S(2)}) %all-to-all-start.1) | async-done | bytes 1835040 | tf_op jit(solution)/shard_map/spanwise_return/all_to_all | solution.py:598
  113.2 4.1 %finish.1 = (f32[12,24,1536]{2,1,0:T(8,128)}, f32[1,100]{1,0:T(1,128)}) custom-call(s32[4]{0:T(128)S(1)} %copy-done.20, f32[1,100]{1,0:T(1,128)S(1)} %bitcast.18, f32[8,128]{1,0:T(8,128)S(1)} %get-tuple-element.49.denom_ref, bf16[128,1536]{1,0:T(8,128)(2,1)S(1)} %copy-done.12, bf16[128,1536]{1,0:T(8,128)(2,1)S(1)} %copy-done.14, f32[288,128]{1,0:T(8,128)S(1)} %copy-done.18, ...), custom_call_target="tpu_custom_call" | custom-call | tf_op jit(solution)/shard_map/finish/pallas_call | solution.py:564
  (73 shorter events, 3.2 us)
Async XLA Ops:
  3.0 10.3 %copy-start = (f32[12,24,1536]{2,1,0:T(8,128)S(1)}, f32[12,24,1536]{2,1,0:T(8,128)}, u32[]{:S(2)}) copy-start(f32[12,24,1536]{2,1,0:T(8,128)} %v_ref.5) | copy-start | bytes 5308420
  3.0 53.4 %all-to-all-start = ((f32[16,27,8,128]{3,2,1,0:T(8,128)}), f32[16,27,8,128]{3,2,1,0:T(8,128)S(1)}, u32[]{:S(2)}, u32[]{:S(2)}) async-start(f32[16,27,8,128]{3,2,1,0:T(8,128)} %y_pack.1), calls=%async_computation | async-start | bytes 3538944 | tf_op jit(solution)/shard_map/spanwise_send/all_to_all | solution.py:586
  13.1 6.1 %copy-start.22 = (s32[100,4]{0,1:T(4,128)S(1)}, s32[100,4]{0,1:T(4,128)}, u32[]{:S(2)}) copy-start(s32[100,4]{0,1:T(4,128)} %param.12) | copy-start | bytes 4804
  13.1 6.1 %copy-start.23 = (s32[100,3]{0,1:T(4,128)S(1)}, s32[100,3]{0,1:T(4,128)}, u32[]{:S(2)}) copy-start(s32[100,3]{0,1:T(4,128)} %param.13) | copy-start | bytes 3604
  13.1 6.1 %copy-start.24 = (f32[12]{0:T(128)S(1)}, f32[12]{0:T(128)}, u32[]{:S(2)}) copy-start(f32[12]{0:T(128)} %wind_ref.3) | copy-start | bytes 148
  13.2 7.5 %copy-start.19 = (s32[4]{0:T(128)}, s32[4]{0:T(128)S(1)}, u32[]{:S(2)}) copy-start(s32[4]{0:T(128)S(1)} %pad_add_fusion.where_ref) | copy-start | bytes 52
  14.1 10.3 %collective-permute-start.6 = (f32[48,8,128]{2,1,0:T(8,128)S(1)}, f32[48,8,128]{2,1,0:T(8,128)S(1)}, u32[]{:S(2)}, u32[]{:S(2)}) collective-permute-start(f32[48,8,128]{2,1,0:T(8,128)S(1)} %get-tuple-element.64), channel_id=1, source_target_pairs={{0,1},{1,2},{2,3},{3,0},{4,5},{5,6},{6,7},{7,4},{8,9},{9,10},{10,1... | collective-permute-start | bytes 589832 | tf_op jit(solution)/shard_map/vertical_send/ppermute | solution.py:338
  15.5 11.8 %collective-permute-start.7 = (f32[48,8,128]{2,1,0:T(8,128)S(1)}, f32[48,8,128]{2,1,0:T(8,128)S(1)}, u32[]{:S(2)}, u32[]{:S(2)}) collective-permute-start(f32[48,8,128]{2,1,0:T(8,128)S(1)} %get-tuple-element.65), channel_id=1, source_target_pairs={{0,2},{1,3},{2,0},{3,1},{4,6},{5,7},{6,4},{7,5},{8,10},{9,11},{10,... | collective-permute-start | bytes 589832 | tf_op jit(solution)/shard_map/vertical_send/ppermute | solution.py:338
  18.1 9.2 %collective-permute-start.8 = (f32[48,8,128]{2,1,0:T(8,128)S(1)}, f32[48,8,128]{2,1,0:T(8,128)S(1)}, u32[]{:S(2)}, u32[]{:S(2)}) collective-permute-start(f32[48,8,128]{2,1,0:T(8,128)S(1)} %get-tuple-element.66), channel_id=1, source_target_pairs={{0,3},{1,0},{2,1},{3,2},{4,7},{5,4},{6,5},{7,6},{8,11},{9,8},{10,9... | collective-permute-start | bytes 589832 | tf_op jit(solution)/shard_map/vertical_send/ppermute | solution.py:338
  20.7 15.1 %copy-start.11 = (bf16[128,1536]{1,0:T(8,128)(2,1)}, bf16[128,1536]{1,0:T(8,128)(2,1)S(1)}, u32[]{:S(2)}) copy-start(bf16[128,1536]{1,0:T(8,128)(2,1)S(1)} %get-tuple-element.50.high_ref) | copy-start | bytes 1179652
  20.7 15.1 %copy-start.13 = (bf16[128,1536]{1,0:T(8,128)(2,1)}, bf16[128,1536]{1,0:T(8,128)(2,1)S(1)}, u32[]{:S(2)}) copy-start(bf16[128,1536]{1,0:T(8,128)(2,1)S(1)} %get-tuple-element.51.low_ref) | copy-start | bytes 1179652
  20.7 15.1 %copy-start.17 = (f32[288,128]{1,0:T(8,128)}, f32[288,128]{1,0:T(8,128)S(1)}, u32[]{:S(2)}) copy-start(f32[288,128]{1,0:T(8,128)S(1)} %get-tuple-element.52.radial_ref) | copy-start | bytes 442372
  21.6 7.9 %collective-permute-start = (f32[61,8,128]{2,1,0:T(8,128)S(1)}, f32[61,8,128]{2,1,0:T(8,128)S(1)}, u32[]{:S(2)}, u32[]{:S(2)}) collective-permute-start(f32[61,8,128]{2,1,0:T(8,128)S(1)} %get-tuple-element.56), channel_id=1, source_target_pairs={{0,4},{1,5},{2,6},{3,7},{4,8},{5,9},{6,10},{7,11},{8,12},{9,13},{1... | collective-permute-start | bytes 749576 | tf_op jit(solution)/shard_map/vertical_send/ppermute | solution.py:338
  21.9 13.0 %collective-permute-start.1 = (f32[61,8,128]{2,1,0:T(8,128)S(1)}, f32[61,8,128]{2,1,0:T(8,128)S(1)}, u32[]{:S(2)}, u32[]{:S(2)}) collective-permute-start(f32[61,8,128]{2,1,0:T(8,128)S(1)} %get-tuple-element.57), channel_id=1, source_target_pairs={{0,8},{1,9},{2,10},{3,11},{4,12},{5,13},{6,14},{7,15},{8,0},{9,1},... | collective-permute-start | bytes 749576 | tf_op jit(solution)/shard_map/vertical_send/ppermute | solution.py:338
  24.4 11.3 %collective-permute-start.2 = (f32[61,8,128]{2,1,0:T(8,128)S(1)}, f32[61,8,128]{2,1,0:T(8,128)S(1)}, u32[]{:S(2)}, u32[]{:S(2)}) collective-permute-start(f32[61,8,128]{2,1,0:T(8,128)S(1)} %get-tuple-element.58), channel_id=1, source_target_pairs={{0,12},{1,13},{2,14},{3,15},{4,0},{5,1},{6,2},{7,3},{8,4},{9,5},{1... | collective-permute-start | bytes 749576 | tf_op jit(solution)/shard_map/vertical_send/ppermute | solution.py:338
  27.3 24.0 %copy-start.6 = (f32[48,8,128]{2,1,0:T(8,128)}, f32[48,8,128]{2,1,0:T(8,128)S(1)}, u32[]{:S(2)}) copy-start(f32[48,8,128]{2,1,0:T(8,128)S(1)} %get-tuple-element.67.refs_4_) | copy-start | bytes 589828
  27.4 13.3 %collective-permute-start.9 = (f32[48,8,128]{2,1,0:T(8,128)S(1)}, f32[48,8,128]{2,1,0:T(8,128)S(1)}, u32[]{:S(2)}, u32[]{:S(2)}) collective-permute-start(f32[48,8,128]{2,1,0:T(8,128)S(1)} %get-tuple-element.68), channel_id=1, source_target_pairs={{0,4},{1,5},{2,6},{3,7},{4,8},{5,9},{6,10},{7,11},{8,12},{9,13},{1... | collective-permute-start | bytes 589832 | tf_op jit(solution)/shard_map/vertical_send/ppermute | solution.py:338
  35.8 15.5 %collective-permute-start.3 = (f32[61,8,128]{2,1,0:T(8,128)S(1)}, f32[61,8,128]{2,1,0:T(8,128)S(1)}, u32[]{:S(2)}, u32[]{:S(2)}) collective-permute-start(f32[61,8,128]{2,1,0:T(8,128)S(1)} %get-tuple-element.60), channel_id=1, source_target_pairs={{0,1},{1,2},{2,3},{3,0},{4,5},{5,6},{6,7},{7,4},{8,9},{9,10},{10,1... | collective-permute-start | bytes 749576 | tf_op jit(solution)/shard_map/vertical_send/ppermute | solution.py:338
  36.3 15.0 %collective-permute-start.4 = (f32[61,8,128]{2,1,0:T(8,128)S(1)}, f32[61,8,128]{2,1,0:T(8,128)S(1)}, u32[]{:S(2)}, u32[]{:S(2)}) collective-permute-start(f32[61,8,128]{2,1,0:T(8,128)S(1)} %get-tuple-element.61), channel_id=1, source_target_pairs={{0,2},{1,3},{2,0},{3,1},{4,6},{5,7},{6,4},{7,5},{8,10},{9,11},{10,... | collective-permute-start | bytes 749576 | tf_op jit(solution)/shard_map/vertical_send/ppermute | solution.py:338
  36.6 14.7 %collective-permute-start.5 = (f32[61,8,128]{2,1,0:T(8,128)S(1)}, f32[61,8,128]{2,1,0:T(8,128)S(1)}, u32[]{:S(2)}, u32[]{:S(2)}) collective-permute-start(f32[61,8,128]{2,1,0:T(8,128)S(1)} %get-tuple-element.62), channel_id=1, source_target_pairs={{0,3},{1,0},{2,1},{3,2},{4,7},{5,4},{6,5},{7,6},{8,11},{9,8},{10,9... | collective-permute-start | bytes 749576 | tf_op jit(solution)/shard_map/vertical_send/ppermute | solution.py:338
  38.8 6.3 %collective-permute-start.10 = (f32[48,8,128]{2,1,0:T(8,128)S(1)}, f32[48,8,128]{2,1,0:T(8,128)S(1)}, u32[]{:S(2)}, u32[]{:S(2)}) collective-permute-start(f32[48,8,128]{2,1,0:T(8,128)S(1)} %get-tuple-element.69), channel_id=1, source_target_pairs={{0,8},{1,9},{2,10},{3,11},{4,12},{5,13},{6,14},{7,15},{8,0},{9,1},... | collective-permute-start | bytes 589832 | tf_op jit(solution)/shard_map/vertical_send/ppermute | solution.py:338
  40.6 10.7 %collective-permute-start.11 = (f32[48,8,128]{2,1,0:T(8,128)S(1)}, f32[48,8,128]{2,1,0:T(8,128)S(1)}, u32[]{:S(2)}, u32[]{:S(2)}) collective-permute-start(f32[48,8,128]{2,1,0:T(8,128)S(1)} %get-tuple-element.70), channel_id=1, source_target_pairs={{0,12},{1,13},{2,14},{3,15},{4,0},{5,1},{6,2},{7,3},{8,4},{9,5},{1... | collective-permute-start | bytes 589832 | tf_op jit(solution)/shard_map/vertical_send/ppermute | solution.py:338
  51.4 0.7 copy-start.2
  52.2 0.7 copy-start.3
  52.9 0.7 copy-start.4
  56.3 1.1 copy-start.10
  59.2 1.2 %copy-start.1 = (f32[16,28,8,128]{3,2,1,0:T(8,128)}, f32[16,28,8,128]{3,2,1,0:T(8,128)S(1)}, u32[]{:S(2)}) copy-start(f32[16,28,8,128]{3,2,1,0:T(8,128)S(1)} %get-tuple-element.89) | copy-start | bytes 5505028
  61.1 52.1 %all-to-all-start.1 = ((f32[16,28,8,128]{3,2,1,0:T(8,128)}), f32[16,28,8,128]{3,2,1,0:T(8,128)}, u32[]{:S(2)}, u32[]{:S(2)}) async-start(f32[16,28,8,128]{3,2,1,0:T(8,128)} %copy-done.1), calls=%async_computation.1 | async-start | bytes 3670016 | tf_op jit(solution)/shard_map/spanwise_return/all_to_all | solution.py:598
  74.5 11.0 %collective-permute-start.18 = (f32[48,8,128]{2,1,0:T(8,128)}, f32[48,8,128]{2,1,0:T(8,128)S(1)}, u32[]{:S(2)}, u32[]{:S(2)}) collective-permute-start(f32[48,8,128]{2,1,0:T(8,128)} %get-tuple-element.82), channel_id=1, source_target_pairs={{0,12},{1,13},{2,14},{3,15},{4,0},{5,1},{6,2},{7,3},{8,4},{9,5},{1... | collective-permute-start | bytes 589832 | tf_op jit(solution)/shard_map/vertical_return/ppermute | solution.py:338
  77.0 8.9 %collective-permute-start.19 = (f32[48,8,128]{2,1,0:T(8,128)}, f32[48,8,128]{2,1,0:T(8,128)S(1)}, u32[]{:S(2)}, u32[]{:S(2)}) collective-permute-start(f32[48,8,128]{2,1,0:T(8,128)} %get-tuple-element.83), channel_id=1, source_target_pairs={{0,8},{1,9},{2,10},{3,11},{4,12},{5,13},{6,14},{7,15},{8,0},{9,1},... | collective-permute-start | bytes 589832 | tf_op jit(solution)/shard_map/vertical_return/ppermute | solution.py:338
  77.6 12.2 %collective-permute-start.20 = (f32[48,8,128]{2,1,0:T(8,128)}, f32[48,8,128]{2,1,0:T(8,128)S(1)}, u32[]{:S(2)}, u32[]{:S(2)}) collective-permute-start(f32[48,8,128]{2,1,0:T(8,128)} %get-tuple-element.84), channel_id=1, source_target_pairs={{0,4},{1,5},{2,6},{3,7},{4,8},{5,9},{6,10},{7,11},{8,12},{9,13},{1... | collective-permute-start | bytes 589832 | tf_op jit(solution)/shard_map/vertical_return/ppermute | solution.py:338
  77.7 15.5 %collective-permute-start.12 = (f32[60,8,128]{2,1,0:T(8,128)}, f32[60,8,128]{2,1,0:T(8,128)S(1)}, u32[]{:S(2)}, u32[]{:S(2)}) collective-permute-start(f32[60,8,128]{2,1,0:T(8,128)} %get-tuple-element.74), channel_id=1, source_target_pairs={{0,3},{1,0},{2,1},{3,2},{4,7},{5,4},{6,5},{7,6},{8,11},{9,8},{10,9... | collective-permute-start | bytes 737288 | tf_op jit(solution)/shard_map/vertical_return/ppermute | solution.py:338
  79.6 14.3 %collective-permute-start.13 = (f32[60,8,128]{2,1,0:T(8,128)}, f32[60,8,128]{2,1,0:T(8,128)S(1)}, u32[]{:S(2)}, u32[]{:S(2)}) collective-permute-start(f32[60,8,128]{2,1,0:T(8,128)} %get-tuple-element.75), channel_id=1, source_target_pairs={{0,2},{1,3},{2,0},{3,1},{4,6},{5,7},{6,4},{7,5},{8,10},{9,11},{10,... | collective-permute-start | bytes 737288 | tf_op jit(solution)/shard_map/vertical_return/ppermute | solution.py:338
  85.5 8.4 %collective-permute-start.14 = (f32[60,8,128]{2,1,0:T(8,128)}, f32[60,8,128]{2,1,0:T(8,128)S(1)}, u32[]{:S(2)}, u32[]{:S(2)}) collective-permute-start(f32[60,8,128]{2,1,0:T(8,128)} %get-tuple-element.76), channel_id=1, source_target_pairs={{0,1},{1,2},{2,3},{3,0},{4,5},{5,6},{6,7},{7,4},{8,9},{9,10},{10,1... | collective-permute-start | bytes 737288 | tf_op jit(solution)/shard_map/vertical_return/ppermute | solution.py:338
  89.8 0.9 copy-start.16
  90.8 9.6 %collective-permute-start.21 = (f32[48,8,128]{2,1,0:T(8,128)S(1)}, f32[48,8,128]{2,1,0:T(8,128)S(1)}, u32[]{:S(2)}, u32[]{:S(2)}) collective-permute-start(f32[48,8,128]{2,1,0:T(8,128)S(1)} %get-tuple-element.86), channel_id=1, source_target_pairs={{0,3},{1,0},{2,1},{3,2},{4,7},{5,4},{6,5},{7,6},{8,11},{9,8},{10,9... | collective-permute-start | bytes 589832 | tf_op jit(solution)/shard_map/vertical_return/ppermute | solution.py:338
  92.9 15.1 %collective-permute-start.22 = (f32[48,8,128]{2,1,0:T(8,128)S(1)}, f32[48,8,128]{2,1,0:T(8,128)S(1)}, u32[]{:S(2)}, u32[]{:S(2)}) collective-permute-start(f32[48,8,128]{2,1,0:T(8,128)S(1)} %get-tuple-element.87), channel_id=1, source_target_pairs={{0,2},{1,3},{2,0},{3,1},{4,6},{5,7},{6,4},{7,5},{8,10},{9,11},{10,... | collective-permute-start | bytes 589832 | tf_op jit(solution)/shard_map/vertical_return/ppermute | solution.py:338
  93.2 14.8 %collective-permute-start.23 = (f32[48,8,128]{2,1,0:T(8,128)S(1)}, f32[48,8,128]{2,1,0:T(8,128)S(1)}, u32[]{:S(2)}, u32[]{:S(2)}) collective-permute-start(f32[48,8,128]{2,1,0:T(8,128)S(1)} %get-tuple-element.88), channel_id=1, source_target_pairs={{0,1},{1,2},{2,3},{3,0},{4,5},{5,6},{6,7},{7,4},{8,9},{9,10},{10,1... | collective-permute-start | bytes 589832 | tf_op jit(solution)/shard_map/vertical_return/ppermute | solution.py:338
  93.9 0.9 copy-start.15
  94.9 13.0 %collective-permute-start.15 = (f32[60,8,128]{2,1,0:T(8,128)S(1)}, f32[60,8,128]{2,1,0:T(8,128)S(1)}, u32[]{:S(2)}, u32[]{:S(2)}) collective-permute-start(f32[60,8,128]{2,1,0:T(8,128)S(1)} %get-tuple-element.78), channel_id=1, source_target_pairs={{0,12},{1,13},{2,14},{3,15},{4,0},{5,1},{6,2},{7,3},{8,4},{9,5},{1... | collective-permute-start | bytes 737288 | tf_op jit(solution)/shard_map/vertical_return/ppermute | solution.py:338
  98.3 9.7 %collective-permute-start.16 = (f32[60,8,128]{2,1,0:T(8,128)S(1)}, f32[60,8,128]{2,1,0:T(8,128)S(1)}, u32[]{:S(2)}, u32[]{:S(2)}) collective-permute-start(f32[60,8,128]{2,1,0:T(8,128)S(1)} %get-tuple-element.79), channel_id=1, source_target_pairs={{0,8},{1,9},{2,10},{3,11},{4,12},{5,13},{6,14},{7,15},{8,0},{9,1},... | collective-permute-start | bytes 737288 | tf_op jit(solution)/shard_map/vertical_return/ppermute | solution.py:338
  100.4 7.6 %copy-start.20 = (s32[4]{0:T(128)S(1)}, s32[4]{0:T(128)}, u32[]{:S(2)}) copy-start(s32[4]{0:T(128)} %copy-done.19) | copy-start | bytes 52
  100.4 7.6 %collective-permute-start.17 = (f32[60,8,128]{2,1,0:T(8,128)S(1)}, f32[60,8,128]{2,1,0:T(8,128)S(1)}, u32[]{:S(2)}, u32[]{:S(2)}) collective-permute-start(f32[60,8,128]{2,1,0:T(8,128)S(1)} %get-tuple-element.80), channel_id=1, source_target_pairs={{0,4},{1,5},{2,6},{3,7},{4,8},{5,9},{6,10},{7,11},{8,12},{9,13},{1... | collective-permute-start | bytes 737288 | tf_op jit(solution)/shard_map/vertical_return/ppermute | solution.py:338
  100.4 1.9 %copy-start.26 = (bf16[8,768,256]{2,1,0:T(8,128)(2,1)S(1)}, bf16[8,768,256]{2,1,0:T(8,128)(2,1)}, u32[]{:S(2)}) copy-start(bf16[8,768,256]{2,1,0:T(8,128)(2,1)} %constant.41.clone.table_ref) | copy-start | bytes 9437188
  108.0 5.2 %copy-start.12 = (bf16[128,1536]{1,0:T(8,128)(2,1)S(1)}, bf16[128,1536]{1,0:T(8,128)(2,1)}, u32[]{:S(2)}) copy-start(bf16[128,1536]{1,0:T(8,128)(2,1)} %copy-done.11) | copy-start | bytes 1179652
  108.0 5.2 %copy-start.14 = (bf16[128,1536]{1,0:T(8,128)(2,1)S(1)}, bf16[128,1536]{1,0:T(8,128)(2,1)}, u32[]{:S(2)}) copy-start(bf16[128,1536]{1,0:T(8,128)(2,1)} %copy-done.13) | copy-start | bytes 1179652
  108.0 5.2 %copy-start.18 = (f32[288,128]{1,0:T(8,128)S(1)}, f32[288,128]{1,0:T(8,128)}, u32[]{:S(2)}) copy-start(f32[288,128]{1,0:T(8,128)} %copy-done.17) | copy-start | bytes 442372
  108.0 5.2 %copy-start.25 = (f32[100]{0:T(128)S(1)}, f32[100]{0:T(128)}, u32[]{:S(2)}) copy-start(f32[100]{0:T(128)} %param.11) | copy-start | bytes 1204
  (5 other events, 3.3 us)
